TPU v7x, 256 devices: a whole 4x4x8 slice. The times are simulated.
256 devices in a mesh: pipe: 4 (over y), dp: 64 (over x, z, core).
Axes of the slice: x: 4, y: 4, z: 8, core: 2. Of those that a mesh axis runs over, the one named last changes fastest.
Arguments:
- features: bfloat16 [1024, 12, 12, 512], P('dp'), may hold values from -16 to 16
- labels: int32 [1024], P('dp'), may hold values from 0 to 999
- micro_count: int32 [64], P('dp'), may hold values from 1 to 8, as said below
- cells_per_section: int32 [4], replicated, may hold values from 1 to 3, as said below
- point_weight: bfloat16 [4, 3, 512, 512], P('pipe'), may hold values from -0.125 to 0.125
- depth_three: bfloat16 [4, 3, 3, 512], P('pipe'), may hold values from -2 to 2
- depth_five: bfloat16 [4, 5, 5, 512], P('pipe'), may hold values from -1.25 to 1.25
- depth_seven: bfloat16 [4, 7, 7, 512], P('pipe'), may hold values from -0.875 to 0.875
- head_weight: float32 [512, 1000], replicated, may hold values from -9 to 9
Outputs:
- loss: float32 [], replicated
- point_grad: float32 [4, 3, 512, 512], P('pipe')
- three_grad: float32 [4, 3, 3, 512], P('pipe')
- five_grad: float32 [4, 5, 5, 512], P('pipe')
- seven_grad: float32 [4, 7, 7, 512], P('pipe')
Inputs may be any that keep to these rules, and one draw needn't show every extreme that they name: Replica r's live micro-batches are its first micro_count[r] ones; some replica has 8. Section q holds cells_per_section[q] cells; some section holds 3.
All inputs are finite; a program needn't handle non-finite values.
Results may differ from a plain program's by a relative error of at most 0.013.
Values may be sent and summed in bfloat16 or wider, within the bound.
A program may use at most 192 MiB of HBM per device.

v0:
```python
import jax
import jax.numpy as jnp
from jax import lax
from jax.sharding import PartitionSpec as P

MB_IMG = 2
MICRO = 8
CELLS_MAX = 3


LOGIT_CAP = 30.0


def passed_along(block, axis, distance):
    devices = range(lax.axis_size(axis))
    route = [(i - distance, i) for i in devices if i - distance in devices]
    return lax.ppermute(block, axis, route)


def depth_conv(rectified, kernel):
    kernel_size = kernel.shape[0]
    half_size = (kernel_size - 1) // 2
    side_rows = rectified.shape[1]
    side_cols = rectified.shape[2]
    padded = jnp.pad(rectified, ((0, 0), (half_size, half_size), (half_size, half_size), (0, 0)))
    running = jnp.zeros_like(rectified)
    for offset_row in range(kernel_size):
        for offset_col in range(kernel_size):
            running = (
                running
                + padded[
                    :, offset_row : offset_row + side_rows, offset_col : offset_col + side_cols, :
                ]
                * kernel[offset_row, offset_col]
            )
    return running


def depth_back(cotangent, kernel):
    kernel_size = kernel.shape[0]
    half_size = (kernel_size - 1) // 2
    side_rows = cotangent.shape[1]
    side_cols = cotangent.shape[2]
    padded = jnp.pad(cotangent, ((0, 0), (half_size, half_size), (half_size, half_size), (0, 0)))
    running = jnp.zeros_like(cotangent)
    for offset_row in range(kernel_size):
        for offset_col in range(kernel_size):
            flip_row = kernel_size - 1 - offset_row
            flip_col = kernel_size - 1 - offset_col
            running = (
                running
                + padded[:, flip_row : flip_row + side_rows, flip_col : flip_col + side_cols, :]
                * kernel[offset_row, offset_col]
            )
    return running


def kernel_terms(rectified, cotangent, kernel_size):
    half_size = (kernel_size - 1) // 2
    side_rows = rectified.shape[1]
    side_cols = rectified.shape[2]
    padded = jnp.pad(rectified, ((0, 0), (half_size, half_size), (half_size, half_size), (0, 0)))
    kernel_rows = []
    for offset_row in range(kernel_size):
        row_terms = []
        for offset_col in range(kernel_size):
            window = padded[
                :, offset_row : offset_row + side_rows, offset_col : offset_col + side_cols, :
            ]
            row_terms.append(jnp.sum(window * cotangent, axis=(0, 1, 2)))
        kernel_rows.append(jnp.stack(row_terms))
    return jnp.stack(kernel_rows)


def make_deep(inputs, kernel):
    rectified = jnp.maximum(inputs, 0).astype(jnp.float32)
    return depth_conv(rectified, kernel.astype(jnp.float32)).astype(jnp.bfloat16)


def forward_cell(inputs, kernel, weight):
    channels = inputs.shape[-1]
    depthwise = make_deep(inputs, kernel)
    mixed = jnp.dot(depthwise.reshape(-1, channels), weight, preferred_element_type=jnp.float32)
    result = inputs.astype(jnp.float32) + mixed.reshape(inputs.shape)
    return (result.astype(jnp.bfloat16), depthwise)


def backward_cell(inputs, depthwise, kernel, weight, cotangent):
    channels = inputs.shape[-1]
    flat_cot = cotangent.reshape(-1, channels)
    point_part = lax.dot_general(
        depthwise.reshape(-1, channels),
        flat_cot,
        (((0,), (0,)), ((), ())),
        preferred_element_type=jnp.float32,
    )
    deep_cot = lax.dot_general(
        flat_cot, weight, (((1,), (1,)), ((), ())), preferred_element_type=jnp.float32
    ).reshape(inputs.shape)
    rectified = jnp.maximum(inputs, 0).astype(jnp.float32)
    kernel_part = kernel_terms(rectified, deep_cot, kernel.shape[0])
    rect_cot = depth_back(deep_cot, kernel.astype(jnp.float32))
    backward = (cotangent.astype(jnp.float32) + jnp.where(inputs > 0, rect_cot, 0.0)).astype(
        jnp.bfloat16
    )
    return (backward, point_part, kernel_part)


def head_loss(final_act, head_weight, targets, live_mask):
    pooled = jnp.mean(final_act.astype(jnp.float32), axis=(1, 2))
    scores = jnp.dot(pooled, head_weight, precision=lax.Precision.HIGHEST)
    capped = jnp.tanh(scores / LOGIT_CAP)
    logits = LOGIT_CAP * capped
    exponent = jnp.exp(logits)
    softmax_total = jnp.sum(exponent, axis=-1, keepdims=True)
    classes = lax.broadcasted_iota(jnp.int32, logits.shape, 1)
    onehot = (classes == targets[:, None]).astype(jnp.float32)
    row_loss = (jnp.log(softmax_total[:, 0]) - jnp.sum(logits * onehot, axis=-1)) * live_mask
    logit_cot = (exponent / softmax_total - onehot) * live_mask[:, None]
    score_cot = logit_cot * (1.0 - capped * capped)
    pooled_cot = lax.dot_general(
        score_cot, head_weight, (((1,), (1,)), ((), ())), precision=lax.Precision.HIGHEST
    )
    positions = final_act.shape[1] * final_act.shape[2]
    spread = jnp.broadcast_to((pooled_cot / positions)[:, None, None, :], final_act.shape)
    return (jnp.sum(row_loss), spread.astype(jnp.bfloat16))


def advance(current, active, kernel, weight):

    def advance_working(inputs):
        return forward_cell(inputs, kernel, weight)

    def advance_resting(inputs):
        return (inputs, jnp.zeros_like(inputs))

    return lax.cond(active, advance_working, advance_resting, current)


def retreat(inputs, stored, current, active, kernel, weight):
    channels = weight.shape[-1]

    def retreat_working(operands):
        cell_in, cell_deep, cell_cot = operands
        return backward_cell(cell_in, cell_deep, kernel, weight, cell_cot)

    def retreat_resting(operands):
        return (
            operands[2],
            jnp.zeros((channels, channels), jnp.float32),
            jnp.zeros(kernel.shape, jnp.float32),
        )

    return lax.cond(active, retreat_working, retreat_resting, (inputs, stored, current))


def shards(
    features,
    labels,
    micro_count,
    cells_per_section,
    point_weight,
    depth_three,
    depth_five,
    depth_seven,
    head_weight,
):
    sections = lax.axis_size("pipe")
    section_index = lax.axis_index("pipe")
    live_count = micro_count[0]
    channels = point_weight.shape[-1]
    micro_shape = (MB_IMG, features.shape[1], features.shape[2], channels)
    live_mask = jnp.ones((MB_IMG,), jnp.float32)
    kernel_zeros = (
        jnp.zeros((3, 3, channels), jnp.float32),
        jnp.zeros((5, 5, channels), jnp.float32),
        jnp.zeros((7, 7, channels), jnp.float32),
    )
    own_point = point_weight[0]
    own_kernels = (depth_three[0], depth_five[0], depth_seven[0])
    cell_count = lax.dynamic_index_in_dim(cells_per_section, section_index, 0, keepdims=False)
    is_last = section_index == sections - 1
    saved_in = jnp.zeros((MICRO, CELLS_MAX) + micro_shape, jnp.bfloat16)
    saved_deep = jnp.zeros((MICRO, CELLS_MAX) + micro_shape, jnp.bfloat16)
    finals = jnp.zeros((MICRO,) + micro_shape, jnp.bfloat16)
    ticks = MICRO + sections - 1

    def forward_tick(tick_index, state_carry):
        incoming, saved_in, saved_deep, finals, loss_sum = state_carry
        micro_index = tick_index - section_index
        is_valid = (micro_index >= 0) & (micro_index < live_count)
        slot_index = jnp.clip(micro_index, 0, MICRO - 1)
        own_images = lax.dynamic_slice_in_dim(features, slot_index * MB_IMG, MB_IMG, 0)
        targets = lax.dynamic_slice_in_dim(labels, slot_index * MB_IMG, MB_IMG, 0)
        section_input = jnp.where(section_index == 0, own_images, incoming)

        def forward_compute(buffers):
            saved_in, saved_deep, finals, loss_sum = buffers
            current = section_input
            for cell_slot in range(CELLS_MAX):
                saved_in = saved_in.at[slot_index, cell_slot].set(current)
                current, depthwise = advance(
                    current, cell_slot < cell_count, own_kernels[cell_slot], own_point[cell_slot]
                )
                saved_deep = saved_deep.at[slot_index, cell_slot].set(depthwise)

            def finish(final_act):
                return head_loss(final_act, head_weight, targets, live_mask)

            def pass_on(final_act):
                return (jnp.zeros((), jnp.float32), jnp.zeros_like(final_act))

            part_loss, final_cot = lax.cond(is_last, finish, pass_on, current)
            finals = finals.at[slot_index].set(final_cot)
            return (current, saved_in, saved_deep, finals, loss_sum + part_loss)

        def forward_passing(buffers):
            return (jnp.zeros_like(section_input),) + buffers

        outgoing, saved_in, saved_deep, finals, loss_sum = lax.cond(
            is_valid, forward_compute, forward_passing, (saved_in, saved_deep, finals, loss_sum)
        )
        incoming = passed_along(outgoing, "pipe", 1)
        return (incoming, saved_in, saved_deep, finals, loss_sum)

    start_state = (
        jnp.zeros(micro_shape, jnp.bfloat16),
        saved_in,
        saved_deep,
        finals,
        jnp.zeros((), jnp.float32),
    )
    spent, saved_in, saved_deep, finals, loss_sum = lax.fori_loop(
        0, ticks, forward_tick, start_state
    )

    def backward_tick(tick_index, state_carry):
        incoming, point_grads, kernel_grads = state_carry
        micro_index = tick_index - (sections - 1 - section_index)
        is_valid = (micro_index >= 0) & (micro_index < live_count)
        slot_index = jnp.clip(micro_index, 0, MICRO - 1)
        section_cot = jnp.where(is_last, finals[slot_index], incoming)

        def backward_compute(grads_in):
            point_grads, kernel_grads = grads_in
            kernel_grads = list(kernel_grads)
            current = section_cot
            for cell_slot in reversed(range(CELLS_MAX)):
                inputs = saved_in[slot_index, cell_slot]
                stored = saved_deep[slot_index, cell_slot]
                current, point_part, kernel_part = retreat(
                    inputs,
                    stored,
                    current,
                    cell_slot < cell_count,
                    own_kernels[cell_slot],
                    own_point[cell_slot],
                )
                point_grads = point_grads.at[cell_slot].add(point_part)
                kernel_grads[cell_slot] = kernel_grads[cell_slot] + kernel_part
            return (current, point_grads, tuple(kernel_grads))

        def backward_passing(grads_in):
            return (jnp.zeros_like(section_cot),) + grads_in

        outgoing, point_grads, kernel_grads = lax.cond(
            is_valid, backward_compute, backward_passing, (point_grads, kernel_grads)
        )
        incoming = passed_along(outgoing, "pipe", -1)
        return (incoming, point_grads, kernel_grads)

    back_state = (
        jnp.zeros(micro_shape, jnp.bfloat16),
        jnp.zeros((CELLS_MAX, channels, channels), jnp.float32),
        kernel_zeros,
    )
    spent, point_grads, kernel_grads = lax.fori_loop(0, ticks, backward_tick, back_state)
    point_local = point_grads[None]
    three_local = kernel_grads[0][None]
    five_local = kernel_grads[1][None]
    seven_local = kernel_grads[2][None]
    point_sum, three_sum, five_sum, seven_sum = lax.psum(
        (point_local, three_local, five_local, seven_local), "dp"
    )
    total_loss = lax.psum(loss_sum, ("pipe", "dp"))
    return (total_loss, point_sum, three_sum, five_sum, seven_sum)


def solution(mesh):
    return jax.shard_map(
        shards,
        mesh=mesh,
        in_specs=(
            P("dp", None, None, None),
            P("dp"),
            P("dp"),
            P(),
            P("pipe", None, None, None),
            P("pipe", None, None, None),
            P("pipe", None, None, None),
            P("pipe", None, None, None),
            P(),
        ),
        out_specs=(
            P(),
            P("pipe", None, None, None),
            P("pipe", None, None, None),
            P("pipe", None, None, None),
            P("pipe", None, None, None),
        ),
        check_vma=False,
    )
```

profile of v0, /device:TPU:1, one launch (start us, length us, event | category | flops | bytes accessed | tf_op | source)
XLA Modules:
  0.0 1776.9 jit_solution(18250166110061454351)
XLA Ops:
  7.2 4.7 copy.16
  14.6 4.8 broadcast.316
  19.4 4.9 broadcast.316.clone
  26.4 517.9 %while.55 = (s32[]{:T(128)}, bf16[2,12,12,512]{3,2,1,0:T(8,128)(2,1)S(1)}, bf16[8,3,2,12,12,512]{5,4,3,2,1,0:T(8,128)(2,1)}, bf16[8,3,2,12,12,512]{5,4,3,2,1,0:T...) while((s32[]{:T(128)}, ...), condition=%wide.region_19.20_spmd, body=%wide.region_0.19_spmd.sunk | while | flops 530232768 | bytes 25358480 | solution.py:233
  39.2 25.0 %conditional.11 = (bf16[2,12,12,512]{3,2,1,0:T(8,128)(2,1)}, bf16[8,3,2,12,12,512]{5,4,3,2,1,0:T(8,128)(2,1)}, bf16[8,3,2,12,12,512]{5,4,3,2,1,0:T(8,128)(2,1)}, bf16[8,2,12,12,512]{4,3,2,1,0:T(8,128)(2,1)}, f32[]{:T(128)}) conditional(s32[]{:T(128)} %convert_element_type.245, (bf16[8,3,2,12,12,512]{5,4,3,2,1,0:T(8,128)(2,1)}, ...), branch_computations={%region_1.1_spmd, %region_2.18_spmd} | conditional | flops 530232768 | bytes 24178412 | solution.py:220
  65.6 5.7 collective-permute-done
  71.9 25.1 %conditional.11 = (bf16[2,12,12,512]{3,2,1,0:T(8,128)(2,1)}, bf16[8,3,2,12,12,512]{5,4,3,2,1,0:T(8,128)(2,1)}, bf16[8,3,2,12,12,512]{5,4,3,2,1,0:T(8,128)(2,1)}, bf16[8,2,12,12,512]{4,3,2,1,0:T(8,128)(2,1)}, f32[]{:T(128)}) conditional(s32[]{:T(128)} %convert_element_type.245, (bf16[8,3,2,12,12,512]{5,4,3,2,1,0:T(8,128)(2,1)}, ...), branch_computations={%region_1.1_spmd, %region_2.18_spmd} | conditional | flops 530232768 | bytes 24178412 | solution.py:220
  97.0 22.6 %collective-permute-start = (bf16[2,12,12,512]{3,2,1,0:T(8,128)(2,1)}, bf16[2,12,12,512]{3,2,1,0:T(8,128)(2,1)S(1)}, u32[]{:S(2)}, u32[]{:S(2)}) collective-permute-start(bf16[2,12,12,512]{3,2,1,0:T(8,128)(2,1)} %get-tuple-element.2218), channel_id=1, source_target_pairs={{0,64},{64,128},{128,192},{1,65},{65,129},{129,193},{2,66},{66,130... | collective-permute-start | bytes 884744 | tf_op jit(solution)/shard_map/while/body/eval_jaxpr/ppermute | solution.py:17
  119.6 5.0 collective-permute-done
  125.3 25.1 %conditional.11 = (bf16[2,12,12,512]{3,2,1,0:T(8,128)(2,1)}, bf16[8,3,2,12,12,512]{5,4,3,2,1,0:T(8,128)(2,1)}, bf16[8,3,2,12,12,512]{5,4,3,2,1,0:T(8,128)(2,1)}, bf16[8,2,12,12,512]{4,3,2,1,0:T(8,128)(2,1)}, f32[]{:T(128)}) conditional(s32[]{:T(128)} %convert_element_type.245, (bf16[8,3,2,12,12,512]{5,4,3,2,1,0:T(8,128)(2,1)}, ...), branch_computations={%region_1.1_spmd, %region_2.18_spmd} | conditional | flops 530232768 | bytes 24178412 | solution.py:220
  150.3 22.4 %collective-permute-start = (bf16[2,12,12,512]{3,2,1,0:T(8,128)(2,1)}, bf16[2,12,12,512]{3,2,1,0:T(8,128)(2,1)S(1)}, u32[]{:S(2)}, u32[]{:S(2)}) collective-permute-start(bf16[2,12,12,512]{3,2,1,0:T(8,128)(2,1)} %get-tuple-element.2218), channel_id=1, source_target_pairs={{0,64},{64,128},{128,192},{1,65},{65,129},{129,193},{2,66},{66,130... | collective-permute-start | bytes 884744 | tf_op jit(solution)/shard_map/while/body/eval_jaxpr/ppermute | solution.py:17
  172.8 5.0 collective-permute-done
  178.4 25.1 %conditional.11 = (bf16[2,12,12,512]{3,2,1,0:T(8,128)(2,1)}, bf16[8,3,2,12,12,512]{5,4,3,2,1,0:T(8,128)(2,1)}, bf16[8,3,2,12,12,512]{5,4,3,2,1,0:T(8,128)(2,1)}, bf16[8,2,12,12,512]{4,3,2,1,0:T(8,128)(2,1)}, f32[]{:T(128)}) conditional(s32[]{:T(128)} %convert_element_type.245, (bf16[8,3,2,12,12,512]{5,4,3,2,1,0:T(8,128)(2,1)}, ...), branch_computations={%region_1.1_spmd, %region_2.18_spmd} | conditional | flops 530232768 | bytes 24178412 | solution.py:220
  203.5 22.4 %collective-permute-start = (bf16[2,12,12,512]{3,2,1,0:T(8,128)(2,1)}, bf16[2,12,12,512]{3,2,1,0:T(8,128)(2,1)S(1)}, u32[]{:S(2)}, u32[]{:S(2)}) collective-permute-start(bf16[2,12,12,512]{3,2,1,0:T(8,128)(2,1)} %get-tuple-element.2218), channel_id=1, source_target_pairs={{0,64},{64,128},{128,192},{1,65},{65,129},{129,193},{2,66},{66,130... | collective-permute-start | bytes 884744 | tf_op jit(solution)/shard_map/while/body/eval_jaxpr/ppermute | solution.py:17
  225.9 5.0 collective-permute-done
  231.5 25.1 %conditional.11 = (bf16[2,12,12,512]{3,2,1,0:T(8,128)(2,1)}, bf16[8,3,2,12,12,512]{5,4,3,2,1,0:T(8,128)(2,1)}, bf16[8,3,2,12,12,512]{5,4,3,2,1,0:T(8,128)(2,1)}, bf16[8,2,12,12,512]{4,3,2,1,0:T(8,128)(2,1)}, f32[]{:T(128)}) conditional(s32[]{:T(128)} %convert_element_type.245, (bf16[8,3,2,12,12,512]{5,4,3,2,1,0:T(8,128)(2,1)}, ...), branch_computations={%region_1.1_spmd, %region_2.18_spmd} | conditional | flops 530232768 | bytes 24178412 | solution.py:220
  256.6 22.4 %collective-permute-start = (bf16[2,12,12,512]{3,2,1,0:T(8,128)(2,1)}, bf16[2,12,12,512]{3,2,1,0:T(8,128)(2,1)S(1)}, u32[]{:S(2)}, u32[]{:S(2)}) collective-permute-start(bf16[2,12,12,512]{3,2,1,0:T(8,128)(2,1)} %get-tuple-element.2218), channel_id=1, source_target_pairs={{0,64},{64,128},{128,192},{1,65},{65,129},{129,193},{2,66},{66,130... | collective-permute-start | bytes 884744 | tf_op jit(solution)/shard_map/while/body/eval_jaxpr/ppermute | solution.py:17
  279.0 5.0 collective-permute-done
  284.6 25.1 %conditional.11 = (bf16[2,12,12,512]{3,2,1,0:T(8,128)(2,1)}, bf16[8,3,2,12,12,512]{5,4,3,2,1,0:T(8,128)(2,1)}, bf16[8,3,2,12,12,512]{5,4,3,2,1,0:T(8,128)(2,1)}, bf16[8,2,12,12,512]{4,3,2,1,0:T(8,128)(2,1)}, f32[]{:T(128)}) conditional(s32[]{:T(128)} %convert_element_type.245, (bf16[8,3,2,12,12,512]{5,4,3,2,1,0:T(8,128)(2,1)}, ...), branch_computations={%region_1.1_spmd, %region_2.18_spmd} | conditional | flops 530232768 | bytes 24178412 | solution.py:220
  302.8 3.1 fusion.190
  309.8 24.0 %collective-permute-start = (bf16[2,12,12,512]{3,2,1,0:T(8,128)(2,1)}, bf16[2,12,12,512]{3,2,1,0:T(8,128)(2,1)S(1)}, u32[]{:S(2)}, u32[]{:S(2)}) collective-permute-start(bf16[2,12,12,512]{3,2,1,0:T(8,128)(2,1)} %get-tuple-element.2218), channel_id=1, source_target_pairs={{0,64},{64,128},{128,192},{1,65},{65,129},{129,193},{2,66},{66,130... | collective-permute-start | bytes 884744 | tf_op jit(solution)/shard_map/while/body/eval_jaxpr/ppermute | solution.py:17
  333.8 5.0 collective-permute-done
  339.4 25.1 %conditional.11 = (bf16[2,12,12,512]{3,2,1,0:T(8,128)(2,1)}, bf16[8,3,2,12,12,512]{5,4,3,2,1,0:T(8,128)(2,1)}, bf16[8,3,2,12,12,512]{5,4,3,2,1,0:T(8,128)(2,1)}, bf16[8,2,12,12,512]{4,3,2,1,0:T(8,128)(2,1)}, f32[]{:T(128)}) conditional(s32[]{:T(128)} %convert_element_type.245, (bf16[8,3,2,12,12,512]{5,4,3,2,1,0:T(8,128)(2,1)}, ...), branch_computations={%region_1.1_spmd, %region_2.18_spmd} | conditional | flops 530232768 | bytes 24178412 | solution.py:220
  357.6 3.1 fusion.190
  364.5 27.5 %collective-permute-start = (bf16[2,12,12,512]{3,2,1,0:T(8,128)(2,1)}, bf16[2,12,12,512]{3,2,1,0:T(8,128)(2,1)S(1)}, u32[]{:S(2)}, u32[]{:S(2)}) collective-permute-start(bf16[2,12,12,512]{3,2,1,0:T(8,128)(2,1)} %get-tuple-element.2218), channel_id=1, source_target_pairs={{0,64},{64,128},{128,192},{1,65},{65,129},{129,193},{2,66},{66,130... | collective-permute-start | bytes 884744 | tf_op jit(solution)/shard_map/while/body/eval_jaxpr/ppermute | solution.py:17
  392.0 5.0 collective-permute-done
  398.4 51.5 %collective-permute-start = (bf16[2,12,12,512]{3,2,1,0:T(8,128)(2,1)}, bf16[2,12,12,512]{3,2,1,0:T(8,128)(2,1)S(1)}, u32[]{:S(2)}, u32[]{:S(2)}) collective-permute-start(bf16[2,12,12,512]{3,2,1,0:T(8,128)(2,1)} %get-tuple-element.2218), channel_id=1, source_target_pairs={{0,64},{64,128},{128,192},{1,65},{65,129},{129,193},{2,66},{66,130... | collective-permute-start | bytes 884744 | tf_op jit(solution)/shard_map/while/body/eval_jaxpr/ppermute | solution.py:17
  450.0 5.0 collective-permute-done
  456.5 11.8 collective-permute-start
  468.2 5.0 collective-permute-done
  474.7 49.4 %collective-permute-start = (bf16[2,12,12,512]{3,2,1,0:T(8,128)(2,1)}, bf16[2,12,12,512]{3,2,1,0:T(8,128)(2,1)S(1)}, u32[]{:S(2)}, u32[]{:S(2)}) collective-permute-start(bf16[2,12,12,512]{3,2,1,0:T(8,128)(2,1)} %get-tuple-element.2218), channel_id=1, source_target_pairs={{0,64},{64,128},{128,192},{1,65},{65,129},{129,193},{2,66},{66,130... | collective-permute-start | bytes 884744 | tf_op jit(solution)/shard_map/while/body/eval_jaxpr/ppermute | solution.py:17
  524.1 5.0 collective-permute-done
  530.6 8.8 collective-permute-start
  539.3 5.0 collective-permute-done
  546.5 714.7 %while.56 = (s32[]{:T(128)}, bf16[2,12,12,512]{3,2,1,0:T(8,128)(2,1)S(1)}, f32[3,512,512]{2,1,0:T(8,128)}, f32[3,3,512]{2,1,0:T(4,128)S(1)}, f32[5,5,512]{2,1,0:...) while((s32[]{:T(128)}, ...), condition=%wide.region_113.114_spmd, body=%wide.region_21.113_spmd.sunk | while | flops 959416320 | bytes 41730304 | solution.py:277
  549.3 55.7 %collective-permute-done.1 = bf16[2,12,12,512]{3,2,1,0:T(8,128)(2,1)S(1)} collective-permute-done((bf16[2,12,12,512]{3,2,1,0:T(8,128)(2,1)}, bf16[2,12,12,512]{3,2,1,0:T(8,128)(2,1)S(1)}, u32[]{:S(2)}, u32[]{:S(2)}) %collective-permute-start.1) | collective-permute-done | bytes 294944 | tf_op jit(solution)/shard_map/while/body/eval_jaxpr/ppermute | solution.py:17
  607.7 10.9 collective-permute-done.1
  621.3 179.9 %collective-permute-done.1 = bf16[2,12,12,512]{3,2,1,0:T(8,128)(2,1)S(1)} collective-permute-done((bf16[2,12,12,512]{3,2,1,0:T(8,128)(2,1)}, bf16[2,12,12,512]{3,2,1,0:T(8,128)(2,1)S(1)}, u32[]{:S(2)}, u32[]{:S(2)}) %collective-permute-start.1) | collective-permute-done | bytes 294944 | tf_op jit(solution)/shard_map/while/body/eval_jaxpr/ppermute | solution.py:17
  801.9 23.5 %conditional.12 = (bf16[2,12,12,512]{3,2,1,0:T(8,128)(2,1)}, f32[3,512,512]{2,1,0:T(8,128)}, f32[3,3,512]{2,1,0:T(4,128)S(1)}, f32[5,5,512]{2,1,0:T(8,128)S(1)}, f32[7,7,512]{2,1,0:T(8,128)S(1)}) conditional(s32[]{:T(128)} %convert_element_type.246, (f32[3,512,512]{2,1,0:T(8,128)}, f32[3,3,512]{2,1,0:T(4,128)S(1)}, f32[5,5,512]{2,1,0:T(8,128)S(1)}, ...), branch_computations={%region_22.22_spmd, %region_23.112_spmd} | conditional | flops 959416320 | bytes 40550252 | solution.py:266
  812.2 8.9 conditional.7
  826.7 43.4 %collective-permute-done.1 = bf16[2,12,12,512]{3,2,1,0:T(8,128)(2,1)S(1)} collective-permute-done((bf16[2,12,12,512]{3,2,1,0:T(8,128)(2,1)}, bf16[2,12,12,512]{3,2,1,0:T(8,128)(2,1)S(1)}, u32[]{:S(2)}, u32[]{:S(2)}) %collective-permute-start.1) | collective-permute-done | bytes 294944 | tf_op jit(solution)/shard_map/while/body/eval_jaxpr/ppermute | solution.py:17
  870.7 23.5 %conditional.12 = (bf16[2,12,12,512]{3,2,1,0:T(8,128)(2,1)}, f32[3,512,512]{2,1,0:T(8,128)}, f32[3,3,512]{2,1,0:T(4,128)S(1)}, f32[5,5,512]{2,1,0:T(8,128)S(1)}, f32[7,7,512]{2,1,0:T(8,128)S(1)}) conditional(s32[]{:T(128)} %convert_element_type.246, (f32[3,512,512]{2,1,0:T(8,128)}, f32[3,3,512]{2,1,0:T(4,128)S(1)}, f32[5,5,512]{2,1,0:T(8,128)S(1)}, ...), branch_computations={%region_22.22_spmd, %region_23.112_spmd} | conditional | flops 959416320 | bytes 40550252 | solution.py:266
  881.0 8.9 conditional.7
  895.5 43.4 %collective-permute-done.1 = bf16[2,12,12,512]{3,2,1,0:T(8,128)(2,1)S(1)} collective-permute-done((bf16[2,12,12,512]{3,2,1,0:T(8,128)(2,1)}, bf16[2,12,12,512]{3,2,1,0:T(8,128)(2,1)S(1)}, u32[]{:S(2)}, u32[]{:S(2)}) %collective-permute-start.1) | collective-permute-done | bytes 294944 | tf_op jit(solution)/shard_map/while/body/eval_jaxpr/ppermute | solution.py:17
  939.5 23.5 %conditional.12 = (bf16[2,12,12,512]{3,2,1,0:T(8,128)(2,1)}, f32[3,512,512]{2,1,0:T(8,128)}, f32[3,3,512]{2,1,0:T(4,128)S(1)}, f32[5,5,512]{2,1,0:T(8,128)S(1)}, f32[7,7,512]{2,1,0:T(8,128)S(1)}) conditional(s32[]{:T(128)} %convert_element_type.246, (f32[3,512,512]{2,1,0:T(8,128)}, f32[3,3,512]{2,1,0:T(4,128)S(1)}, f32[5,5,512]{2,1,0:T(8,128)S(1)}, ...), branch_computations={%region_22.22_spmd, %region_23.112_spmd} | conditional | flops 959416320 | bytes 40550252 | solution.py:266
  949.8 8.9 conditional.7
  964.3 45.2 %collective-permute-done.1 = bf16[2,12,12,512]{3,2,1,0:T(8,128)(2,1)S(1)} collective-permute-done((bf16[2,12,12,512]{3,2,1,0:T(8,128)(2,1)}, bf16[2,12,12,512]{3,2,1,0:T(8,128)(2,1)S(1)}, u32[]{:S(2)}, u32[]{:S(2)}) %collective-permute-start.1) | collective-permute-done | bytes 294944 | tf_op jit(solution)/shard_map/while/body/eval_jaxpr/ppermute | solution.py:17
  1010.2 23.5 %conditional.12 = (bf16[2,12,12,512]{3,2,1,0:T(8,128)(2,1)}, f32[3,512,512]{2,1,0:T(8,128)}, f32[3,3,512]{2,1,0:T(4,128)S(1)}, f32[5,5,512]{2,1,0:T(8,128)S(1)}, f32[7,7,512]{2,1,0:T(8,128)S(1)}) conditional(s32[]{:T(128)} %convert_element_type.246, (f32[3,512,512]{2,1,0:T(8,128)}, f32[3,3,512]{2,1,0:T(4,128)S(1)}, f32[5,5,512]{2,1,0:T(8,128)S(1)}, ...), branch_computations={%region_22.22_spmd, %region_23.112_spmd} | conditional | flops 959416320 | bytes 40550252 | solution.py:266
  1020.5 8.9 conditional.7
  1035.0 45.6 %collective-permute-done.1 = bf16[2,12,12,512]{3,2,1,0:T(8,128)(2,1)S(1)} collective-permute-done((bf16[2,12,12,512]{3,2,1,0:T(8,128)(2,1)}, bf16[2,12,12,512]{3,2,1,0:T(8,128)(2,1)S(1)}, u32[]{:S(2)}, u32[]{:S(2)}) %collective-permute-start.1) | collective-permute-done | bytes 294944 | tf_op jit(solution)/shard_map/while/body/eval_jaxpr/ppermute | solution.py:17
  1081.2 23.5 %conditional.12 = (bf16[2,12,12,512]{3,2,1,0:T(8,128)(2,1)}, f32[3,512,512]{2,1,0:T(8,128)}, f32[3,3,512]{2,1,0:T(4,128)S(1)}, f32[5,5,512]{2,1,0:T(8,128)S(1)}, f32[7,7,512]{2,1,0:T(8,128)S(1)}) conditional(s32[]{:T(128)} %convert_element_type.246, (f32[3,512,512]{2,1,0:T(8,128)}, f32[3,3,512]{2,1,0:T(4,128)S(1)}, f32[5,5,512]{2,1,0:T(8,128)S(1)}, ...), branch_computations={%region_22.22_spmd, %region_23.112_spmd} | conditional | flops 959416320 | bytes 40550252 | solution.py:266
  1091.5 8.9 conditional.7
  1106.0 43.4 %collective-permute-done.1 = bf16[2,12,12,512]{3,2,1,0:T(8,128)(2,1)S(1)} collective-permute-done((bf16[2,12,12,512]{3,2,1,0:T(8,128)(2,1)}, bf16[2,12,12,512]{3,2,1,0:T(8,128)(2,1)S(1)}, u32[]{:S(2)}, u32[]{:S(2)}) %collective-permute-start.1) | collective-permute-done | bytes 294944 | tf_op jit(solution)/shard_map/while/body/eval_jaxpr/ppermute | solution.py:17
  1150.0 23.5 %conditional.12 = (bf16[2,12,12,512]{3,2,1,0:T(8,128)(2,1)}, f32[3,512,512]{2,1,0:T(8,128)}, f32[3,3,512]{2,1,0:T(4,128)S(1)}, f32[5,5,512]{2,1,0:T(8,128)S(1)}, f32[7,7,512]{2,1,0:T(8,128)S(1)}) conditional(s32[]{:T(128)} %convert_element_type.246, (f32[3,512,512]{2,1,0:T(8,128)}, f32[3,3,512]{2,1,0:T(4,128)S(1)}, f32[5,5,512]{2,1,0:T(8,128)S(1)}, ...), branch_computations={%region_22.22_spmd, %region_23.112_spmd} | conditional | flops 959416320 | bytes 40550252 | solution.py:266
  1160.3 8.9 conditional.7
  1174.8 43.4 %collective-permute-done.1 = bf16[2,12,12,512]{3,2,1,0:T(8,128)(2,1)S(1)} collective-permute-done((bf16[2,12,12,512]{3,2,1,0:T(8,128)(2,1)}, bf16[2,12,12,512]{3,2,1,0:T(8,128)(2,1)S(1)}, u32[]{:S(2)}, u32[]{:S(2)}) %collective-permute-start.1) | collective-permute-done | bytes 294944 | tf_op jit(solution)/shard_map/while/body/eval_jaxpr/ppermute | solution.py:17
  1218.8 23.5 %conditional.12 = (bf16[2,12,12,512]{3,2,1,0:T(8,128)(2,1)}, f32[3,512,512]{2,1,0:T(8,128)}, f32[3,3,512]{2,1,0:T(4,128)S(1)}, f32[5,5,512]{2,1,0:T(8,128)S(1)}, f32[7,7,512]{2,1,0:T(8,128)S(1)}) conditional(s32[]{:T(128)} %convert_element_type.246, (f32[3,512,512]{2,1,0:T(8,128)}, f32[3,3,512]{2,1,0:T(4,128)S(1)}, f32[5,5,512]{2,1,0:T(8,128)S(1)}, ...), branch_computations={%region_22.22_spmd, %region_23.112_spmd} | conditional | flops 959416320 | bytes 40550252 | solution.py:266
  1229.1 8.9 conditional.7
  1243.6 7.4 collective-permute-done.1
  1253.8 7.4 collective-permute-done.1
  1263.3 214.6 %psum.35 = f32[]{:T(128)} all-reduce(f32[]{:T(128)} %get-tuple-element.1631), channel_id=1, replica_groups=mesh['pipe'=4,'dp'=64] {'pipe','dp'}, use_global_device_ids=true, to_apply=%region_20.21 | all-reduce | flops 1 | bytes 8 | tf_op jit(solution)/shard_map/psum | solution.py:285
  1477.9 93.8 %all-reduce.14.cloned.1.call-done = (f32[1,3,3,512]{3,0,2,1:T(1,128)}, f32[1,5,5,512]{3,0,2,1:T(1,128)}) async-done(((f32[1,3,3,512]{3,0,2,1:T(1,128)}, f32[1,5,5,512]{3,0,2,1:T(1,128)}), (f32[1,3,3,512]{3,0,2,1:T(1,128)}, f32[1,5,5,512]{3,0,2,1:T(1,128)})) %all-reduce.14.cloned.1.call-update) | async-done | bytes 69648 | tf_op jit(solution)/shard_map/psum | solution.py:282
  1571.7 192.2 %all-reduce.16.cloned.1.call-done = (f32[1,3,512,512]{3,2,1,0:T(8,128)}, f32[1,7,7,512]{3,0,2,1:T(1,128)}) async-done(((f32[1,3,512,512]{3,2,1,0:T(8,128)}, f32[1,7,7,512]{3,0,2,1:T(1,128)}), (f32[1,3,512,512]{3,2,1,0:T(8,128)}, f32[1,7,7,512]{3,0,2,1:T(1,128)})) %all-reduce.16.cloned.1.call-update) | async-done | bytes 3246096 | tf_op jit(solution)/shard_map/psum | solution.py:282
  1763.9 3.9 copy.140
  (430 shorter events, 381.6 us)
Async XLA Ops:
  7.2 1564.5 %all-reduce.14.cloned.1.call-start = ((), (), s32[]{:S(2)}) async-start(), calls=%async_computation | async-start | bytes 139264 | tf_op jit(solution)/shard_map/psum | solution.py:282
  12.0 1.9 copy-start.6
  24.3 2.1 copy-start
  24.3 2.1 copy-start.1
  24.3 2.1 copy-start.2
  57.4 3.1 copy-start.7
  60.4 0.7 copy-start.8
  64.3 7.0 collective-permute-start
  90.1 3.1 copy-start.7
  93.2 0.7 copy-start.8
  97.0 27.6 %collective-permute-start = (bf16[2,12,12,512]{3,2,1,0:T(8,128)(2,1)}, bf16[2,12,12,512]{3,2,1,0:T(8,128)(2,1)S(1)}, u32[]{:S(2)}, u32[]{:S(2)}) collective-permute-start(bf16[2,12,12,512]{3,2,1,0:T(8,128)(2,1)} %get-tuple-element.2218), channel_id=1, source_target_pairs={{0,64},{64,128},{128,192},{1,65},{65,129},{129,193},{2,66},{66,130... | collective-permute-start | bytes 884744 | tf_op jit(solution)/shard_map/while/body/eval_jaxpr/ppermute | solution.py:17
  143.5 3.1 copy-start.7
  146.5 0.7 copy-start.8
  150.3 27.4 %collective-permute-start = (bf16[2,12,12,512]{3,2,1,0:T(8,128)(2,1)}, bf16[2,12,12,512]{3,2,1,0:T(8,128)(2,1)S(1)}, u32[]{:S(2)}, u32[]{:S(2)}) collective-permute-start(bf16[2,12,12,512]{3,2,1,0:T(8,128)(2,1)} %get-tuple-element.2218), channel_id=1, source_target_pairs={{0,64},{64,128},{128,192},{1,65},{65,129},{129,193},{2,66},{66,130... | collective-permute-start | bytes 884744 | tf_op jit(solution)/shard_map/while/body/eval_jaxpr/ppermute | solution.py:17
  196.6 3.1 copy-start.7
  199.7 0.7 copy-start.8
  203.5 27.4 %collective-permute-start = (bf16[2,12,12,512]{3,2,1,0:T(8,128)(2,1)}, bf16[2,12,12,512]{3,2,1,0:T(8,128)(2,1)S(1)}, u32[]{:S(2)}, u32[]{:S(2)}) collective-permute-start(bf16[2,12,12,512]{3,2,1,0:T(8,128)(2,1)} %get-tuple-element.2218), channel_id=1, source_target_pairs={{0,64},{64,128},{128,192},{1,65},{65,129},{129,193},{2,66},{66,130... | collective-permute-start | bytes 884744 | tf_op jit(solution)/shard_map/while/body/eval_jaxpr/ppermute | solution.py:17
  249.7 3.1 copy-start.7
  252.8 0.7 copy-start.8
  256.6 27.4 %collective-permute-start = (bf16[2,12,12,512]{3,2,1,0:T(8,128)(2,1)}, bf16[2,12,12,512]{3,2,1,0:T(8,128)(2,1)S(1)}, u32[]{:S(2)}, u32[]{:S(2)}) collective-permute-start(bf16[2,12,12,512]{3,2,1,0:T(8,128)(2,1)} %get-tuple-element.2218), channel_id=1, source_target_pairs={{0,64},{64,128},{128,192},{1,65},{65,129},{129,193},{2,66},{66,130... | collective-permute-start | bytes 884744 | tf_op jit(solution)/shard_map/while/body/eval_jaxpr/ppermute | solution.py:17
  302.8 3.1 copy-start.7
  306.0 0.7 copy-start.8
  309.8 29.0 %collective-permute-start = (bf16[2,12,12,512]{3,2,1,0:T(8,128)(2,1)}, bf16[2,12,12,512]{3,2,1,0:T(8,128)(2,1)S(1)}, u32[]{:S(2)}, u32[]{:S(2)}) collective-permute-start(bf16[2,12,12,512]{3,2,1,0:T(8,128)(2,1)} %get-tuple-element.2218), channel_id=1, source_target_pairs={{0,64},{64,128},{128,192},{1,65},{65,129},{129,193},{2,66},{66,130... | collective-permute-start | bytes 884744 | tf_op jit(solution)/shard_map/while/body/eval_jaxpr/ppermute | solution.py:17
  357.6 3.1 copy-start.7
  360.7 0.7 copy-start.8
  364.5 32.5 %collective-permute-start = (bf16[2,12,12,512]{3,2,1,0:T(8,128)(2,1)}, bf16[2,12,12,512]{3,2,1,0:T(8,128)(2,1)S(1)}, u32[]{:S(2)}, u32[]{:S(2)}) collective-permute-start(bf16[2,12,12,512]{3,2,1,0:T(8,128)(2,1)} %get-tuple-element.2218), channel_id=1, source_target_pairs={{0,64},{64,128},{128,192},{1,65},{65,129},{129,193},{2,66},{66,130... | collective-permute-start | bytes 884744 | tf_op jit(solution)/shard_map/while/body/eval_jaxpr/ppermute | solution.py:17
  398.4 56.6 %collective-permute-start = (bf16[2,12,12,512]{3,2,1,0:T(8,128)(2,1)}, bf16[2,12,12,512]{3,2,1,0:T(8,128)(2,1)S(1)}, u32[]{:S(2)}, u32[]{:S(2)}) collective-permute-start(bf16[2,12,12,512]{3,2,1,0:T(8,128)(2,1)} %get-tuple-element.2218), channel_id=1, source_target_pairs={{0,64},{64,128},{128,192},{1,65},{65,129},{129,193},{2,66},{66,130... | collective-permute-start | bytes 884744 | tf_op jit(solution)/shard_map/while/body/eval_jaxpr/ppermute | solution.py:17
  456.5 16.8 collective-permute-start
  474.7 54.4 %collective-permute-start = (bf16[2,12,12,512]{3,2,1,0:T(8,128)(2,1)}, bf16[2,12,12,512]{3,2,1,0:T(8,128)(2,1)S(1)}, u32[]{:S(2)}, u32[]{:S(2)}) collective-permute-start(bf16[2,12,12,512]{3,2,1,0:T(8,128)(2,1)} %get-tuple-element.2218), channel_id=1, source_target_pairs={{0,64},{64,128},{128,192},{1,65},{65,129},{129,193},{2,66},{66,130... | collective-permute-start | bytes 884744 | tf_op jit(solution)/shard_map/while/body/eval_jaxpr/ppermute | solution.py:17
  530.6 13.8 collective-permute-start
  548.0 57.0 %collective-permute-start.1 = (bf16[2,12,12,512]{3,2,1,0:T(8,128)(2,1)}, bf16[2,12,12,512]{3,2,1,0:T(8,128)(2,1)S(1)}, u32[]{:S(2)}, u32[]{:S(2)}) collective-permute-start(bf16[2,12,12,512]{3,2,1,0:T(8,128)(2,1)} %get-tuple-element.2240), channel_id=1, source_target_pairs={{64,0},{128,64},{192,128},{65,1},{129,65},{193,129},{66,2},{130,66... | collective-permute-start | bytes 884744 | tf_op jit(solution)/shard_map/while/body/eval_jaxpr/ppermute | solution.py:17
  606.4 12.2 collective-permute-start.1
  620.1 181.2 %collective-permute-start.1 = (bf16[2,12,12,512]{3,2,1,0:T(8,128)(2,1)}, bf16[2,12,12,512]{3,2,1,0:T(8,128)(2,1)S(1)}, u32[]{:S(2)}, u32[]{:S(2)}) collective-permute-start(bf16[2,12,12,512]{3,2,1,0:T(8,128)(2,1)} %get-tuple-element.2240), channel_id=1, source_target_pairs={{64,0},{128,64},{192,128},{65,1},{129,65},{193,129},{66,2},{130,66... | collective-permute-start | bytes 884744 | tf_op jit(solution)/shard_map/while/body/eval_jaxpr/ppermute | solution.py:17
  825.4 44.7 %collective-permute-start.1 = (bf16[2,12,12,512]{3,2,1,0:T(8,128)(2,1)}, bf16[2,12,12,512]{3,2,1,0:T(8,128)(2,1)S(1)}, u32[]{:S(2)}, u32[]{:S(2)}) collective-permute-start(bf16[2,12,12,512]{3,2,1,0:T(8,128)(2,1)} %get-tuple-element.2240), channel_id=1, source_target_pairs={{64,0},{128,64},{192,128},{65,1},{129,65},{193,129},{66,2},{130,66... | collective-permute-start | bytes 884744 | tf_op jit(solution)/shard_map/while/body/eval_jaxpr/ppermute | solution.py:17
  894.2 44.7 %collective-permute-start.1 = (bf16[2,12,12,512]{3,2,1,0:T(8,128)(2,1)}, bf16[2,12,12,512]{3,2,1,0:T(8,128)(2,1)S(1)}, u32[]{:S(2)}, u32[]{:S(2)}) collective-permute-start(bf16[2,12,12,512]{3,2,1,0:T(8,128)(2,1)} %get-tuple-element.2240), channel_id=1, source_target_pairs={{64,0},{128,64},{192,128},{65,1},{129,65},{193,129},{66,2},{130,66... | collective-permute-start | bytes 884744 | tf_op jit(solution)/shard_map/while/body/eval_jaxpr/ppermute | solution.py:17
  963.0 46.6 %collective-permute-start.1 = (bf16[2,12,12,512]{3,2,1,0:T(8,128)(2,1)}, bf16[2,12,12,512]{3,2,1,0:T(8,128)(2,1)S(1)}, u32[]{:S(2)}, u32[]{:S(2)}) collective-permute-start(bf16[2,12,12,512]{3,2,1,0:T(8,128)(2,1)} %get-tuple-element.2240), channel_id=1, source_target_pairs={{64,0},{128,64},{192,128},{65,1},{129,65},{193,129},{66,2},{130,66... | collective-permute-start | bytes 884744 | tf_op jit(solution)/shard_map/while/body/eval_jaxpr/ppermute | solution.py:17
  1033.7 46.9 %collective-permute-start.1 = (bf16[2,12,12,512]{3,2,1,0:T(8,128)(2,1)}, bf16[2,12,12,512]{3,2,1,0:T(8,128)(2,1)S(1)}, u32[]{:S(2)}, u32[]{:S(2)}) collective-permute-start(bf16[2,12,12,512]{3,2,1,0:T(8,128)(2,1)} %get-tuple-element.2240), channel_id=1, source_target_pairs={{64,0},{128,64},{192,128},{65,1},{129,65},{193,129},{66,2},{130,66... | collective-permute-start | bytes 884744 | tf_op jit(solution)/shard_map/while/body/eval_jaxpr/ppermute | solution.py:17
  1104.7 44.7 %collective-permute-start.1 = (bf16[2,12,12,512]{3,2,1,0:T(8,128)(2,1)}, bf16[2,12,12,512]{3,2,1,0:T(8,128)(2,1)S(1)}, u32[]{:S(2)}, u32[]{:S(2)}) collective-permute-start(bf16[2,12,12,512]{3,2,1,0:T(8,128)(2,1)} %get-tuple-element.2240), channel_id=1, source_target_pairs={{64,0},{128,64},{192,128},{65,1},{129,65},{193,129},{66,2},{130,66... | collective-permute-start | bytes 884744 | tf_op jit(solution)/shard_map/while/body/eval_jaxpr/ppermute | solution.py:17
  1173.5 44.7 %collective-permute-start.1 = (bf16[2,12,12,512]{3,2,1,0:T(8,128)(2,1)}, bf16[2,12,12,512]{3,2,1,0:T(8,128)(2,1)S(1)}, u32[]{:S(2)}, u32[]{:S(2)}) collective-permute-start(bf16[2,12,12,512]{3,2,1,0:T(8,128)(2,1)} %get-tuple-element.2240), channel_id=1, source_target_pairs={{64,0},{128,64},{192,128},{65,1},{129,65},{193,129},{66,2},{130,66... | collective-permute-start | bytes 884744 | tf_op jit(solution)/shard_map/while/body/eval_jaxpr/ppermute | solution.py:17
  1242.3 8.7 collective-permute-start.1
  1252.5 8.7 collective-permute-start.1
  1262.5 501.4 %all-reduce.16.cloned.1.call-start = ((), (), s32[]{:S(2)}) async-start(), calls=%async_computation.1 | async-start | bytes 6492160 | tf_op jit(solution)/shard_map/psum | solution.py:282
  1763.9 3.9 copy-start.5
  1763.9 4.5 copy-start.4
  1763.9 5.1 copy-start.3
Sparse Core Ops, SparseCore 0:
  1262.6 308.9 all-reduce.13
  1575.8 188.0 all-reduce.15
where the time goes:
time: 1790 us; the launch traced here: 1780 us
  waiting for transfers between devices  867 us (48%)
  starting transfers between devices  278 us (16%)
  other arithmetic  232 us (13%)
  blocking collectives  215 us (12%)
  local copies, waits for them, and re-layouts  78.9 us (4%)
  loops' own time  58.5 us (3%)
  matrix products  33.3 us (2%)
    ppermute x22, waiting for transfers between devices, passed_along(): return lax.ppermute(block, axis, route)  581 us
    psum x2, waiting for transfers between devices, shards(): lax.psum((point_local, three_local, five_local, seven_local), 'dp')  286 us
    ppermute x22, starting transfers between devices, passed_along(): return lax.ppermute(block, axis, route)  278 us
    psum x1, blocking collectives, shards(): total_loss = lax.psum(loss_sum, ('pipe', 'dp'))  215 us
    scatter x21, other arithmetic, forward_compute(): saved_in = saved_in.at[slot_index, cell_slot].set(current)  58.4 us
    scatter-add x21, other arithmetic, backward_compute(): point_grads = point_grads.at[cell_slot].add(point_part)  50.7 us
  transfers between devices with their start and end apart: 24, of which 24 were waited for; matrix products, arithmetic and copies ran while one was open for 0% of the time, Pallas kernels for 0%

commit v1 on v0

v1 whole, which is shorter than its diff:
```python
import functools

import jax
import jax.numpy as jnp
import ml_dtypes
import numpy as np
from jax import lax
from jax.experimental import pallas as pl
from jax.experimental.pallas import tpu as pltpu
from jax.sharding import PartitionSpec as P

SIDE = 12
AREA = SIDE * SIDE
MB_IMG = 2
CELLS_MAX = 3
TAPS = 7
TAP_ROWS = 64
LOGIT_CAP = 30.0
CYCLE = SIDE + TAPS // 2
HALF = 128
IMAGES = 4


def transform_tables():
    slots = [(0, 0)]
    seen = {(0, 0)}
    for u in range(CYCLE):
        for v in range(CYCLE):
            if (u, v) in seen:
                continue
            seen.add((u, v))
            seen.add(((-u) % CYCLE, (-v) % CYCLE))
            slots.append((u, v))
    count = len(slots)
    waves = np.array(slots, np.float64)
    sites = np.array([(i, j) for i in range(SIDE) for j in range(SIDE)], np.float64)
    reach = TAPS // 2
    shifts = np.array(
        [(u - reach, v - reach) for u in range(TAPS) for v in range(TAPS)], np.float64
    )
    weight = np.where((waves == 0).all(1), 1.0, 2.0)[:, None] / CYCLE**2
    site_angle = 2 * np.pi * ((waves @ sites.T) % CYCLE) / CYCLE
    tap_angle = 2 * np.pi * ((waves @ shifts.T) % CYCLE) / CYCLE
    into = np.zeros((2 * HALF, AREA))
    into[:count] = np.cos(site_angle)
    into[HALF : HALF + count] = -np.sin(site_angle)
    back = np.zeros((AREA, 2 * HALF))
    back[:, :count] = (np.cos(site_angle) * weight).T
    back[:, HALF : HALF + count] = -(np.sin(site_angle) * weight).T
    tap_into = np.zeros((2 * HALF, TAP_ROWS))
    tap_into[:count, : TAPS * TAPS] = np.cos(tap_angle)
    tap_into[HALF : HALF + count, : TAPS * TAPS] = np.sin(tap_angle)
    tap_back = np.zeros((TAP_ROWS, 2 * HALF))
    tap_back[: TAPS * TAPS, :count] = (np.cos(tap_angle) * weight).T
    tap_back[: TAPS * TAPS, HALF : HALF + count] = -(np.sin(tap_angle) * weight).T
    return [pair_of(table) for table in (into, back, tap_into, tap_back)]


def pair_of(table):
    high = table.astype(ml_dtypes.bfloat16)
    low = (table - high.astype(np.float64)).astype(ml_dtypes.bfloat16)
    return np.stack([high, low])


def mul(a, b):
    return jnp.dot(a, b, preferred_element_type=jnp.float32)


def halves(values):
    high = values.astype(jnp.bfloat16)
    low = (values - high.astype(jnp.float32)).astype(jnp.bfloat16)
    return high, low


def cells_kernel(
    cells_ref,
    features_ref,
    targets_ref,
    live_ref,
    weight_ref,
    taps_ref,
    head_ref,
    into_ref,
    back_ref,
    tap_into_ref,
    tap_back_ref,
    point_ref,
    kernel_ref,
    loss_ref,
    order_ref,
    acts_ref,
    deep_ref,
    wave_ref,
    cot_ref,
    deep_cot_ref,
    total_ref,
):
    sections = weight_ref.shape[0] // CELLS_MAX
    count = jnp.int32(0)
    for section in range(sections):
        held = cells_ref[section]
        for slot in range(CELLS_MAX):
            order_ref[count + slot] = section * CELLS_MAX + slot
        for slot in range(1, CELLS_MAX):

            @pl.when(slot >= held)
            def _(cell=section * CELLS_MAX + slot):
                point_ref[cell] = jnp.zeros(point_ref.shape[1:], point_ref.dtype)
                kernel_ref[cell] = jnp.zeros(kernel_ref.shape[1:], kernel_ref.dtype)

        count = count + held

    acts_ref[0] = features_ref[...]

    def rows_of(image):
        return pl.ds(image * AREA, AREA)

    def forward(step, _):
        cell = order_ref[step]
        taps = taps_ref[cell]
        wave = mul(tap_into_ref[0], taps) + mul(tap_into_ref[1], taps)
        wave_ref[step] = wave
        wave_re, wave_im = wave[:HALF], wave[HALF:]
        for image in range(IMAGES):
            site = jnp.maximum(acts_ref[step, rows_of(image)], 0)
            seen = mul(into_ref[0], site) + mul(into_ref[1], site)
            seen_re, seen_im = seen[:HALF], seen[HALF:]
            mixed = jnp.concatenate(
                [
                    seen_re * wave_re - seen_im * wave_im,
                    seen_re * wave_im + seen_im * wave_re,
                ],
                axis=0,
            )
            high, low = halves(mixed)
            deep = mul(back_ref[0], high) + mul(back_ref[0], low) + mul(back_ref[1], high)
            deep_ref[step, rows_of(image)] = deep.astype(jnp.bfloat16)
        mixed = mul(deep_ref[step], weight_ref[cell])
        acts_ref[step + 1] = (acts_ref[step].astype(jnp.float32) + mixed).astype(jnp.bfloat16)
        return 0

    lax.fori_loop(0, count, forward, 0)

    means = [
        jnp.sum(acts_ref[count, rows_of(image)].astype(jnp.float32), axis=0, keepdims=True)
        for image in range(IMAGES)
    ]
    spare = jnp.zeros((8 - IMAGES, features_ref.shape[1]), jnp.float32)
    pooled = jnp.concatenate(means + [spare], axis=0) / AREA
    head = head_ref[...]
    scores = jnp.dot(
        pooled, head, precision=lax.Precision.HIGHEST, preferred_element_type=jnp.float32
    )
    capped = jnp.tanh(scores / LOGIT_CAP)
    logits = LOGIT_CAP * capped
    exponent = jnp.exp(logits)
    total = jnp.sum(exponent, axis=1, keepdims=True)
    classes = lax.broadcasted_iota(jnp.int32, logits.shape, 1)
    onehot = (classes == targets_ref[...]).astype(jnp.float32)
    live = live_ref[...]
    row_loss = (jnp.log(total) - jnp.sum(logits * onehot, axis=1, keepdims=True)) * live
    loss_ref[...] = jnp.broadcast_to(
        jnp.sum(row_loss, axis=0, keepdims=True), loss_ref.shape
    )
    score_cot = (exponent / total - onehot) * live * (1.0 - capped * capped)
    pooled_cot = lax.dot_general(
        score_cot,
        head,
        (((1,), (1,)), ((), ())),
        precision=lax.Precision.HIGHEST,
        preferred_element_type=jnp.float32,
    )
    spread = pooled_cot / AREA
    for image in range(IMAGES):
        cot_ref[rows_of(image)] = jnp.broadcast_to(
            spread[image : image + 1], (AREA, spread.shape[1])
        ).astype(jnp.bfloat16)

    def backward(turn, _):
        step = count - 1 - turn
        cell = order_ref[step]
        cot = cot_ref[...]
        point_ref[cell] = lax.dot_general(
            deep_ref[step], cot, (((0,), (0,)), ((), ())), preferred_element_type=jnp.float32
        )
        deep_cot_ref[...] = lax.dot_general(
            cot, weight_ref[cell], (((1,), (1,)), ((), ())), preferred_element_type=jnp.float32
        ).astype(jnp.bfloat16)
        wave_re, wave_im = wave_ref[step, :HALF], wave_ref[step, HALF:]
        for image in range(IMAGES):
            acts = acts_ref[step, rows_of(image)]
            seen = mul(into_ref[0], jnp.maximum(acts, 0))
            seen_re, seen_im = seen[:HALF], seen[HALF:]
            sent = mul(into_ref[0], deep_cot_ref[rows_of(image)])
            sent_re, sent_im = sent[:HALF], sent[HALF:]
            part_re = seen_re * sent_re + seen_im * sent_im
            part_im = seen_im * sent_re - seen_re * sent_im
            if image == 0:
                total_ref[:HALF] = part_re
                total_ref[HALF:] = part_im
            else:
                total_ref[:HALF] += part_re
                total_ref[HALF:] += part_im
            mixed = jnp.concatenate(
                [
                    sent_re * wave_re + sent_im * wave_im,
                    sent_im * wave_re - sent_re * wave_im,
                ],
                axis=0,
            ).astype(jnp.bfloat16)
            rect_cot = mul(back_ref[0], mixed)
            cot_ref[rows_of(image)] = (
                cot_ref[rows_of(image)].astype(jnp.float32)
                + jnp.where(acts.astype(jnp.float32) > 0, rect_cot, 0.0)
            ).astype(jnp.bfloat16)
        high, low = halves(total_ref[...])
        kernel_ref[cell] = (
            mul(tap_back_ref[0], high) + mul(tap_back_ref[0], low) + mul(tap_back_ref[1], high)
        )
        return 0

    lax.fori_loop(0, count, backward, 0)


def run_cells(cells, features, targets, live, weights, taps, head):
    slots, channels = weights.shape[0], weights.shape[-1]
    tables = [jnp.asarray(table) for table in transform_tables()]
    vmem = pl.BlockSpec(memory_space=pltpu.VMEM)
    rows = IMAGES * AREA
    return pl.pallas_call(
        cells_kernel,
        out_shape=(
            jax.ShapeDtypeStruct((slots, channels, channels), jnp.float32),
            jax.ShapeDtypeStruct((slots, TAP_ROWS, channels), jnp.float32),
            jax.ShapeDtypeStruct((8, 128), jnp.float32),
        ),
        in_specs=[pl.BlockSpec(memory_space=pltpu.SMEM)] + [vmem] * 10,
        out_specs=(vmem, vmem, vmem),
        scratch_shapes=[
            pltpu.SMEM((slots + CELLS_MAX,), jnp.int32),
            pltpu.VMEM((slots + 1, rows, channels), jnp.bfloat16),
            pltpu.VMEM((slots, rows, channels), jnp.bfloat16),
            pltpu.VMEM((slots, 2 * HALF, channels), jnp.float32),
            pltpu.VMEM((rows, channels), jnp.bfloat16),
            pltpu.VMEM((rows, channels), jnp.bfloat16),
            pltpu.VMEM((2 * HALF, channels), jnp.float32),
        ],
        compiler_params=pltpu.CompilerParams(vmem_limit_bytes=60 * 1024 * 1024),
        name="cells",
    )(cells, features, targets, live, weights, taps, head, *tables)


def padded_taps(kernel):
    edge = (TAPS - kernel.shape[1]) // 2
    wide = jnp.pad(kernel, ((0, 0), (edge, edge), (edge, edge), (0, 0)))
    flat = wide.reshape(kernel.shape[0], TAPS * TAPS, kernel.shape[-1])
    return jnp.pad(flat, ((0, 0), (0, TAP_ROWS - TAPS * TAPS), (0, 0)))


def own_taps(rows, size):
    edge = (TAPS - size) // 2
    window = rows[: TAPS * TAPS].reshape(TAPS, TAPS, rows.shape[-1])
    return window[edge : edge + size, edge : edge + size]


def shards(
    features,
    labels,
    micro_count,
    cells_per_section,
    point_weight,
    depth_three,
    depth_five,
    depth_seven,
    head_weight,
):
    sections = lax.axis_size("pipe")
    section_index = lax.axis_index("pipe")
    channels = point_weight.shape[-1]
    weights = lax.all_gather(point_weight[0], "pipe")
    taps = jnp.concatenate(
        [padded_taps(kernel) for kernel in (depth_three, depth_five, depth_seven)], axis=0
    )
    taps = lax.all_gather(taps, "pipe")
    slots = sections * CELLS_MAX

    per_replica = features.shape[0]
    share = per_replica // sections
    grouped = features.reshape(share, sections, AREA, channels)
    own = lax.dynamic_index_in_dim(grouped, section_index, 1, keepdims=False)
    own = own.reshape(share * AREA, channels)
    image = section_index + sections * lax.iota(jnp.int32, share)
    own_live = (image // MB_IMG < micro_count[0]).astype(jnp.float32)
    own_labels = labels[image]
    live = jnp.pad(own_live, (0, 8 - share))[:, None]
    targets = jnp.pad(own_labels, (0, 8 - share))[:, None]

    point_part, kernel_part, loss_part = run_cells(
        cells_per_section,
        own,
        targets,
        live,
        weights.reshape(slots, channels, channels),
        taps.reshape(slots, TAP_ROWS, channels),
        head_weight,
    )
    point_part = point_part.reshape(sections, CELLS_MAX, channels, channels)
    kernel_part = kernel_part.reshape(sections, CELLS_MAX, TAP_ROWS, channels)
    point_sum = lax.psum_scatter(point_part, "pipe")
    kernel_sum = lax.psum_scatter(kernel_part, "pipe")
    point_sum, kernel_sum = lax.psum((point_sum, kernel_sum), "dp")
    total_loss = lax.psum(loss_part[0, 0], ("pipe", "dp"))
    return (
        total_loss,
        point_sum[None],
        own_taps(kernel_sum[0], 3)[None],
        own_taps(kernel_sum[1], 5)[None],
        own_taps(kernel_sum[2], 7)[None],
    )


def solution(mesh):
    return jax.shard_map(
        shards,
        mesh=mesh,
        in_specs=(
            P("dp", None, None, None),
            P("dp"),
            P("dp"),
            P(),
            P("pipe", None, None, None),
            P("pipe", None, None, None),
            P("pipe", None, None, None),
            P("pipe", None, None, None),
            P(),
        ),
        out_specs=(
            P(),
            P("pipe", None, None, None),
            P("pipe", None, None, None),
            P("pipe", None, None, None),
            P("pipe", None, None, None),
        ),
        check_vma=False,
    )
```

time: 1790 us -> 505 us (0.28)
  waiting for transfers between devices: 867 us -> 317 us
  starting transfers between devices: 278 us -> 0.16 us
  other arithmetic: 232 us -> 0.05 us
  blocking collectives: 215 us -> 92 us
  Pallas kernels: 0 us -> 60.7 us
  local copies, waits for them, and re-layouts: 78.9 us -> 20.1 us
  loops' own time: 58.5 us -> 0 us
  matrix products: 33.3 us -> 0 us
    ppermute x22 -> x0, waiting for transfers between devices: 581 us -> none  [passed_along(): return lax.ppermute(block, axis, route)]
    ppermute x22 -> x0, starting transfers between devices: 278 us -> none  [passed_along(): return lax.ppermute(block, axis, route)]
    psum x2 -> x1, waiting for transfers between devices: 286 us -> 118 us  [shards(): point_sum, kernel_sum = lax.psum((point_sum, kernel_sum), 'dp')]
    reduce_scatter x0 -> x2, waiting for transfers between devices: none -> 148 us  [the longest x1 120 us: shards(): point_sum = lax.psum_scatter(point_part, 'pipe')]
    psum x1, blocking collectives: 215 us -> 76 us  [shards(): total_loss = lax.psum(loss_part[0, 0], ('pipe', 'dp'))]
    scatter x42 -> x0, other arithmetic: 111 us -> none  [the longest x21 58.4 us: forward_compute(): saved_in = saved_in.at[slot_index, cell_slot].set(current)]
    pallas_call x0 -> x1, Pallas kernels: none -> 60.7 us  [run_cells(): pl.pallas_call(cells_kernel, out_shape=(jax.ShapeDtypeStruct((slots, chan...]
    another operation x73 -> x0, loops' own time: 58.5 us -> none  [the longest x1 19.5 us: shards(): lax.fori_loop(0, ticks, forward_tick, start_state)]
  transfers between devices with their start and end apart: 24 -> 4, of which waited for: 24 -> 4; matrix products, arithmetic and copies ran while one was open for 0% -> 3% of each run, Pallas kernels for 0% -> 0%
where the time goes in v1:
time: 505 us; the launch traced here: 504 us
  waiting for transfers between devices  317 us (63%)
  blocking collectives  92 us (18%)
  Pallas kernels  60.7 us (12%)
  local copies, waits for them, and re-layouts  20.1 us (4%)
  between operations  14.5 us (3%)
    reduce_scatter x1, waiting for transfers between devices, shards(): point_sum = lax.psum_scatter(point_part, 'pipe')  120 us
    psum x1, waiting for transfers between devices, shards(): point_sum, kernel_sum = lax.psum((point_sum, kernel_sum), 'dp')  118 us
    psum x1, blocking collectives, shards(): total_loss = lax.psum(loss_part[0, 0], ('pipe', 'dp'))  76 us
    pallas_call x1, Pallas kernels, run_cells(): pl.pallas_call(cells_kernel, out_shape=(jax.ShapeDtypeStruct((slots, chan...  60.7 us
    all_gather x1, waiting for transfers between devices, shards(): weights = lax.all_gather(point_weight[0], 'pipe')  48.6 us
    reduce_scatter x1, waiting for transfers between devices, shards(): kernel_sum = lax.psum_scatter(kernel_part, 'pipe')  27.9 us
    all_gather x1, blocking collectives, shards(): taps = lax.all_gather(taps, 'pipe')  16 us
  transfers between devices with their start and end apart: 4, of which 4 were waited for; matrix products, arithmetic and copies ran while one was open for 3% of the time, Pallas kernels for 0%

profile of v1, /device:TPU:1, one launch (start us, length us, event | category | flops | bytes accessed | tf_op | source)
XLA Modules:
  0.0 504.2 jit_solution(11734305447470737382)
XLA Ops:
  7.2 0.0 copy-start
  7.2 0.0 copy-start.2
  7.2 0.0 copy-start.1
  7.2 0.0 all-gather.3.cloned.1.call-start
  7.2 0.7 all-gather.3.cloned.1.call-update
  7.9 0.0 reduce-scatter.5.cloned.1.call-start
  8.7 0.7 copy.31.live_ref
  9.4 0.0 copy-done
  9.4 0.6 gather_fusion
  10.0 0.7 copy.30.targets_ref
  10.7 0.7 pad.29
  11.4 0.8 pad.31
  12.3 0.0 copy-done.2
  12.3 0.0 copy-done.1
  12.3 1.8 copy.32.head_ref
  14.2 4.1 reshape.69
  18.2 1.2 constant_dynamic-slice_fusion
  19.5 1.1 copy.35
  20.7 16.0 %all-gather.taps_ref = bf16[12,64,512]{2,1,0:T(8,128)(2,1)} all-gather(bf16[3,64,512]{2,1,0:T(8,128)(2,1)S(1)} %fusion.5), channel_id=2, replica_groups=mesh['pipe'=4,'dp'=64] {'pipe'}, dimensions={0}, use_global_device_ids=true | all-gather | bytes 983040 | tf_op jit(solution)/shard_map/all_gather | solution.py:284
  36.6 48.6 %all-gather.3.cloned.1.call-done = bf16[4,3,512,512]{3,2,1,0:T(8,128)(2,1)} async-done(((bf16[1,3,512,512]{3,2,1,0:T(8,128)(2,1)}), bf16[4,3,512,512]{3,2,1,0:T(8,128)(2,1)}) %all-gather.3.cloned.1.call-update) | async-done | bytes 6291472 | tf_op jit(solution)/shard_map/all_gather | solution.py:280
  85.2 60.7 %cells.1 = (f32[12,512,512]{2,1,0:T(8,128)}, f32[12,64,512]{2,1,0:T(8,128)}, f32[8,128]{1,0:T(8,128)}) custom-call(s32[4]{0:T(128)} %cells_ref.1, bf16[576,512]{1,0:T(8,128)(2,1)} %bitcast.24, s32[8,1]{1,0:T(8,128)} %copy.30.targets_ref, f32[8,1]{1,0:T(8,128)} %copy.31.live_ref, bf16[12,512,512]{2,1,0:T(8,128)(2,1)} %bitcast.23, ...), custom_call_target="tpu_custom_call" | custom-call | tf_op jit(solution)/shard_map/cells/pallas_call | solution.py:230
  145.9 0.0 reduce-scatter.5.cloned.1.call-update
  146.0 0.0 reduce-scatter.3.cloned.1.call-start
  146.0 0.7 reduce-scatter.3.cloned.1.call-update
  146.7 0.0 all-reduce.10.cloned.1.call-start
  146.7 27.9 %reduce-scatter.5.cloned.1.call-done = f32[1,3,64,512]{3,2,1,0:T(8,128)} async-done(((f32[4,3,64,512]{3,2,1,0:T(8,128)}), f32[1,3,64,512]{3,2,1,0:T(8,128)}) %reduce-scatter.5.cloned.1.call-update) | async-done | bytes 393232 | tf_op jit(solution)/shard_map/reduce_scatter | solution.py:310
  174.6 120.4 %reduce-scatter.3.cloned.1.call-done = f32[1,3,512,512]{3,2,1,0:T(8,128)} async-done(((f32[4,3,512,512]{3,2,1,0:T(8,128)}), f32[1,3,512,512]{3,2,1,0:T(8,128)}) %reduce-scatter.3.cloned.1.call-update) | async-done | bytes 3145744 | tf_op jit(solution)/shard_map/reduce_scatter | solution.py:309
  295.1 0.0 all-reduce.10.cloned.1.call-update
  295.1 1.2 slice.27
  296.3 76.0 %psum.21 = f32[]{:T(128)} all-reduce(f32[]{:T(128)} %bitcast.6), channel_id=1, replica_groups=mesh['pipe'=4,'dp'=64] {'pipe','dp'}, use_global_device_ids=true, to_apply=%region_0.1 | all-reduce | flops 1 | bytes 8 | tf_op jit(solution)/shard_map/psum | solution.py:312
  372.3 118.4 %all-reduce.10.cloned.1.call-done = (f32[1,3,512,512]{3,2,1,0:T(8,128)}, f32[3,64,512]{2,1,0:T(8,128)}) async-done(((f32[1,3,512,512]{3,2,1,0:T(8,128)}, f32[3,64,512]{2,1,0:T(8,128)}), (f32[1,3,512,512]{3,2,1,0:T(8,128)}, f32[3,64,512]{2,1,0:T(8,128)})) %all-reduce.10.cloned.1.call-update) | async-done | bytes 3538960 | tf_op jit(solution)/shard_map/psum | solution.py:311
  490.7 1.0 fusion.9
  491.7 0.8 broadcast_in_dim_reshape.3
  492.5 0.7 copy.34
  493.2 0.6 copy.33
  493.8 3.9 copy.39
  (13 shorter events, 0.2 us)
Async XLA Ops:
  7.2 2.2 copy-start
  7.2 5.1 %copy-start.2 = (bf16[1,7,7,512]{3,2,1,0:T(8,128)(2,1)S(1)}, bf16[1,7,7,512]{3,2,1,0:T(8,128)(2,1)}, u32[]{:S(2)}) copy-start(bf16[1,7,7,512]{3,2,1,0:T(8,128)(2,1)} %param.20) | copy-start | bytes 150532
  7.2 5.1 %copy-start.1 = (f32[512,1000]{0,1:T(8,128)S(1)}, f32[512,1000]{0,1:T(8,128)}, u32[]{:S(2)}) copy-start(f32[512,1000]{0,1:T(8,128)} %param.21) | copy-start | bytes 6144004
  7.2 78.0 %all-gather.3.cloned.1.call-start = ((), (), s32[]{:S(2)}) async-start(), calls=%async_computation.2 | async-start | bytes 7864320 | tf_op jit(solution)/shard_map/all_gather | solution.py:280
  7.9 166.7 %reduce-scatter.5.cloned.1.call-start = ((), (), s32[]{:S(2)}) async-start(), calls=%async_computation.4 | async-start | bytes 1966080 | tf_op jit(solution)/shard_map/reduce_scatter | solution.py:310
  146.0 149.1 %reduce-scatter.3.cloned.1.call-start = ((), (), s32[]{:S(2)}) async-start(), calls=%async_computation.3 | async-start | bytes 15728640 | tf_op jit(solution)/shard_map/reduce_scatter | solution.py:309
  146.7 344.0 %all-reduce.10.cloned.1.call-start = ((), (), s32[]{:S(2)}) async-start(), calls=%async_computation.5 | async-start | bytes 7077888 | tf_op jit(solution)/shard_map/psum | solution.py:311
Sparse Core Ops, SparseCore 0:
  9.8 75.3 all-gather.2
  146.1 28.4 reduce-scatter.4
  177.2 117.7 reduce-scatter.2
  298.4 192.1 all-reduce.9

commit v2 on v1

--- a/solution.py
+++ b/solution.py
@@ -19,6 +19,19 @@
 CYCLE = SIDE + TAPS // 2
 HALF = 128
 IMAGES = 4
+CHIPS_X = 4
+CHIPS_Z = 8
+CORES = 2
+LANES = 128
+MESH = pl.DeviceIdType.MESH
+TAP_SPANS = (16, 32, 64)
+TAP_STARTS = (0, 16, 48)
+TAP_BLOCK = 112
+CHUNK = 112
+CHUNK_A = 64
+CHUNK_B = CHUNK - CHUNK_A
+BLOCK = CORES * CHIPS_Z * CHUNK
+WEIGHT_A = 96
 
 
 def transform_tables():
@@ -34,25 +47,28 @@
     count = len(slots)
     waves = np.array(slots, np.float64)
     sites = np.array([(i, j) for i in range(SIDE) for j in range(SIDE)], np.float64)
-    reach = TAPS // 2
-    shifts = np.array(
-        [(u - reach, v - reach) for u in range(TAPS) for v in range(TAPS)], np.float64
-    )
     weight = np.where((waves == 0).all(1), 1.0, 2.0)[:, None] / CYCLE**2
     site_angle = 2 * np.pi * ((waves @ sites.T) % CYCLE) / CYCLE
-    tap_angle = 2 * np.pi * ((waves @ shifts.T) % CYCLE) / CYCLE
     into = np.zeros((2 * HALF, AREA))
     into[:count] = np.cos(site_angle)
     into[HALF : HALF + count] = -np.sin(site_angle)
     back = np.zeros((AREA, 2 * HALF))
     back[:, :count] = (np.cos(site_angle) * weight).T
     back[:, HALF : HALF + count] = -(np.sin(site_angle) * weight).T
-    tap_into = np.zeros((2 * HALF, TAP_ROWS))
-    tap_into[:count, : TAPS * TAPS] = np.cos(tap_angle)
-    tap_into[HALF : HALF + count, : TAPS * TAPS] = np.sin(tap_angle)
-    tap_back = np.zeros((TAP_ROWS, 2 * HALF))
-    tap_back[: TAPS * TAPS, :count] = (np.cos(tap_angle) * weight).T
-    tap_back[: TAPS * TAPS, HALF : HALF + count] = -(np.sin(tap_angle) * weight).T
+    tap_into = np.zeros((CELLS_MAX, 2 * HALF, TAP_ROWS))
+    tap_back = np.zeros((CELLS_MAX, TAP_ROWS, 2 * HALF))
+    for slot in range(CELLS_MAX):
+        size = 2 * slot + 3
+        reach = size // 2
+        shifts = np.array(
+            [(u - reach, v - reach) for u in range(size) for v in range(size)], np.float64
+        )
+        taps = size * size
+        tap_angle = 2 * np.pi * ((waves @ shifts.T) % CYCLE) / CYCLE
+        tap_into[slot, :count, :taps] = np.cos(tap_angle)
+        tap_into[slot, HALF : HALF + count, :taps] = np.sin(tap_angle)
+        tap_back[slot, :taps, :count] = (np.cos(tap_angle) * weight).T
+        tap_back[slot, :taps, HALF : HALF + count] = -(np.sin(tap_angle) * weight).T
     return [pair_of(table) for table in (into, back, tap_into, tap_back)]
 
 
@@ -74,6 +90,7 @@
 
 def cells_kernel(
     cells_ref,
+    device_ref,
     features_ref,
     targets_ref,
     live_ref,
@@ -84,9 +101,7 @@
     back_ref,
     tap_into_ref,
     tap_back_ref,
-    point_ref,
-    kernel_ref,
-    loss_ref,
+    grad_ref,
     order_ref,
     acts_ref,
     deep_ref,
@@ -95,7 +110,10 @@
     deep_cot_ref,
     total_ref,
 ):
-    sections = weight_ref.shape[0] // CELLS_MAX
+    slots, channels = weight_ref.shape[0], weight_ref.shape[-1]
+    sections = slots // CELLS_MAX
+    point_rows = CELLS_MAX * channels
+    loss_start = point_rows + TAP_BLOCK
     count = jnp.int32(0)
     for section in range(sections):
         held = cells_ref[section]
@@ -104,9 +122,14 @@
         for slot in range(1, CELLS_MAX):
 
             @pl.when(slot >= held)
-            def _(cell=section * CELLS_MAX + slot):
-                point_ref[cell] = jnp.zeros(point_ref.shape[1:], point_ref.dtype)
-                kernel_ref[cell] = jnp.zeros(kernel_ref.shape[1:], kernel_ref.dtype)
+            def _(start=section * BLOCK, slot=slot):
+                grad_ref[start + slot * channels : start + (slot + 1) * channels] = jnp.zeros(
+                    (channels, channels), jnp.bfloat16
+                )
+                taps = start + point_rows + TAP_STARTS[slot]
+                grad_ref[taps : taps + TAP_SPANS[slot]] = jnp.zeros(
+                    (TAP_SPANS[slot], channels), jnp.bfloat16
+                )
 
         count = count + held
 
@@ -117,8 +140,9 @@
 
     def forward(step, _):
         cell = order_ref[step]
+        slot = lax.rem(cell, CELLS_MAX)
         taps = taps_ref[cell]
-        wave = mul(tap_into_ref[0], taps) + mul(tap_into_ref[1], taps)
+        wave = mul(tap_into_ref[0, slot], taps) + mul(tap_into_ref[1, slot], taps)
         wave_ref[step] = wave
         wave_re, wave_im = wave[:HALF], wave[HALF:]
         for image in range(IMAGES):
@@ -145,7 +169,7 @@
         jnp.sum(acts_ref[count, rows_of(image)].astype(jnp.float32), axis=0, keepdims=True)
         for image in range(IMAGES)
     ]
-    spare = jnp.zeros((8 - IMAGES, features_ref.shape[1]), jnp.float32)
+    spare = jnp.zeros((8 - IMAGES, channels), jnp.float32)
     pooled = jnp.concatenate(means + [spare], axis=0) / AREA
     head = head_ref[...]
     scores = jnp.dot(
@@ -159,9 +183,6 @@
     onehot = (classes == targets_ref[...]).astype(jnp.float32)
     live = live_ref[...]
     row_loss = (jnp.log(total) - jnp.sum(logits * onehot, axis=1, keepdims=True)) * live
-    loss_ref[...] = jnp.broadcast_to(
-        jnp.sum(row_loss, axis=0, keepdims=True), loss_ref.shape
-    )
     score_cot = (exponent / total - onehot) * live * (1.0 - capped * capped)
     pooled_cot = lax.dot_general(
         score_cot,
@@ -173,16 +194,35 @@
     spread = pooled_cot / AREA
     for image in range(IMAGES):
         cot_ref[rows_of(image)] = jnp.broadcast_to(
-            spread[image : image + 1], (AREA, spread.shape[1])
+            spread[image : image + 1], (AREA, channels)
         ).astype(jnp.bfloat16)
+
+    loss = jnp.broadcast_to(jnp.sum(row_loss, axis=0, keepdims=True), (16, channels))
+    high = loss.astype(jnp.bfloat16).astype(jnp.float32)
+    middle = (loss - high).astype(jnp.bfloat16).astype(jnp.float32)
+    low = loss - high - middle
+    part = lax.broadcasted_iota(jnp.int32, loss.shape, 0)
+    own = lax.broadcasted_iota(jnp.int32, loss.shape, 1) == device_ref[0]
+    parts = jnp.where(part == 0, high, jnp.where(part == 1, middle, low))
+    parts = jnp.where(own & (part < 3), parts, 0.0).astype(jnp.bfloat16)
+    for section in range(sections):
+        start = section * BLOCK + loss_start
+        grad_ref[start : start + 16] = parts
+        grad_ref[start + 16 : (section + 1) * BLOCK] = jnp.zeros(
+            (BLOCK - loss_start - 16, channels), jnp.bfloat16
+        )
 
     def backward(turn, _):
         step = count - 1 - turn
         cell = order_ref[step]
+        section = lax.div(cell, CELLS_MAX)
+        slot = lax.rem(cell, CELLS_MAX)
+        start = pl.multiple_of(section * BLOCK, 16)
         cot = cot_ref[...]
-        point_ref[cell] = lax.dot_general(
+        point = pl.multiple_of(start + slot * channels, 16)
+        grad_ref[pl.ds(point, channels)] = lax.dot_general(
             deep_ref[step], cot, (((0,), (0,)), ((), ())), preferred_element_type=jnp.float32
-        )
+        ).astype(jnp.bfloat16)
         deep_cot_ref[...] = lax.dot_general(
             cot, weight_ref[cell], (((1,), (1,)), ((), ())), preferred_element_type=jnp.float32
         ).astype(jnp.bfloat16)
@@ -214,28 +254,34 @@
                 + jnp.where(acts.astype(jnp.float32) > 0, rect_cot, 0.0)
             ).astype(jnp.bfloat16)
         high, low = halves(total_ref[...])
-        kernel_ref[cell] = (
-            mul(tap_back_ref[0], high) + mul(tap_back_ref[0], low) + mul(tap_back_ref[1], high)
-        )
+        taps = (
+            mul(tap_back_ref[0, slot], high)
+            + mul(tap_back_ref[0, slot], low)
+            + mul(tap_back_ref[1, slot], high)
+        ).astype(jnp.bfloat16)
+        for kind in range(CELLS_MAX):
+
+            @pl.when(slot == kind)
+            def _(kind=kind):
+                row = pl.multiple_of(start + point_rows + TAP_STARTS[kind], 16)
+                grad_ref[pl.ds(row, TAP_SPANS[kind])] = taps[: TAP_SPANS[kind]]
+
         return 0
 
     lax.fori_loop(0, count, backward, 0)
 
 
-def run_cells(cells, features, targets, live, weights, taps, head):
+def run_cells(cells, device, features, targets, live, weights, taps, head):
     slots, channels = weights.shape[0], weights.shape[-1]
     tables = [jnp.asarray(table) for table in transform_tables()]
     vmem = pl.BlockSpec(memory_space=pltpu.VMEM)
+    smem = pl.BlockSpec(memory_space=pltpu.SMEM)
     rows = IMAGES * AREA
     return pl.pallas_call(
         cells_kernel,
-        out_shape=(
-            jax.ShapeDtypeStruct((slots, channels, channels), jnp.float32),
-            jax.ShapeDtypeStruct((slots, TAP_ROWS, channels), jnp.float32),
-            jax.ShapeDtypeStruct((8, 128), jnp.float32),
-        ),
-        in_specs=[pl.BlockSpec(memory_space=pltpu.SMEM)] + [vmem] * 10,
-        out_specs=(vmem, vmem, vmem),
+        out_shape=jax.ShapeDtypeStruct((slots // CELLS_MAX * BLOCK, channels), jnp.bfloat16),
+        in_specs=[smem, smem] + [vmem] * 10,
+        out_specs=vmem,
         scratch_shapes=[
             pltpu.SMEM((slots + CELLS_MAX,), jnp.int32),
             pltpu.VMEM((slots + 1, rows, channels), jnp.bfloat16),
@@ -247,20 +293,460 @@
         ],
         compiler_params=pltpu.CompilerParams(vmem_limit_bytes=60 * 1024 * 1024),
         name="cells",
-    )(cells, features, targets, live, weights, taps, head, *tables)
+    )(cells, device, features, targets, live, weights, taps, head, *tables)
+
+
+class Place:
+    def __init__(self, sections):
+        self.sections = sections
+        self.pipe = lax.axis_index("pipe")
+        place = lax.axis_index("dp")
+        self.core = lax.rem(place, CORES)
+        self.z = lax.rem(lax.div(place, CORES), CHIPS_Z)
+        self.x = lax.div(place, CORES * CHIPS_Z)
+
+    def device(self, pipe=0, x=0, z=0, core=0):
+        pipe = lax.rem(self.pipe + pipe, self.sections)
+        x = lax.rem(self.x + x, CHIPS_X)
+        z = lax.rem(self.z + z, CHIPS_Z)
+        core = lax.rem(self.core + core, CORES)
+        return (pipe, (x * CHIPS_Z + z) * CORES + core)
+
+    def greet(self, partners):
+        barrier = pltpu.get_barrier_semaphore()
+        for partner in partners:
+            pl.semaphore_signal(barrier, inc=1, device_id=partner, device_id_type=MESH)
+        pl.semaphore_wait(barrier, len(partners))
+
+
+def start_remote(source, target, send_sems, recv_sems, index, device):
+    copy = pltpu.make_async_remote_copy(
+        src_ref=source,
+        dst_ref=target,
+        send_sem=send_sems.at[index],
+        recv_sem=recv_sems.at[index],
+        device_id=device,
+        device_id_type=MESH,
+    )
+    copy.start()
+    return copy
+
+
+def start_local(source, target, sems, index):
+    copy = pltpu.make_async_copy(source, target, sems.at[index])
+    copy.start()
+    return copy
+
+
+def gather_kernel(
+    sections,
+    weight_ref,
+    taps_ref,
+    weights_ref,
+    all_taps_ref,
+    direct_send,
+    direct_recv,
+    split_send,
+    split_recv,
+    spread_send,
+    spread_recv,
+    taps_send,
+    taps_recv,
+    core_send,
+    core_recv,
+    local_sem,
+):
+    at = Place(sections)
+    others_y = range(1, sections)
+    others_x = range(1, CHIPS_X)
+    at.greet(
+        [at.device(pipe=d) for d in others_y]
+        + [at.device(x=d) for d in others_x]
+        + [at.device(core=1)]
+    )
+    core = at.core
+    lanes = pl.ds(pl.multiple_of(at.x * LANES, LANES), LANES)
+    cells = pl.ds(0, CELLS_MAX)
+    near = pl.ds(0, WEIGHT_A)
+    far = pl.ds(WEIGHT_A, weight_ref.shape[2] - WEIGHT_A)
+    split = [
+        start_remote(
+            weight_ref.at[cells, core, far, lanes],
+            weights_ref.at[at.pipe, cells, core, far, lanes],
+            split_send,
+            split_recv,
+            d - 1,
+            at.device(pipe=d),
+        )
+        for d in others_y
+    ]
+    direct = [
+        start_remote(
+            weight_ref.at[cells, core, near],
+            weights_ref.at[at.pipe, cells, core, near],
+            direct_send,
+            direct_recv,
+            d - 1,
+            at.device(pipe=d),
+        )
+        for d in others_y
+    ]
+    tap_copies = [
+        start_remote(
+            taps_ref, all_taps_ref.at[at.pipe], taps_send, taps_recv, d - 1, at.device(pipe=d)
+        )
+        for d in others_y
+    ]
+    local = [
+        start_local(weight_ref, weights_ref.at[at.pipe], local_sem, 0),
+        start_local(taps_ref, all_taps_ref.at[at.pipe], local_sem, 1),
+    ]
+    spread = []
+    for d in others_y:
+        split[d - 1].wait_recv()
+        source = lax.rem(at.pipe + sections - d, sections)
+        piece = weights_ref.at[source, cells, core, far, lanes]
+        spread.append(
+            [
+                start_remote(
+                    piece,
+                    piece,
+                    spread_send,
+                    spread_recv,
+                    (d - 1) * (CHIPS_X - 1) + e - 1,
+                    at.device(x=e),
+                )
+                for e in others_x
+            ]
+        )
+    shared = []
+    for d in others_y:
+        direct[d - 1].wait_recv()
+        for copy in spread[d - 1]:
+            copy.wait_recv()
+        source = lax.rem(at.pipe + sections - d, sections)
+        piece = weights_ref.at[source, cells, core]
+        shared.append(start_remote(piece, piece, core_send, core_recv, d - 1, at.device(core=1)))
+    for copy in local:
+        copy.wait()
+    for copy in tap_copies + shared:
+        copy.wait()
+    for copy in split + direct + [copy for copies in spread for copy in copies]:
+        copy.wait_send()
+
+
+def gather_weights(weight, taps, sections):
+    cells, channels = weight.shape[0], weight.shape[-1]
+    weight = weight.reshape(cells, CORES, channels // CORES, channels)
+    anywhere = pl.BlockSpec(memory_space=pl.ANY)
+    dma = pltpu.SemaphoreType.DMA
+    ys, xs = sections - 1, CHIPS_X - 1
+    weights, all_taps = pl.pallas_call(
+        functools.partial(gather_kernel, sections),
+        out_shape=(
+            jax.ShapeDtypeStruct((sections,) + weight.shape, weight.dtype),
+            jax.ShapeDtypeStruct((sections,) + taps.shape, taps.dtype),
+        ),
+        in_specs=[anywhere, anywhere],
+        out_specs=(anywhere, anywhere),
+        scratch_shapes=[
+            dma((ys,)),
+            dma((ys,)),
+            dma((ys,)),
+            dma((ys,)),
+            dma((ys * xs,)),
+            dma((ys * xs,)),
+            dma((ys,)),
+            dma((ys,)),
+            dma((ys,)),
+            dma((ys,)),
+            dma((2,)),
+        ],
+        compiler_params=pltpu.CompilerParams(collective_id=0, has_side_effects=True),
+        name="gather",
+    )(weight, taps)
+    return weights.reshape(sections * cells, channels, channels), all_taps
+
+
+def reduce_kernel(
+    sections,
+    grad_ref,
+    out_ref,
+    own_ref,
+    pair_ref,
+    part_a_ref,
+    part_b_ref,
+    in_a1_ref,
+    in_b1_ref,
+    mid_a_ref,
+    mid_b_ref,
+    in_a2_ref,
+    in_b2_ref,
+    small_ref,
+    in_z_ref,
+    line_ref,
+    plane_ref,
+    pair_send,
+    pair_recv,
+    a1_send,
+    a1_recv,
+    b1_send,
+    b1_recv,
+    a2_send,
+    a2_recv,
+    b2_send,
+    b2_recv,
+    z_send,
+    z_recv,
+    line_send,
+    line_recv,
+    plane_send,
+    plane_recv,
+    core_send,
+    core_recv,
+    local_sem,
+):
+    at = Place(sections)
+    others_y = range(1, sections)
+    others_x = range(1, CHIPS_X)
+    others_z = range(1, CHIPS_Z)
+    partner = at.device(core=1)
+    at.greet(
+        [partner]
+        + [at.device(pipe=d) for d in others_y]
+        + [at.device(x=d) for d in others_x]
+        + [at.device(z=d) for d in others_z]
+    )
+    f32 = jnp.float32
+    bf16 = jnp.bfloat16
+
+    def lanes(x):
+        return pl.ds(pl.multiple_of(x * LANES, LANES), LANES)
+
+    order = [lax.rem(at.pipe + d, sections) for d in (2, 1, 3, 0)]
+    paired, local = [], []
+    for k, section in enumerate(order):
+        paired.append(
+            start_remote(
+                grad_ref.at[section, lax.rem(at.core + 1, CORES)],
+                pair_ref.at[section],
+                pair_send,
+                pair_recv,
+                k,
+                partner,
+            )
+        )
+        local.append(start_local(grad_ref.at[section, at.core], own_ref.at[section], local_sem, k))
+    a1, b1 = {}, []
+    for k, section in enumerate(order):
+        local[k].wait()
+        paired[k].wait_recv()
+
+        def add_pair(z, _, section=section):
+            total = own_ref[section, z].astype(f32) + pair_ref[section, z].astype(f32)
+            part_a_ref[section, z] = total[:CHUNK_A].astype(bf16)
+            part_b_ref[section, z] = total[CHUNK_A:].astype(bf16)
+            return 0
+
+        lax.fori_loop(0, CHIPS_Z, add_pair, 0)
+        d = (2, 1, 3, 0)[k]
+        if d:
+            a1[d] = start_remote(
+                part_a_ref.at[section],
+                in_a1_ref.at[d - 1],
+                a1_send,
+                a1_recv,
+                d - 1,
+                at.device(pipe=d),
+            )
+        for e in others_x:
+            b1.append(
+                start_remote(
+                    part_b_ref.at[
+                        section,
+                        pl.ds(0, CHIPS_Z),
+                        pl.ds(0, CHUNK_B),
+                        lanes(lax.rem(at.x + e, CHIPS_X)),
+                    ],
+                    in_b1_ref.at[e - 1, section],
+                    b1_send,
+                    b1_recv,
+                    k * (CHIPS_X - 1) + e - 1,
+                    at.device(x=e),
+                )
+            )
+    b2 = {}
+    for k, section in enumerate(order):
+        for e in others_x:
+            b1[k * (CHIPS_X - 1) + e - 1].wait_recv()
+
+        def add_b1(z, _, section=section):
+            total = part_b_ref[section, z, :, lanes(at.x)].astype(f32)
+            for e in others_x:
+                total = total + in_b1_ref[e - 1, section, z].astype(f32)
+            mid_b_ref[section, z] = total.astype(bf16)
+            return 0
+
+        lax.fori_loop(0, CHIPS_Z, add_b1, 0)
+        d = (2, 1, 3, 0)[k]
+        if d:
+            b2[d] = start_remote(
+                mid_b_ref.at[section],
+                in_b2_ref.at[d - 1],
+                b2_send,
+                b2_recv,
+                d - 1,
+                at.device(pipe=d),
+            )
+    for d in others_y:
+        a1[d].wait_recv()
+
+    def add_a1(z, _):
+        total = part_a_ref[at.pipe, z].astype(f32)
+        for d in others_y:
+            total = total + in_a1_ref[d - 1, z].astype(f32)
+        mid_a_ref[z] = total.astype(bf16)
+        return 0
+
+    lax.fori_loop(0, CHIPS_Z, add_a1, 0)
+    a2 = [
+        start_remote(
+            mid_a_ref.at[
+                pl.ds(0, CHIPS_Z), pl.ds(0, CHUNK_A), lanes(lax.rem(at.x + e, CHIPS_X))
+            ],
+            in_a2_ref.at[e - 1],
+            a2_send,
+            a2_recv,
+            e - 1,
+            at.device(x=e),
+        )
+        for e in others_x
+    ]
+    for d in others_y:
+        b2[d].wait_recv()
+    for copy in a2:
+        copy.wait_recv()
+
+    def add_second(z, _):
+        total_a = mid_a_ref[z, :, lanes(at.x)].astype(f32)
+        total_b = mid_b_ref[at.pipe, z].astype(f32)
+        for e in others_x:
+            total_a = total_a + in_a2_ref[e - 1, z].astype(f32)
+        for d in others_y:
+            total_b = total_b + in_b2_ref[d - 1, z].astype(f32)
+        small_ref[z, :CHUNK_A] = total_a.astype(bf16)
+        small_ref[z, CHUNK_A:] = total_b.astype(bf16)
+        return 0
+
+    lax.fori_loop(0, CHIPS_Z, add_second, 0)
+    to_z = [
+        start_remote(
+            small_ref.at[lax.rem(at.z + d, CHIPS_Z)],
+            in_z_ref.at[d - 1],
+            z_send,
+            z_recv,
+            d - 1,
+            at.device(z=d),
+        )
+        for d in others_z
+    ]
+    for copy in to_z:
+        copy.wait_recv()
+    total = small_ref[at.z].astype(f32)
+    for d in others_z:
+        total = total + in_z_ref[d - 1].astype(f32)
+    line_ref[at.z] = total.astype(bf16)
+    piece = line_ref.at[at.z]
+    line = [
+        start_remote(piece, piece, line_send, line_recv, d - 1, at.device(z=d)) for d in others_z
+    ]
+    for copy in line:
+        copy.wait_recv()
+    column = plane_ref.at[pl.ds(0, CHIPS_Z), pl.ds(0, CHUNK), lanes(at.x)]
+    plane = [
+        start_remote(line_ref, column, plane_send, plane_recv, e - 1, at.device(x=e))
+        for e in others_x
+    ]
+    own_column = start_local(line_ref, column, local_sem, 0)
+    own_column.wait()
+    for copy in plane:
+        copy.wait_recv()
+    half = out_ref.at[at.core]
+    last = start_remote(plane_ref, half, core_send, core_recv, 0, partner)
+    own_half = start_local(plane_ref, half, local_sem, 1)
+    own_half.wait()
+    last.wait()
+    for copy in paired + b1 + list(a1.values()) + list(b2.values()) + a2 + to_z + line + plane:
+        copy.wait_send()
+
+
+def reduce_grads(grads, sections):
+    channels = grads.shape[-1]
+    grads = grads.reshape(sections, CORES, CHIPS_Z, CHUNK, channels)
+    anywhere = pl.BlockSpec(memory_space=pl.ANY)
+    dma = pltpu.SemaphoreType.DMA
+    ys, xs, zs = sections - 1, CHIPS_X - 1, CHIPS_Z - 1
+
+    def vmem(*shape):
+        return pltpu.VMEM(shape, jnp.bfloat16)
+
+    out = pl.pallas_call(
+        functools.partial(reduce_kernel, sections),
+        out_shape=jax.ShapeDtypeStruct((CORES, CHIPS_Z, CHUNK, channels), jnp.bfloat16),
+        in_specs=[anywhere],
+        out_specs=anywhere,
+        scratch_shapes=[
+            vmem(sections, CHIPS_Z, CHUNK, channels),
+            vmem(sections, CHIPS_Z, CHUNK, channels),
+            vmem(sections, CHIPS_Z, CHUNK_A, channels),
+            vmem(sections, CHIPS_Z, CHUNK_B, channels),
+            vmem(ys, CHIPS_Z, CHUNK_A, channels),
+            vmem(xs, sections, CHIPS_Z, CHUNK_B, LANES),
+            vmem(CHIPS_Z, CHUNK_A, channels),
+            vmem(sections, CHIPS_Z, CHUNK_B, LANES),
+            vmem(xs, CHIPS_Z, CHUNK_A, LANES),
+            vmem(ys, CHIPS_Z, CHUNK_B, LANES),
+            vmem(CHIPS_Z, CHUNK, LANES),
+            vmem(zs, CHUNK, LANES),
+            vmem(CHIPS_Z, CHUNK, LANES),
+            vmem(CHIPS_Z, CHUNK, channels),
+            dma((sections,)),
+            dma((sections,)),
+            dma((ys,)),
+            dma((ys,)),
+            dma((sections * xs,)),
+            dma((sections * xs,)),
+            dma((xs,)),
+            dma((xs,)),
+            dma((ys,)),
+            dma((ys,)),
+            dma((zs,)),
+            dma((zs,)),
+            dma((zs,)),
+            dma((zs,)),
+            dma((xs,)),
+            dma((xs,)),
+            dma((1,)),
+            dma((1,)),
+            dma((sections,)),
+        ],
+        compiler_params=pltpu.CompilerParams(
+            collective_id=1, has_side_effects=True, vmem_limit_bytes=40 * 1024 * 1024
+        ),
+        name="reduce",
+    )(grads)
+    return out.reshape(BLOCK, channels)
 
 
 def padded_taps(kernel):
-    edge = (TAPS - kernel.shape[1]) // 2
-    wide = jnp.pad(kernel, ((0, 0), (edge, edge), (edge, edge), (0, 0)))
-    flat = wide.reshape(kernel.shape[0], TAPS * TAPS, kernel.shape[-1])
-    return jnp.pad(flat, ((0, 0), (0, TAP_ROWS - TAPS * TAPS), (0, 0)))
-
-
-def own_taps(rows, size):
-    edge = (TAPS - size) // 2
-    window = rows[: TAPS * TAPS].reshape(TAPS, TAPS, rows.shape[-1])
-    return window[edge : edge + size, edge : edge + size]
+    flat = kernel[0].reshape(-1, kernel.shape[-1])
+    return jnp.pad(flat, ((0, TAP_ROWS - flat.shape[0]), (0, 0)))
+
+
+def own_taps(block, slot, start):
+    size = 2 * slot + 3
+    rows = block[start + TAP_STARTS[slot] :][: size * size].astype(jnp.float32)
+    return rows.reshape(1, size, size, block.shape[-1])
 
 
 def shards(
@@ -277,12 +763,8 @@
     sections = lax.axis_size("pipe")
     section_index = lax.axis_index("pipe")
     channels = point_weight.shape[-1]
-    weights = lax.all_gather(point_weight[0], "pipe")
-    taps = jnp.concatenate(
-        [padded_taps(kernel) for kernel in (depth_three, depth_five, depth_seven)], axis=0
-    )
-    taps = lax.all_gather(taps, "pipe")
-    slots = sections * CELLS_MAX
+    taps = jnp.stack([padded_taps(kernel) for kernel in (depth_three, depth_five, depth_seven)])
+    weights, taps = gather_weights(point_weight[0], taps, sections)
 
     per_replica = features.shape[0]
     share = per_replica // sections
@@ -294,28 +776,29 @@
     own_labels = labels[image]
     live = jnp.pad(own_live, (0, 8 - share))[:, None]
     targets = jnp.pad(own_labels, (0, 8 - share))[:, None]
-
-    point_part, kernel_part, loss_part = run_cells(
+    device = (lax.axis_index("dp") * sections + section_index)[None]
+
+    grads = run_cells(
         cells_per_section,
+        device,
         own,
         targets,
         live,
-        weights.reshape(slots, channels, channels),
-        taps.reshape(slots, TAP_ROWS, channels),
+        weights,
+        taps.reshape(sections * CELLS_MAX, TAP_ROWS, channels),
         head_weight,
     )
-    point_part = point_part.reshape(sections, CELLS_MAX, channels, channels)
-    kernel_part = kernel_part.reshape(sections, CELLS_MAX, TAP_ROWS, channels)
-    point_sum = lax.psum_scatter(point_part, "pipe")
-    kernel_sum = lax.psum_scatter(kernel_part, "pipe")
-    point_sum, kernel_sum = lax.psum((point_sum, kernel_sum), "dp")
-    total_loss = lax.psum(loss_part[0, 0], ("pipe", "dp"))
+    block = reduce_grads(grads, sections)
+    taps_start = CELLS_MAX * channels
+    loss_start = taps_start + TAP_BLOCK
+    total_loss = jnp.sum(block[loss_start : loss_start + 3].astype(jnp.float32))
+    point_sum = block[:taps_start].astype(jnp.float32)
     return (
         total_loss,
-        point_sum[None],
-        own_taps(kernel_sum[0], 3)[None],
-        own_taps(kernel_sum[1], 5)[None],
-        own_taps(kernel_sum[2], 7)[None],
+        point_sum.reshape(1, CELLS_MAX, channels, channels),
+        own_taps(block, 0, taps_start),
+        own_taps(block, 1, taps_start),
+        own_taps(block, 2, taps_start),
     )
 
 

time: 505 us -> 206 us (0.41)
  waiting for transfers between devices: 317 us -> 0 us
  Pallas kernels: 60.7 us -> 182 us
  blocking collectives: 92 us -> 0 us
  between operations: 14.5 us -> 1.39 us
    reduce_scatter x2 -> x0, waiting for transfers between devices: 148 us -> none  [the longest x1 120 us: shards(): point_sum = lax.psum_scatter(point_part, 'pipe')]
    pallas_call x1 -> x3, Pallas kernels: 60.7 us -> 182 us  [the longest x1 75.4 us: reduce_grads(): pl.pallas_call(functools.partial(reduce_kernel, sections), out_shape=jax....]
    psum x1 -> x0, waiting for transfers between devices: 118 us -> none  [shards(): point_sum, kernel_sum = lax.psum((point_sum, kernel_sum), 'dp')]
    psum x1 -> x0, blocking collectives: 76 us -> none  [shards(): total_loss = lax.psum(loss_part[0, 0], ('pipe', 'dp'))]
    all_gather x1 -> x0, waiting for transfers between devices: 48.6 us -> none  [shards(): weights = lax.all_gather(point_weight[0], 'pipe')]
    all_gather x1 -> x0, blocking collectives: 16 us -> none  [shards(): taps = lax.all_gather(taps, 'pipe')]
  transfers between devices with their start and end apart: 4 -> 0, of which waited for: 4 -> 0; matrix products, arithmetic and copies ran while one was open for 3% -> 0% of each run, Pallas kernels for 0% -> 0%
where the time goes in v2:
time: 206 us
  Pallas kernels  182 us (88%)
  local copies, waits for them, and re-layouts  19 us (9%)
  other arithmetic  3.45 us (2%)
    pallas_call x1, Pallas kernels, reduce_grads(): pl.pallas_call(functools.partial(reduce_kernel, sections), out_shape=jax....  75.4 us
    pallas_call x1, Pallas kernels, gather_weights(): pl.pallas_call(functools.partial(gather_kernel, sections), out_shape=(jax...  58.9 us
    pallas_call x1, Pallas kernels, run_cells(): pl.pallas_call(cells_kernel, out_shape=jax.ShapeDtypeStruct((slots // CEL...  47.8 us
    unnamed x6, local copies, waits for them, and re-layouts  7.12 us

profile of v2, /device:TPU:1, one launch (start us, length us, event | category | flops | bytes accessed | tf_op | source)
XLA Modules:
  0.0 205.9 jit_solution(10115424844338864239)
XLA Ops:
  0.6 0.0 copy-start
  1.3 0.7 copy.24.live_ref
  2.0 0.0 copy-done
  2.0 0.6 gather_fusion
  2.7 0.7 copy.23.targets_ref
  3.4 0.7 reshape_squeeze.13
  4.1 0.8 reshape_squeeze.14
  4.9 0.8 reshape_squeeze.15
  5.8 0.7 pad_maximum_fusion.taps_ref
  6.5 2.9 %copy.25.head_ref = f32[512,1000]{1,0:T(8,128)} copy(f32[512,1000]{0,1:T(8,128)} %param.21) | data formatting | bytes 4096000 | tf_op args[8]
  9.3 4.1 %reshape.72 = bf16[4,4,144,512]{3,1,0,2:T(4,128)(2,1)S(1)} reshape(bf16[16,12,12,512]{3,0,2,1:T(8,128)(2,1)} %param.13) | data formatting | bytes 4718592 | tf_op jit(solution)/shard_map/reshape | solution.py:771
  13.4 1.2 constant_dynamic-slice_fusion
  14.7 1.2 copy.26
  15.8 58.9 %gather.7 = (bf16[4,3,2,256,512]{4,3,2,1,0:T(8,128)(2,1)}, bf16[4,3,64,512]{3,2,1,0:T(8,128)(2,1)}) custom-call(bf16[3,2,256,512]{3,2,1,0:T(8,128)(2,1)} %bitcast.36, bf16[3,64,512]{2,1,0:T(8,128)(2,1)} %pad_maximum_fusion.taps_ref), custom_call_target="tpu_custom_call" | custom-call | tf_op jit(solution)/shard_map/gather/pallas_call | solution.py:444
  74.7 47.8 %cells.1 = bf16[7168,512]{1,0:T(8,128)(2,1)} custom-call(s32[4]{0:T(128)} %cells_ref.1, s32[1]{0:T(128)} %bitcast.device_ref, bf16[576,512]{1,0:T(8,128)(2,1)} %bitcast.35, s32[8,1]{1,0:T(8,128)} %copy.23.targets_ref, f32[8,1]{1,0:T(8,128)} %copy.24.live_ref, bf16[12,512,512]{2,1,0:T(8,128)(2,1)} %bitcast.33, bf16[12,64,512]{2,1,0:T(8,128)(2,1)} %bitcast.37, ...), custom_call_target="tpu_custom_call" | custom-call | tf_op jit(solution)/shard_map/cells/pallas_call | solution.py:280
  122.5 0.0 copy-start.1
  122.5 3.1 %copy-done.1 = bf16[7168,512]{1,0:T(8,128)(2,1)S(1)} copy-done((bf16[7168,512]{1,0:T(8,128)(2,1)S(1)}, bf16[7168,512]{1,0:T(8,128)(2,1)}, u32[]{:S(2)}) %copy-start.1) | copy-done | bytes 7340056
  125.6 75.4 %reduce.1 = bf16[2,8,112,512]{3,2,1,0:T(8,128)(2,1)S(1)} custom-call(bf16[4,2,8,112,512]{4,3,2,1,0:T(8,128)(2,1)S(1)} %bitcast.27), custom_call_target="tpu_custom_call" | custom-call | tf_op jit(solution)/shard_map/reduce/pallas_call | solution.py:693
  201.0 0.6 convert_reduce_fusion
  201.6 0.6 reshape.90
  202.2 0.7 reshape.92
  202.9 0.1 slice.29
  203.0 0.8 reshape.94
  203.8 2.1 %convert.7 = f32[1,3,512,512]{3,2,1,0:T(8,128)} convert(bf16[1,3,512,512]{3,2,1,0:T(8,128)(2,1)S(1)} %bitcast.34) | non-fusion elementwise | flops 786432 | bytes 4718592 | tf_op jit(solution)/shard_map/reshape | solution.py:798
  (10 shorter events, 0.1 us)
Async XLA Ops:
  0.6 1.4 copy-start
  122.5 3.1 %copy-start.1 = (bf16[7168,512]{1,0:T(8,128)(2,1)S(1)}, bf16[7168,512]{1,0:T(8,128)(2,1)}, u32[]{:S(2)}) copy-start(bf16[7168,512]{1,0:T(8,128)(2,1)} %cells.1) | copy-start | bytes 22020100

commit v3 on v2

--- a/solution.py
+++ b/solution.py
@@ -19,19 +19,22 @@
 CYCLE = SIDE + TAPS // 2
 HALF = 128
 IMAGES = 4
+GROUP = 16
 CHIPS_X = 4
 CHIPS_Z = 8
 CORES = 2
 LANES = 128
 MESH = pl.DeviceIdType.MESH
+TAP_HALVES = (0, 0, 1)
+TAP_STARTS = (0, 16, 0)
 TAP_SPANS = (16, 32, 64)
-TAP_STARTS = (0, 16, 48)
-TAP_BLOCK = 112
 CHUNK = 112
 CHUNK_A = 64
 CHUNK_B = CHUNK - CHUNK_A
-BLOCK = CORES * CHIPS_Z * CHUNK
-WEIGHT_A = 96
+HALF_ROWS = CHIPS_Z * CHUNK
+LOSS_ROWS = 16
+WEIGHT_A = 272
+CELLS_MB = 32
 
 
 def transform_tables():
@@ -63,12 +66,12 @@
         shifts = np.array(
             [(u - reach, v - reach) for u in range(size) for v in range(size)], np.float64
         )
-        taps = size * size
+        taps = slice(TAP_STARTS[slot], TAP_STARTS[slot] + size * size)
         tap_angle = 2 * np.pi * ((waves @ shifts.T) % CYCLE) / CYCLE
-        tap_into[slot, :count, :taps] = np.cos(tap_angle)
-        tap_into[slot, HALF : HALF + count, :taps] = np.sin(tap_angle)
-        tap_back[slot, :taps, :count] = (np.cos(tap_angle) * weight).T
-        tap_back[slot, :taps, HALF : HALF + count] = -(np.sin(tap_angle) * weight).T
+        tap_into[slot, :count, taps] = np.cos(tap_angle)
+        tap_into[slot, HALF : HALF + count, taps] = np.sin(tap_angle)
+        tap_back[slot, taps, :count] = (np.cos(tap_angle) * weight).T
+        tap_back[slot, taps, HALF : HALF + count] = -(np.sin(tap_angle) * weight).T
     return [pair_of(table) for table in (into, back, tap_into, tap_back)]
 
 
@@ -90,12 +93,10 @@
 
 def cells_kernel(
     cells_ref,
-    device_ref,
+    labels_ref,
+    live_count_ref,
     features_ref,
-    targets_ref,
-    live_ref,
     weight_ref,
-    taps_ref,
     head_ref,
     into_ref,
     back_ref,
@@ -110,10 +111,11 @@
     deep_cot_ref,
     total_ref,
 ):
-    slots, channels = weight_ref.shape[0], weight_ref.shape[-1]
-    sections = slots // CELLS_MAX
-    point_rows = CELLS_MAX * channels
-    loss_start = point_rows + TAP_BLOCK
+    sections, channels = weight_ref.shape[0], weight_ref.shape[-1]
+    span = channels // CORES
+    point_rows = CELLS_MAX * span
+    loss_start = point_rows + TAP_ROWS
+    pipe = lax.axis_index("pipe")
     count = jnp.int32(0)
     for section in range(sections):
         held = cells_ref[section]
@@ -122,12 +124,13 @@
         for slot in range(1, CELLS_MAX):
 
             @pl.when(slot >= held)
-            def _(start=section * BLOCK, slot=slot):
-                grad_ref[start + slot * channels : start + (slot + 1) * channels] = jnp.zeros(
-                    (channels, channels), jnp.bfloat16
-                )
-                taps = start + point_rows + TAP_STARTS[slot]
-                grad_ref[taps : taps + TAP_SPANS[slot]] = jnp.zeros(
+            def _(section=section, slot=slot):
+                for core in range(CORES):
+                    grad_ref[section, core, slot * span : (slot + 1) * span] = jnp.zeros(
+                        (span, channels), jnp.bfloat16
+                    )
+                row = point_rows + TAP_STARTS[slot]
+                grad_ref[section, TAP_HALVES[slot], row : row + TAP_SPANS[slot]] = jnp.zeros(
                     (TAP_SPANS[slot], channels), jnp.bfloat16
                 )
 
@@ -140,8 +143,9 @@
 
     def forward(step, _):
         cell = order_ref[step]
+        section = lax.div(cell, CELLS_MAX)
         slot = lax.rem(cell, CELLS_MAX)
-        taps = taps_ref[cell]
+        taps = weight_ref[section, lax.div(slot, CELLS_MAX - 1), point_rows:]
         wave = mul(tap_into_ref[0, slot], taps) + mul(tap_into_ref[1, slot], taps)
         wave_ref[step] = wave
         wave_re, wave_im = wave[:HALF], wave[HALF:]
@@ -159,7 +163,10 @@
             high, low = halves(mixed)
             deep = mul(back_ref[0], high) + mul(back_ref[0], low) + mul(back_ref[1], high)
             deep_ref[step, rows_of(image)] = deep.astype(jnp.bfloat16)
-        mixed = mul(deep_ref[step], weight_ref[cell])
+        rows = pl.ds(pl.multiple_of(slot * span, span), span)
+        mixed = mul(deep_ref[step, :, :span], weight_ref[section, 0, rows]) + mul(
+            deep_ref[step, :, span:], weight_ref[section, 1, rows]
+        )
         acts_ref[step + 1] = (acts_ref[step].astype(jnp.float32) + mixed).astype(jnp.bfloat16)
         return 0
 
@@ -172,24 +179,31 @@
     spare = jnp.zeros((8 - IMAGES, channels), jnp.float32)
     pooled = jnp.concatenate(means + [spare], axis=0) / AREA
     head = head_ref[...]
-    scores = jnp.dot(
-        pooled, head, precision=lax.Precision.HIGHEST, preferred_element_type=jnp.float32
+    scores = lax.dot_general(
+        pooled,
+        head,
+        (((1,), (1,)), ((), ())),
+        precision=lax.Precision.HIGHEST,
+        preferred_element_type=jnp.float32,
     )
     capped = jnp.tanh(scores / LOGIT_CAP)
     logits = LOGIT_CAP * capped
     exponent = jnp.exp(logits)
     total = jnp.sum(exponent, axis=1, keepdims=True)
     classes = lax.broadcasted_iota(jnp.int32, logits.shape, 1)
-    onehot = (classes == targets_ref[...]).astype(jnp.float32)
-    live = live_ref[...]
+    image_row = lax.broadcasted_iota(jnp.int32, (8, 1), 0)
+    targets = jnp.zeros((8, 1), jnp.int32)
+    live = jnp.zeros((8, 1), jnp.float32)
+    for image in range(IMAGES):
+        place = pipe + sections * image
+        is_live = (lax.div(place, MB_IMG) < live_count_ref[0]).astype(jnp.float32)
+        targets = jnp.where(image_row == image, labels_ref[place], targets)
+        live = jnp.where(image_row == image, is_live, live)
+    onehot = (classes == targets).astype(jnp.float32)
     row_loss = (jnp.log(total) - jnp.sum(logits * onehot, axis=1, keepdims=True)) * live
     score_cot = (exponent / total - onehot) * live * (1.0 - capped * capped)
-    pooled_cot = lax.dot_general(
-        score_cot,
-        head,
-        (((1,), (1,)), ((), ())),
-        precision=lax.Precision.HIGHEST,
-        preferred_element_type=jnp.float32,
+    pooled_cot = jnp.dot(
+        score_cot, head, precision=lax.Precision.HIGHEST, preferred_element_type=jnp.float32
     )
     spread = pooled_cot / AREA
     for image in range(IMAGES):
@@ -197,35 +211,43 @@
             spread[image : image + 1], (AREA, channels)
         ).astype(jnp.bfloat16)
 
-    loss = jnp.broadcast_to(jnp.sum(row_loss, axis=0, keepdims=True), (16, channels))
+    loss = jnp.broadcast_to(jnp.sum(row_loss, axis=0, keepdims=True), (LOSS_ROWS, channels))
     high = loss.astype(jnp.bfloat16).astype(jnp.float32)
     middle = (loss - high).astype(jnp.bfloat16).astype(jnp.float32)
     low = loss - high - middle
+    device = lax.axis_index("dp") * sections + pipe
     part = lax.broadcasted_iota(jnp.int32, loss.shape, 0)
-    own = lax.broadcasted_iota(jnp.int32, loss.shape, 1) == device_ref[0]
+    own = lax.broadcasted_iota(jnp.int32, loss.shape, 1) == device
     parts = jnp.where(part == 0, high, jnp.where(part == 1, middle, low))
     parts = jnp.where(own & (part < 3), parts, 0.0).astype(jnp.bfloat16)
     for section in range(sections):
-        start = section * BLOCK + loss_start
-        grad_ref[start : start + 16] = parts
-        grad_ref[start + 16 : (section + 1) * BLOCK] = jnp.zeros(
-            (BLOCK - loss_start - 16, channels), jnp.bfloat16
-        )
+        for core in range(CORES):
+            grad_ref[section, core, loss_start : loss_start + LOSS_ROWS] = parts
+            grad_ref[section, core, loss_start + LOSS_ROWS :] = jnp.zeros(
+                (HALF_ROWS - loss_start - LOSS_ROWS, channels), jnp.bfloat16
+            )
 
     def backward(turn, _):
         step = count - 1 - turn
         cell = order_ref[step]
         section = lax.div(cell, CELLS_MAX)
         slot = lax.rem(cell, CELLS_MAX)
-        start = pl.multiple_of(section * BLOCK, 16)
+        rows = pl.ds(pl.multiple_of(slot * span, span), span)
         cot = cot_ref[...]
-        point = pl.multiple_of(start + slot * channels, 16)
-        grad_ref[pl.ds(point, channels)] = lax.dot_general(
-            deep_ref[step], cot, (((0,), (0,)), ((), ())), preferred_element_type=jnp.float32
-        ).astype(jnp.bfloat16)
-        deep_cot_ref[...] = lax.dot_general(
-            cot, weight_ref[cell], (((1,), (1,)), ((), ())), preferred_element_type=jnp.float32
-        ).astype(jnp.bfloat16)
+        for core in range(CORES):
+            columns = slice(core * span, (core + 1) * span)
+            grad_ref[section, core, rows] = lax.dot_general(
+                deep_ref[step, :, columns],
+                cot,
+                (((0,), (0,)), ((), ())),
+                preferred_element_type=jnp.float32,
+            ).astype(jnp.bfloat16)
+            deep_cot_ref[:, columns] = lax.dot_general(
+                cot,
+                weight_ref[section, core, rows],
+                (((1,), (1,)), ((), ())),
+                preferred_element_type=jnp.float32,
+            ).astype(jnp.bfloat16)
         wave_re, wave_im = wave_ref[step, :HALF], wave_ref[step, HALF:]
         for image in range(IMAGES):
             acts = acts_ref[step, rows_of(image)]
@@ -263,24 +285,27 @@
 
             @pl.when(slot == kind)
             def _(kind=kind):
-                row = pl.multiple_of(start + point_rows + TAP_STARTS[kind], 16)
-                grad_ref[pl.ds(row, TAP_SPANS[kind])] = taps[: TAP_SPANS[kind]]
+                first, last = TAP_STARTS[kind], TAP_STARTS[kind] + TAP_SPANS[kind]
+                grad_ref[section, TAP_HALVES[kind], point_rows + first : point_rows + last] = taps[
+                    first:last
+                ]
 
         return 0
 
     lax.fori_loop(0, count, backward, 0)
 
 
-def run_cells(cells, device, features, targets, live, weights, taps, head):
-    slots, channels = weights.shape[0], weights.shape[-1]
+def run_cells(cells, labels, live_count, features, weights, head):
+    sections, channels = weights.shape[0], weights.shape[-1]
+    slots = sections * CELLS_MAX
     tables = [jnp.asarray(table) for table in transform_tables()]
     vmem = pl.BlockSpec(memory_space=pltpu.VMEM)
     smem = pl.BlockSpec(memory_space=pltpu.SMEM)
     rows = IMAGES * AREA
     return pl.pallas_call(
         cells_kernel,
-        out_shape=jax.ShapeDtypeStruct((slots // CELLS_MAX * BLOCK, channels), jnp.bfloat16),
-        in_specs=[smem, smem] + [vmem] * 10,
+        out_shape=jax.ShapeDtypeStruct((sections, CORES, HALF_ROWS, channels), jnp.bfloat16),
+        in_specs=[smem] * 3 + [vmem] * 7,
         out_specs=vmem,
         scratch_shapes=[
             pltpu.SMEM((slots + CELLS_MAX,), jnp.int32),
@@ -291,9 +316,9 @@
             pltpu.VMEM((rows, channels), jnp.bfloat16),
             pltpu.VMEM((2 * HALF, channels), jnp.float32),
         ],
-        compiler_params=pltpu.CompilerParams(vmem_limit_bytes=60 * 1024 * 1024),
+        compiler_params=pltpu.CompilerParams(vmem_limit_bytes=CELLS_MB * 1024 * 1024),
         name="cells",
-    )(cells, device, features, targets, live, weights, taps, head, *tables)
+    )(cells, labels, live_count, features, weights, head, *tables)
 
 
 class Place:
@@ -312,11 +337,13 @@
         core = lax.rem(self.core + core, CORES)
         return (pipe, (x * CHIPS_Z + z) * CORES + core)
 
-    def greet(self, partners):
+    def signal(self, partners):
         barrier = pltpu.get_barrier_semaphore()
         for partner in partners:
             pl.semaphore_signal(barrier, inc=1, device_id=partner, device_id_type=MESH)
-        pl.semaphore_wait(barrier, len(partners))
+
+    def wait(self, partners):
+        pl.semaphore_wait(pltpu.get_barrier_semaphore(), partners)
 
 
 def start_remote(source, target, send_sems, recv_sems, index, device):
@@ -341,131 +368,154 @@
 def gather_kernel(
     sections,
     weight_ref,
+    three_ref,
+    five_ref,
+    seven_ref,
+    features_ref,
+    weights_ref,
+    own_ref,
     taps_ref,
-    weights_ref,
-    all_taps_ref,
     direct_send,
     direct_recv,
     split_send,
     split_recv,
     spread_send,
     spread_recv,
-    taps_send,
-    taps_recv,
     core_send,
     core_recv,
-    local_sem,
+    weight_sem,
 ):
     at = Place(sections)
     others_y = range(1, sections)
     others_x = range(1, CHIPS_X)
-    at.greet(
+    core = at.core
+    channels = weights_ref.shape[-1]
+    span = channels // CORES
+    point_rows = CELLS_MAX * span
+    at.signal(
         [at.device(pipe=d) for d in others_y]
         + [at.device(x=d) for d in others_x]
         + [at.device(core=1)]
     )
-    core = at.core
-    lanes = pl.ds(pl.multiple_of(at.x * LANES, LANES), LANES)
-    cells = pl.ds(0, CELLS_MAX)
+    loads = []
+    for half in (core, lax.rem(core + 1, CORES)):
+        for cell in range(CELLS_MAX):
+            loads.append(
+                start_local(
+                    weight_ref.at[cell, half],
+                    weights_ref.at[at.pipe, half, pl.ds(cell * span, span)],
+                    weight_sem,
+                    len(loads),
+                )
+            )
+    taps_ref[...] = jnp.zeros_like(taps_ref)
+    for slot, ref in enumerate((three_ref, five_ref, seven_ref)):
+        size = 2 * slot + 3
+        for u in range(size):
+            row = TAP_STARTS[slot] + u * size
+            taps_ref[TAP_HALVES[slot], row : row + size] = ref[u].astype(jnp.float32)
+    for half in range(CORES):
+        weights_ref[at.pipe, half, point_rows:] = taps_ref[half].astype(jnp.bfloat16)
+    for copy in loads[:CELLS_MAX]:
+        copy.wait()
+    at.wait((sections - 1) + (CHIPS_X - 1) + 1)
+
     near = pl.ds(0, WEIGHT_A)
-    far = pl.ds(WEIGHT_A, weight_ref.shape[2] - WEIGHT_A)
-    split = [
-        start_remote(
-            weight_ref.at[cells, core, far, lanes],
-            weights_ref.at[at.pipe, cells, core, far, lanes],
-            split_send,
-            split_recv,
-            d - 1,
-            at.device(pipe=d),
+    far = pl.ds(WEIGHT_A, point_rows + TAP_ROWS - WEIGHT_A)
+
+    def lanes(x):
+        return pl.ds(pl.multiple_of(x * LANES, LANES), LANES)
+
+    split, direct = [], []
+    for d in others_y:
+        piece = weights_ref.at[at.pipe, core, far, lanes(at.x)]
+        split.append(
+            start_remote(piece, piece, split_send, split_recv, d - 1, at.device(pipe=d))
         )
-        for d in others_y
-    ]
-    direct = [
-        start_remote(
-            weight_ref.at[cells, core, near],
-            weights_ref.at[at.pipe, cells, core, near],
-            direct_send,
-            direct_recv,
-            d - 1,
-            at.device(pipe=d),
+    for d in others_y:
+        piece = weights_ref.at[at.pipe, core, near]
+        direct.append(
+            start_remote(piece, piece, direct_send, direct_recv, d - 1, at.device(pipe=d))
         )
-        for d in others_y
-    ]
-    tap_copies = [
-        start_remote(
-            taps_ref, all_taps_ref.at[at.pipe], taps_send, taps_recv, d - 1, at.device(pipe=d)
-        )
-        for d in others_y
-    ]
-    local = [
-        start_local(weight_ref, weights_ref.at[at.pipe], local_sem, 0),
-        start_local(taps_ref, all_taps_ref.at[at.pipe], local_sem, 1),
-    ]
-    spread = []
+    per_replica = features_ref.shape[0] // AREA
+    group = (GROUP * IMAGES, GROUP * per_replica)
+    row = lax.broadcasted_iota(jnp.int32, group, 0)
+    column = lax.broadcasted_iota(jnp.int32, group, 1)
+    wanted = lax.rem(row, GROUP) * per_replica + lax.div(row, GROUP) * sections + at.pipe
+    pick = (column == wanted).astype(jnp.float32).astype(jnp.bfloat16)
+    for g in range(AREA // GROUP):
+        picked = mul(pick, features_ref[g * group[1] : (g + 1) * group[1]]).astype(jnp.bfloat16)
+        for k in range(IMAGES):
+            row = k * AREA + g * GROUP
+            own_ref[row : row + GROUP] = picked[k * GROUP : (k + 1) * GROUP]
+
+    spread, shared = [], []
+
+    def share(piece):
+        k = len(shared)
+        shared.append(start_remote(piece, piece, core_send, core_recv, k, at.device(core=1)))
+
+    def source(d):
+        return lax.rem(at.pipe + sections - d, sections)
+
     for d in others_y:
         split[d - 1].wait_recv()
-        source = lax.rem(at.pipe + sections - d, sections)
-        piece = weights_ref.at[source, cells, core, far, lanes]
-        spread.append(
-            [
-                start_remote(
-                    piece,
-                    piece,
-                    spread_send,
-                    spread_recv,
-                    (d - 1) * (CHIPS_X - 1) + e - 1,
-                    at.device(x=e),
-                )
-                for e in others_x
-            ]
-        )
-    shared = []
+        piece = weights_ref.at[source(d), core, far, lanes(at.x)]
+        for e in others_x:
+            k = (d - 1) * (CHIPS_X - 1) + e - 1
+            spread.append(
+                start_remote(piece, piece, spread_send, spread_recv, k, at.device(x=e))
+            )
+        share(piece)
     for d in others_y:
         direct[d - 1].wait_recv()
-        for copy in spread[d - 1]:
-            copy.wait_recv()
-        source = lax.rem(at.pipe + sections - d, sections)
-        piece = weights_ref.at[source, cells, core]
-        shared.append(start_remote(piece, piece, core_send, core_recv, d - 1, at.device(core=1)))
-    for copy in local:
+        share(weights_ref.at[source(d), core, near])
+    for d in others_y:
+        for e in others_x:
+            spread[(d - 1) * (CHIPS_X - 1) + e - 1].wait_recv()
+            x = lax.rem(at.x + CHIPS_X - e, CHIPS_X)
+            share(weights_ref.at[source(d), core, far, lanes(x)])
+    for copy in loads[CELLS_MAX:]:
         copy.wait()
-    for copy in tap_copies + shared:
-        copy.wait()
-    for copy in split + direct + [copy for copies in spread for copy in copies]:
+    for copy in shared:
+        copy.wait_recv()
+    for copy in shared + split + direct + spread:
         copy.wait_send()
 
 
-def gather_weights(weight, taps, sections):
+def gather_weights(weight, three, five, seven, features, sections):
     cells, channels = weight.shape[0], weight.shape[-1]
     weight = weight.reshape(cells, CORES, channels // CORES, channels)
+    vmem = pl.BlockSpec(memory_space=pltpu.VMEM)
     anywhere = pl.BlockSpec(memory_space=pl.ANY)
     dma = pltpu.SemaphoreType.DMA
     ys, xs = sections - 1, CHIPS_X - 1
-    weights, all_taps = pl.pallas_call(
+    rows = cells * channels // CORES + TAP_ROWS
+    return pl.pallas_call(
         functools.partial(gather_kernel, sections),
         out_shape=(
-            jax.ShapeDtypeStruct((sections,) + weight.shape, weight.dtype),
-            jax.ShapeDtypeStruct((sections,) + taps.shape, taps.dtype),
+            jax.ShapeDtypeStruct((sections, CORES, rows, channels), weight.dtype),
+            jax.ShapeDtypeStruct((IMAGES * AREA, channels), features.dtype),
         ),
-        in_specs=[anywhere, anywhere],
-        out_specs=(anywhere, anywhere),
+        in_specs=[anywhere, vmem, vmem, vmem, vmem],
+        out_specs=(vmem, vmem),
         scratch_shapes=[
+            pltpu.VMEM((CORES, TAP_ROWS, channels), jnp.float32),
             dma((ys,)),
             dma((ys,)),
             dma((ys,)),
             dma((ys,)),
             dma((ys * xs,)),
             dma((ys * xs,)),
-            dma((ys,)),
-            dma((ys,)),
-            dma((ys,)),
-            dma((ys,)),
-            dma((2,)),
+            dma((2 * ys + ys * xs,)),
+            dma((2 * ys + ys * xs,)),
+            dma((CORES * cells,)),
         ],
-        compiler_params=pltpu.CompilerParams(collective_id=0, has_side_effects=True),
+        compiler_params=pltpu.CompilerParams(
+            collective_id=0, has_side_effects=True, vmem_limit_bytes=24 * 1024 * 1024
+        ),
         name="gather",
-    )(weight, taps)
-    return weights.reshape(sections * cells, channels, channels), all_taps
+    )(weight, three, five, seven, features)
 
 
 def reduce_kernel(
@@ -511,12 +561,13 @@
     others_x = range(1, CHIPS_X)
     others_z = range(1, CHIPS_Z)
     partner = at.device(core=1)
-    at.greet(
+    at.signal(
         [partner]
         + [at.device(pipe=d) for d in others_y]
         + [at.device(x=d) for d in others_x]
         + [at.device(z=d) for d in others_z]
     )
+    at.wait(1 + len(others_y) + len(others_x) + len(others_z))
     f32 = jnp.float32
     bf16 = jnp.bfloat16
 
@@ -681,7 +732,7 @@
 
 
 def reduce_grads(grads, sections):
-    channels = grads.shape[-1]
+    rows, channels = grads.shape[2:]
     grads = grads.reshape(sections, CORES, CHIPS_Z, CHUNK, channels)
     anywhere = pl.BlockSpec(memory_space=pl.ANY)
     dma = pltpu.SemaphoreType.DMA
@@ -735,17 +786,13 @@
         ),
         name="reduce",
     )(grads)
-    return out.reshape(BLOCK, channels)
-
-
-def padded_taps(kernel):
-    flat = kernel[0].reshape(-1, kernel.shape[-1])
-    return jnp.pad(flat, ((0, TAP_ROWS - flat.shape[0]), (0, 0)))
-
-
-def own_taps(block, slot, start):
+    return out.reshape(CORES, rows, channels)
+
+
+def own_taps(block, slot):
     size = 2 * slot + 3
-    rows = block[start + TAP_STARTS[slot] :][: size * size].astype(jnp.float32)
+    start = CELLS_MAX * block.shape[-1] // CORES + TAP_STARTS[slot]
+    rows = block[TAP_HALVES[slot], start : start + size * size].astype(jnp.float32)
     return rows.reshape(1, size, size, block.shape[-1])
 
 
@@ -761,44 +808,25 @@
     head_weight,
 ):
     sections = lax.axis_size("pipe")
-    section_index = lax.axis_index("pipe")
     channels = point_weight.shape[-1]
-    taps = jnp.stack([padded_taps(kernel) for kernel in (depth_three, depth_five, depth_seven)])
-    weights, taps = gather_weights(point_weight[0], taps, sections)
-
-    per_replica = features.shape[0]
-    share = per_replica // sections
-    grouped = features.reshape(share, sections, AREA, channels)
-    own = lax.dynamic_index_in_dim(grouped, section_index, 1, keepdims=False)
-    own = own.reshape(share * AREA, channels)
-    image = section_index + sections * lax.iota(jnp.int32, share)
-    own_live = (image // MB_IMG < micro_count[0]).astype(jnp.float32)
-    own_labels = labels[image]
-    live = jnp.pad(own_live, (0, 8 - share))[:, None]
-    targets = jnp.pad(own_labels, (0, 8 - share))[:, None]
-    device = (lax.axis_index("dp") * sections + section_index)[None]
-
-    grads = run_cells(
-        cells_per_section,
-        device,
-        own,
-        targets,
-        live,
-        weights,
-        taps.reshape(sections * CELLS_MAX, TAP_ROWS, channels),
-        head_weight,
+    by_position = features.transpose(1, 2, 0, 3).reshape(-1, channels)
+    weights, own = gather_weights(
+        point_weight[0], depth_three[0], depth_five[0], depth_seven[0], by_position, sections
     )
+    grads = run_cells(cells_per_section, labels, micro_count, own, weights, head_weight.T)
     block = reduce_grads(grads, sections)
-    taps_start = CELLS_MAX * channels
-    loss_start = taps_start + TAP_BLOCK
-    total_loss = jnp.sum(block[loss_start : loss_start + 3].astype(jnp.float32))
-    point_sum = block[:taps_start].astype(jnp.float32)
+    span = channels // CORES
+    point_rows = CELLS_MAX * span
+    loss_start = point_rows + TAP_ROWS
+    total_loss = jnp.sum(block[0, loss_start : loss_start + 3].astype(jnp.float32))
+    point_sum = block[:, :point_rows].reshape(CORES, CELLS_MAX, span, channels)
+    point_sum = point_sum.transpose(1, 0, 2, 3).astype(jnp.float32)
     return (
         total_loss,
         point_sum.reshape(1, CELLS_MAX, channels, channels),
-        own_taps(block, 0, taps_start),
-        own_taps(block, 1, taps_start),
-        own_taps(block, 2, taps_start),
+        own_taps(block, 0),
+        own_taps(block, 1),
+        own_taps(block, 2),
     )
 
 

time: 206 us -> 166 us (0.81)
  Pallas kernels: 182 us -> 153 us
  local copies, waits for them, and re-layouts: 19 us -> 7.75 us
    pallas_call x1, Pallas kernels: 58.9 us -> 32.7 us  [gather_weights(): pl.pallas_call(functools.partial(gather_kernel, sections), out_shape=(jax...]
    reshape x4 -> x1, local copies, waits for them, and re-layouts: 6.14 us -> 2.1 us  [shards(): point_sum.reshape(1, CELLS_MAX, channels, channels)]
    pallas_call x1, Pallas kernels: 75.4 us -> 71.4 us  [reduce_grads(): pl.pallas_call(functools.partial(reduce_kernel, sections), out_shape=jax....]
    another operation x5 -> x0, local copies, waits for them, and re-layouts: 2.39 us -> none  [the longest x3 2.37 us: padded_taps(): flat = kernel[0].reshape(-1, kernel.shape[-1])]
    reshape x4 -> x0, other arithmetic: 2.13 us -> none  [the longest x1 2.11 us: shards(): point_sum.reshape(1, CELLS_MAX, channels, channels)]
    unnamed x6 -> x27, local copies, waits for them, and re-layouts: 7.12 us -> 5.54 us
where the time goes in v3:
time: 166 us; the launch traced here: 165 us
  Pallas kernels  153 us (92%)
  local copies, waits for them, and re-layouts  7.75 us (5%)
  other arithmetic  2.65 us (2%)
    pallas_call x1, Pallas kernels, reduce_grads(): pl.pallas_call(functools.partial(reduce_kernel, sections), out_shape=jax....  71.4 us
    pallas_call x1, Pallas kernels, run_cells(): pl.pallas_call(cells_kernel, out_shape=jax.ShapeDtypeStruct((sections, CO...  49.4 us
    pallas_call x1, Pallas kernels, gather_weights(): pl.pallas_call(functools.partial(gather_kernel, sections), out_shape=(jax...  32.7 us
    unnamed x27, local copies, waits for them, and re-layouts  5.54 us

profile of v3, /device:TPU:1, one launch (start us, length us, event | category | flops | bytes accessed | tf_op | source)
XLA Modules:
  0.0 165.3 jit_solution(10293803760127121805)
XLA Ops:
  0.6 0.0 copy-start.10
  0.6 0.0 copy-start.11
  1.3 0.0 copy-start
  1.3 1.7 %copy-done = bf16[16,12,12,512]{3,0,2,1:T(8,128)(2,1)S(1)} copy-done((bf16[16,12,12,512]{3,0,2,1:T(8,128)(2,1)S(1)}, bf16[16,12,12,512]{3,0,2,1:T(8,128)(2,1)}, u32[]{:S(2)}) %copy-start) | copy-done | bytes 2359320
  3.0 0.0 copy-start.2
  3.0 1.4 copy-done.2
  4.4 0.0 copy-start.7
  4.4 0.8 copy-done.7
  5.2 0.0 copy-start.8
  5.2 0.8 copy-done.8
  6.0 0.0 copy-start.9
  6.0 0.7 copy-done.9
  6.7 0.0 copy-start.1
  6.7 0.0 copy-start.3
  6.7 0.0 copy-start.4
  6.7 0.0 copy-start.5
  6.7 0.0 copy-start.6
  6.7 32.7 %gather.1 = (bf16[4,2,832,512]{3,2,1,0:T(8,128)(2,1)S(1)}, bf16[576,512]{1,0:T(8,128)(2,1)S(1)}) custom-call(bf16[3,2,256,512]{3,2,1,0:T(8,128)(2,1)S(1)} %bitcast.29, bf16[3,3,512]{2,1,0:T(4,128)(2,1)S(1)} %bitcast.32, bf16[5,5,512]{2,1,0:T(8,128)(2,1)S(1)} %bitcast.31, bf16[7,7,512]{2,1,0:T(8,128)(2,1)S(1)} %bitcast.30, bf16[2304,512]{1,0:T(8,128)(2,1)S(1)} %bitcast.27), custom_call_target="tpu_custom_call" | custom-call | tf_op jit(solution)/shard_map/gather/pallas_call | solution.py:494
  39.4 0.0 copy-done.10
  39.4 0.0 copy-done.11
  39.4 0.0 copy-done.1
  39.4 0.0 copy-done.3
  39.4 0.0 copy-done.4
  39.5 0.0 copy-done.5
  39.5 0.0 copy-done.6
  39.5 49.4 %cells.1 = bf16[4,2,896,512]{3,2,1,0:T(8,128)(2,1)S(1)} custom-call(s32[4]{0:T(128)S(1)} %copy-done.10, s32[16]{0:T(128)S(1)} %copy-done.11, s32[1]{0:T(128)S(6)} %copy.26.live_count_ref, bf16[576,512]{1,0:T(8,128)(2,1)S(1)} %get-tuple-element.7.features_ref, bf16[4,2,832,512]{3,2,1,0:T(8,128)(2,1)S(1)} %get-tuple-element.8.weight_ref, ...), custom_call_target="tpu_custom_call" | custom-call | tf_op jit(solution)/shard_map/cells/pallas_call | solution.py:305
  88.8 71.4 %reduce.2 = bf16[2,8,112,512]{3,2,1,0:T(8,128)(2,1)S(1)} custom-call(bf16[4,2,8,112,512]{4,3,2,1,0:T(8,128)(2,1)S(1)} %bitcast.21), custom_call_target="tpu_custom_call" | custom-call | tf_op jit(solution)/shard_map/reduce/pallas_call | solution.py:744
  160.3 0.6 convert_reduce_fusion
  160.9 0.6 convert.7
  161.6 0.7 convert.8
  162.3 0.1 slice.21
  162.4 0.1 copy.25
  162.5 0.7 convert.9
  163.2 2.1 %copy.19 = f32[2,3,256,512]{3,2,0,1:T(8,128)} copy(bf16[2,3,256,512]{3,2,1,0:T(8,128)(2,1)S(1)} %bitcast.33) | data formatting | bytes 4718592 | tf_op jit(solution)/shard_map/reshape | solution.py:826
  (5 shorter events, 0.1 us)
Async XLA Ops:
  0.6 38.8 %copy-start.10 = (s32[4]{0:T(128)S(1)}, s32[4]{0:T(128)}, u32[]{:S(2)}) copy-start(s32[4]{0:T(128)} %cells_ref.1) | copy-start | bytes 52
  0.6 38.8 %copy-start.11 = (s32[16]{0:T(128)S(1)}, s32[16]{0:T(128)}, u32[]{:S(2)}) copy-start(s32[16]{0:T(128)} %labels_ref.1) | copy-start | bytes 196
  1.3 1.7 %copy-start = (bf16[16,12,12,512]{3,0,2,1:T(8,128)(2,1)S(1)}, bf16[16,12,12,512]{3,0,2,1:T(8,128)(2,1)}, u32[]{:S(2)}) copy-start(bf16[16,12,12,512]{3,0,2,1:T(8,128)(2,1)} %param.13) | copy-start | bytes 7077892
  3.0 1.4 copy-start.2
  4.4 0.8 copy-start.7
  5.2 0.8 copy-start.8
  6.0 0.7 copy-start.9
  6.7 32.7 %copy-start.1 = (f32[512,1000]{0,1:T(8,128)S(1)}, f32[512,1000]{0,1:T(8,128)}, u32[]{:S(2)}) copy-start(f32[512,1000]{0,1:T(8,128)} %param.21) | copy-start | bytes 6144004
  6.7 32.7 %copy-start.3 = (bf16[2,3,256,64]{3,2,1,0:T(8,128)(2,1)S(1)}, bf16[2,3,256,64]{3,2,1,0:T(8,128)(2,1)}, u32[]{:S(2)}) copy-start(bf16[2,3,256,64]{3,2,1,0:T(8,128)(2,1)} %constant.12.clone.tap_into_ref) | copy-start | bytes 589828
  6.7 32.7 %copy-start.4 = (bf16[2,256,144]{2,1,0:T(8,128)(2,1)S(1)}, bf16[2,256,144]{2,1,0:T(8,128)(2,1)}, u32[]{:S(2)}) copy-start(bf16[2,256,144]{2,1,0:T(8,128)(2,1)} %constant.10.clone.into_ref) | copy-start | bytes 442372
  6.7 32.7 %copy-start.5 = (bf16[2,3,64,256]{3,2,1,0:T(8,128)(2,1)S(1)}, bf16[2,3,64,256]{3,2,1,0:T(8,128)(2,1)}, u32[]{:S(2)}) copy-start(bf16[2,3,64,256]{3,2,1,0:T(8,128)(2,1)} %constant.13.clone.tap_back_ref) | copy-start | bytes 589828
  6.7 32.8 %copy-start.6 = (bf16[2,144,256]{2,1,0:T(8,128)(2,1)S(1)}, bf16[2,144,256]{2,1,0:T(8,128)(2,1)}, u32[]{:S(2)}) copy-start(bf16[2,144,256]{2,1,0:T(8,128)(2,1)} %constant.11.clone.back_ref) | copy-start | bytes 442372

commit v4 on v3

--- a/solution.py
+++ b/solution.py
@@ -17,7 +17,7 @@
 TAP_ROWS = 64
 LOGIT_CAP = 30.0
 CYCLE = SIDE + TAPS // 2
-HALF = 128
+HALF = 120
 IMAGES = 4
 GROUP = 16
 CHIPS_X = 4
@@ -29,11 +29,13 @@
 TAP_STARTS = (0, 16, 0)
 TAP_SPANS = (16, 32, 64)
 CHUNK = 112
-CHUNK_A = 64
-CHUNK_B = CHUNK - CHUNK_A
+STREAMS = ((0, 32), (32, 32), (64, 32), (96, 16))
+TURNS = (0, 1, 2, 3, 0, 1, 0, 2, 1, 0, 0, 3, 2, 1, 0, 1, 3, 2, 1, 2, 0, 3, 2, 3, 1, 3, 2, 3)
+FIRST_Z = 4
+LAST_Z = CHIPS_Z - FIRST_Z
 HALF_ROWS = CHIPS_Z * CHUNK
 LOSS_ROWS = 16
-WEIGHT_A = 272
+WEIGHT_A = 320
 CELLS_MB = 32
 
 
@@ -72,7 +74,7 @@
         tap_into[slot, HALF : HALF + count, taps] = np.sin(tap_angle)
         tap_back[slot, taps, :count] = (np.cos(tap_angle) * weight).T
         tap_back[slot, taps, HALF : HALF + count] = -(np.sin(tap_angle) * weight).T
-    return [pair_of(table) for table in (into, back, tap_into, tap_back)]
+    return [pair_of(into)[0], pair_of(back)[0], pair_of(tap_into), pair_of(tap_back)]
 
 
 def pair_of(table):
@@ -141,6 +143,12 @@
     def rows_of(image):
         return pl.ds(image * AREA, AREA)
 
+    def lanes_of(image):
+        return slice(image * channels, (image + 1) * channels)
+
+    def abreast(ref):
+        return jnp.concatenate([ref[rows_of(image)] for image in range(IMAGES)], axis=1)
+
     def forward(step, _):
         cell = order_ref[step]
         section = lax.div(cell, CELLS_MAX)
@@ -149,20 +157,23 @@
         wave = mul(tap_into_ref[0, slot], taps) + mul(tap_into_ref[1, slot], taps)
         wave_ref[step] = wave
         wave_re, wave_im = wave[:HALF], wave[HALF:]
+        seen = mul(into_ref[...], jnp.maximum(abreast(acts_ref.at[step]), 0))
+        mixed = []
         for image in range(IMAGES):
-            site = jnp.maximum(acts_ref[step, rows_of(image)], 0)
-            seen = mul(into_ref[0], site) + mul(into_ref[1], site)
-            seen_re, seen_im = seen[:HALF], seen[HALF:]
-            mixed = jnp.concatenate(
-                [
-                    seen_re * wave_re - seen_im * wave_im,
-                    seen_re * wave_im + seen_im * wave_re,
-                ],
-                axis=0,
-            )
-            high, low = halves(mixed)
-            deep = mul(back_ref[0], high) + mul(back_ref[0], low) + mul(back_ref[1], high)
-            deep_ref[step, rows_of(image)] = deep.astype(jnp.bfloat16)
+            lanes = lanes_of(image)
+            seen_re, seen_im = seen[:HALF, lanes], seen[HALF:, lanes]
+            mixed.append(
+                jnp.concatenate(
+                    [
+                        seen_re * wave_re - seen_im * wave_im,
+                        seen_re * wave_im + seen_im * wave_re,
+                    ],
+                    axis=0,
+                ).astype(jnp.bfloat16)
+            )
+        deep = mul(back_ref[...], jnp.concatenate(mixed, axis=1)).astype(jnp.bfloat16)
+        for image in range(IMAGES):
+            deep_ref[step, rows_of(image)] = deep[:, lanes_of(image)]
         rows = pl.ds(pl.multiple_of(slot * span, span), span)
         mixed = mul(deep_ref[step, :, :span], weight_ref[section, 0, rows]) + mul(
             deep_ref[step, :, span:], weight_ref[section, 1, rows]
@@ -249,12 +260,14 @@
                 preferred_element_type=jnp.float32,
             ).astype(jnp.bfloat16)
         wave_re, wave_im = wave_ref[step, :HALF], wave_ref[step, HALF:]
+        acts = abreast(acts_ref.at[step])
+        seen = mul(into_ref[...], jnp.maximum(acts, 0))
+        sent = mul(into_ref[...], abreast(deep_cot_ref))
+        mixed = []
         for image in range(IMAGES):
-            acts = acts_ref[step, rows_of(image)]
-            seen = mul(into_ref[0], jnp.maximum(acts, 0))
-            seen_re, seen_im = seen[:HALF], seen[HALF:]
-            sent = mul(into_ref[0], deep_cot_ref[rows_of(image)])
-            sent_re, sent_im = sent[:HALF], sent[HALF:]
+            lanes = lanes_of(image)
+            seen_re, seen_im = seen[:HALF, lanes], seen[HALF:, lanes]
+            sent_re, sent_im = sent[:HALF, lanes], sent[HALF:, lanes]
             part_re = seen_re * sent_re + seen_im * sent_im
             part_im = seen_im * sent_re - seen_re * sent_im
             if image == 0:
@@ -263,17 +276,21 @@
             else:
                 total_ref[:HALF] += part_re
                 total_ref[HALF:] += part_im
-            mixed = jnp.concatenate(
-                [
-                    sent_re * wave_re + sent_im * wave_im,
-                    sent_im * wave_re - sent_re * wave_im,
-                ],
-                axis=0,
-            ).astype(jnp.bfloat16)
-            rect_cot = mul(back_ref[0], mixed)
+            mixed.append(
+                jnp.concatenate(
+                    [
+                        sent_re * wave_re + sent_im * wave_im,
+                        sent_im * wave_re - sent_re * wave_im,
+                    ],
+                    axis=0,
+                ).astype(jnp.bfloat16)
+            )
+        rect_cot = mul(back_ref[...], jnp.concatenate(mixed, axis=1))
+        for image in range(IMAGES):
+            lanes = lanes_of(image)
+            passed = jnp.where(acts[:, lanes].astype(jnp.float32) > 0, rect_cot[:, lanes], 0.0)
             cot_ref[rows_of(image)] = (
-                cot_ref[rows_of(image)].astype(jnp.float32)
-                + jnp.where(acts.astype(jnp.float32) > 0, rect_cot, 0.0)
+                cot_ref[rows_of(image)].astype(jnp.float32) + passed
             ).astype(jnp.bfloat16)
         high, low = halves(total_ref[...])
         taps = (
@@ -522,10 +539,8 @@
     sections,
     grad_ref,
     out_ref,
-    own_ref,
     pair_ref,
-    part_a_ref,
-    part_b_ref,
+    part_ref,
     in_a1_ref,
     in_b1_ref,
     mid_a_ref,
@@ -554,7 +569,8 @@
     plane_recv,
     core_send,
     core_recv,
-    local_sem,
+    column_sem,
+    half_sem,
 ):
     at = Place(sections)
     others_y = range(1, sections)
@@ -570,173 +586,204 @@
     at.wait(1 + len(others_y) + len(others_x) + len(others_z))
     f32 = jnp.float32
     bf16 = jnp.bfloat16
+    order = (2, 1, 3, 0)
+    other_core = lax.rem(at.core + 1, CORES)
+    all_z = pl.ds(0, CHIPS_Z)
+    first_z = pl.ds(0, FIRST_Z)
+    last_z = pl.ds(FIRST_Z, LAST_Z)
+    last_all = pl.ds(0, LAST_Z)
 
     def lanes(x):
         return pl.ds(pl.multiple_of(x * LANES, LANES), LANES)
 
-    order = [lax.rem(at.pipe + d, sections) for d in (2, 1, 3, 0)]
-    paired, local = [], []
-    for k, section in enumerate(order):
-        paired.append(
-            start_remote(
-                grad_ref.at[section, lax.rem(at.core + 1, CORES)],
-                pair_ref.at[section],
+    def section_at(d):
+        return lax.rem(at.pipe + d, sections)
+
+    def stream(turn, start, size):
+        rows = pl.ds(start, size)
+        paired, a1, b1, a2, b2 = {}, {}, {}, {}, {}
+        for k, d in enumerate(order):
+            section = section_at(d)
+            paired[d] = start_remote(
+                grad_ref.at[section, other_core, all_z, rows],
+                pair_ref.at[section, all_z, rows],
                 pair_send,
                 pair_recv,
-                k,
+                turn * sections + k,
                 partner,
             )
-        )
-        local.append(start_local(grad_ref.at[section, at.core], own_ref.at[section], local_sem, k))
-    a1, b1 = {}, []
-    for k, section in enumerate(order):
-        local[k].wait()
-        paired[k].wait_recv()
-
-        def add_pair(z, _, section=section):
-            total = own_ref[section, z].astype(f32) + pair_ref[section, z].astype(f32)
-            part_a_ref[section, z] = total[:CHUNK_A].astype(bf16)
-            part_b_ref[section, z] = total[CHUNK_A:].astype(bf16)
-            return 0
-
-        lax.fori_loop(0, CHIPS_Z, add_pair, 0)
-        d = (2, 1, 3, 0)[k]
-        if d:
-            a1[d] = start_remote(
-                part_a_ref.at[section],
-                in_a1_ref.at[d - 1],
-                a1_send,
-                a1_recv,
-                d - 1,
-                at.device(pipe=d),
-            )
-        for e in others_x:
-            b1.append(
-                start_remote(
-                    part_b_ref.at[
-                        section,
-                        pl.ds(0, CHIPS_Z),
-                        pl.ds(0, CHUNK_B),
-                        lanes(lax.rem(at.x + e, CHIPS_X)),
-                    ],
-                    in_b1_ref.at[e - 1, section],
+        yield
+        for d in order:
+            section = section_at(d)
+            paired[d].wait_recv()
+
+            def add_pair(z, _, section=section):
+                total = grad_ref[section, at.core, z, rows].astype(f32)
+                total = total + pair_ref[section, z, rows].astype(f32)
+                part_ref[section, z, rows] = total.astype(bf16)
+                return 0
+
+            lax.fori_loop(0, CHIPS_Z, add_pair, 0)
+            if d:
+                a1[d] = start_remote(
+                    part_ref.at[section, first_z, rows],
+                    in_a1_ref.at[d - 1, first_z, rows],
+                    a1_send,
+                    a1_recv,
+                    turn * len(others_y) + d - 1,
+                    at.device(pipe=d),
+                )
+            for e in others_x:
+                b1[d, e] = start_remote(
+                    part_ref.at[section, last_z, rows, lanes(lax.rem(at.x + e, CHIPS_X))],
+                    in_b1_ref.at[e - 1, section, last_all, rows],
                     b1_send,
                     b1_recv,
-                    k * (CHIPS_X - 1) + e - 1,
+                    (turn * sections + d) * len(others_x) + e - 1,
                     at.device(x=e),
                 )
-            )
-    b2 = {}
-    for k, section in enumerate(order):
+        yield
+        for d in order:
+            section = section_at(d)
+            for e in others_x:
+                b1[d, e].wait_recv()
+
+            def add_b1(z, _, section=section):
+                total = part_ref[section, FIRST_Z + z, rows, lanes(at.x)].astype(f32)
+                for e in others_x:
+                    total = total + in_b1_ref[e - 1, section, z, rows].astype(f32)
+                mid_b_ref[section, z, rows] = total.astype(bf16)
+                return 0
+
+            lax.fori_loop(0, LAST_Z, add_b1, 0)
+            if d:
+                b2[d] = start_remote(
+                    mid_b_ref.at[section, last_all, rows],
+                    in_b2_ref.at[d - 1, last_all, rows],
+                    b2_send,
+                    b2_recv,
+                    turn * len(others_y) + d - 1,
+                    at.device(pipe=d),
+                )
+        for d in others_y:
+            a1[d].wait_recv()
+
+        def add_a1(z, _):
+            total = part_ref[at.pipe, z, rows].astype(f32)
+            for d in others_y:
+                total = total + in_a1_ref[d - 1, z, rows].astype(f32)
+            mid_a_ref[z, rows] = total.astype(bf16)
+            return 0
+
+        lax.fori_loop(0, FIRST_Z, add_a1, 0)
         for e in others_x:
-            b1[k * (CHIPS_X - 1) + e - 1].wait_recv()
-
-        def add_b1(z, _, section=section):
-            total = part_b_ref[section, z, :, lanes(at.x)].astype(f32)
+            a2[e] = start_remote(
+                mid_a_ref.at[first_z, rows, lanes(lax.rem(at.x + e, CHIPS_X))],
+                in_a2_ref.at[e - 1, first_z, rows],
+                a2_send,
+                a2_recv,
+                turn * len(others_x) + e - 1,
+                at.device(x=e),
+            )
+        yield
+        for d in others_y:
+            b2[d].wait_recv()
+        for e in others_x:
+            a2[e].wait_recv()
+
+        def add_a2(z, _):
+            total = mid_a_ref[z, rows, lanes(at.x)].astype(f32)
             for e in others_x:
-                total = total + in_b1_ref[e - 1, section, z].astype(f32)
-            mid_b_ref[section, z] = total.astype(bf16)
+                total = total + in_a2_ref[e - 1, z, rows].astype(f32)
+            small_ref[z, rows] = total.astype(bf16)
             return 0
 
-        lax.fori_loop(0, CHIPS_Z, add_b1, 0)
-        d = (2, 1, 3, 0)[k]
-        if d:
-            b2[d] = start_remote(
-                mid_b_ref.at[section],
-                in_b2_ref.at[d - 1],
-                b2_send,
-                b2_recv,
-                d - 1,
-                at.device(pipe=d),
-            )
-    for d in others_y:
-        a1[d].wait_recv()
-
-    def add_a1(z, _):
-        total = part_a_ref[at.pipe, z].astype(f32)
-        for d in others_y:
-            total = total + in_a1_ref[d - 1, z].astype(f32)
-        mid_a_ref[z] = total.astype(bf16)
-        return 0
-
-    lax.fori_loop(0, CHIPS_Z, add_a1, 0)
-    a2 = [
-        start_remote(
-            mid_a_ref.at[
-                pl.ds(0, CHIPS_Z), pl.ds(0, CHUNK_A), lanes(lax.rem(at.x + e, CHIPS_X))
-            ],
-            in_a2_ref.at[e - 1],
-            a2_send,
-            a2_recv,
-            e - 1,
-            at.device(x=e),
+        def add_b2(z, _):
+            total = mid_b_ref[at.pipe, z, rows].astype(f32)
+            for d in others_y:
+                total = total + in_b2_ref[d - 1, z, rows].astype(f32)
+            small_ref[FIRST_Z + z, rows] = total.astype(bf16)
+            return 0
+
+        lax.fori_loop(0, FIRST_Z, add_a2, 0)
+        lax.fori_loop(0, LAST_Z, add_b2, 0)
+        to_z = [
+            start_remote(
+                small_ref.at[lax.rem(at.z + d, CHIPS_Z), rows],
+                in_z_ref.at[d - 1, rows],
+                z_send,
+                z_recv,
+                turn * len(others_z) + d - 1,
+                at.device(z=d),
+            )
+            for d in others_z
+        ]
+        yield
+        for copy in to_z:
+            copy.wait_recv()
+        total = small_ref[at.z, rows].astype(f32)
+        for d in others_z:
+            total = total + in_z_ref[d - 1, rows].astype(f32)
+        line_ref[at.z, rows] = total.astype(bf16)
+        piece = line_ref.at[at.z, rows]
+        line = [
+            start_remote(
+                piece,
+                piece,
+                line_send,
+                line_recv,
+                turn * len(others_z) + d - 1,
+                at.device(z=d),
+            )
+            for d in others_z
+        ]
+        yield
+        for copy in line:
+            copy.wait_recv()
+        column = plane_ref.at[all_z, rows, lanes(at.x)]
+        plane = [
+            start_remote(
+                line_ref.at[all_z, rows],
+                column,
+                plane_send,
+                plane_recv,
+                turn * len(others_x) + e - 1,
+                at.device(x=e),
+            )
+            for e in others_x
+        ]
+        own_column = start_local(line_ref.at[all_z, rows], column, column_sem, turn)
+        yield
+        own_column.wait()
+        for copy in plane:
+            copy.wait_recv()
+        half = out_ref.at[at.core, all_z, rows]
+        last = start_remote(
+            plane_ref.at[all_z, rows], half, core_send, core_recv, turn, partner
         )
-        for e in others_x
-    ]
-    for d in others_y:
-        b2[d].wait_recv()
-    for copy in a2:
-        copy.wait_recv()
-
-    def add_second(z, _):
-        total_a = mid_a_ref[z, :, lanes(at.x)].astype(f32)
-        total_b = mid_b_ref[at.pipe, z].astype(f32)
-        for e in others_x:
-            total_a = total_a + in_a2_ref[e - 1, z].astype(f32)
-        for d in others_y:
-            total_b = total_b + in_b2_ref[d - 1, z].astype(f32)
-        small_ref[z, :CHUNK_A] = total_a.astype(bf16)
-        small_ref[z, CHUNK_A:] = total_b.astype(bf16)
-        return 0
-
-    lax.fori_loop(0, CHIPS_Z, add_second, 0)
-    to_z = [
-        start_remote(
-            small_ref.at[lax.rem(at.z + d, CHIPS_Z)],
-            in_z_ref.at[d - 1],
-            z_send,
-            z_recv,
-            d - 1,
-            at.device(z=d),
-        )
-        for d in others_z
-    ]
-    for copy in to_z:
-        copy.wait_recv()
-    total = small_ref[at.z].astype(f32)
-    for d in others_z:
-        total = total + in_z_ref[d - 1].astype(f32)
-    line_ref[at.z] = total.astype(bf16)
-    piece = line_ref.at[at.z]
-    line = [
-        start_remote(piece, piece, line_send, line_recv, d - 1, at.device(z=d)) for d in others_z
-    ]
-    for copy in line:
-        copy.wait_recv()
-    column = plane_ref.at[pl.ds(0, CHIPS_Z), pl.ds(0, CHUNK), lanes(at.x)]
-    plane = [
-        start_remote(line_ref, column, plane_send, plane_recv, e - 1, at.device(x=e))
-        for e in others_x
-    ]
-    own_column = start_local(line_ref, column, local_sem, 0)
-    own_column.wait()
-    for copy in plane:
-        copy.wait_recv()
-    half = out_ref.at[at.core]
-    last = start_remote(plane_ref, half, core_send, core_recv, 0, partner)
-    own_half = start_local(plane_ref, half, local_sem, 1)
-    own_half.wait()
-    last.wait()
-    for copy in paired + b1 + list(a1.values()) + list(b2.values()) + a2 + to_z + line + plane:
-        copy.wait_send()
+        own_half = start_local(plane_ref.at[all_z, rows], half, half_sem, turn)
+        yield
+        own_half.wait()
+        last.wait()
+        for copies in (paired, a1, b1, a2, b2):
+            for copy in copies.values():
+                copy.wait_send()
+        for copy in to_z + line + plane:
+            copy.wait_send()
+
+    running = [stream(turn, *span) for turn, span in enumerate(STREAMS)]
+    for turn in TURNS:
+        next(running[turn])
+    for one in running:
+        for _ in one:
+            pass
 
 
 def reduce_grads(grads, sections):
     rows, channels = grads.shape[2:]
     grads = grads.reshape(sections, CORES, CHIPS_Z, CHUNK, channels)
-    anywhere = pl.BlockSpec(memory_space=pl.ANY)
     dma = pltpu.SemaphoreType.DMA
-    ys, xs, zs = sections - 1, CHIPS_X - 1, CHIPS_Z - 1
+    ys, xs, zs, turns = sections - 1, CHIPS_X - 1, CHIPS_Z - 1, len(STREAMS)
 
     def vmem(*shape):
         return pltpu.VMEM(shape, jnp.bfloat16)
@@ -744,45 +791,30 @@
     out = pl.pallas_call(
         functools.partial(reduce_kernel, sections),
         out_shape=jax.ShapeDtypeStruct((CORES, CHIPS_Z, CHUNK, channels), jnp.bfloat16),
-        in_specs=[anywhere],
-        out_specs=anywhere,
+        in_specs=[pl.BlockSpec(memory_space=pltpu.VMEM)],
+        out_specs=pl.BlockSpec(memory_space=pl.ANY),
         scratch_shapes=[
             vmem(sections, CHIPS_Z, CHUNK, channels),
             vmem(sections, CHIPS_Z, CHUNK, channels),
-            vmem(sections, CHIPS_Z, CHUNK_A, channels),
-            vmem(sections, CHIPS_Z, CHUNK_B, channels),
-            vmem(ys, CHIPS_Z, CHUNK_A, channels),
-            vmem(xs, sections, CHIPS_Z, CHUNK_B, LANES),
-            vmem(CHIPS_Z, CHUNK_A, channels),
-            vmem(sections, CHIPS_Z, CHUNK_B, LANES),
-            vmem(xs, CHIPS_Z, CHUNK_A, LANES),
-            vmem(ys, CHIPS_Z, CHUNK_B, LANES),
+            vmem(ys, FIRST_Z, CHUNK, channels),
+            vmem(xs, sections, LAST_Z, CHUNK, LANES),
+            vmem(FIRST_Z, CHUNK, channels),
+            vmem(sections, LAST_Z, CHUNK, LANES),
+            vmem(xs, FIRST_Z, CHUNK, LANES),
+            vmem(ys, LAST_Z, CHUNK, LANES),
             vmem(CHIPS_Z, CHUNK, LANES),
             vmem(zs, CHUNK, LANES),
             vmem(CHIPS_Z, CHUNK, LANES),
             vmem(CHIPS_Z, CHUNK, channels),
-            dma((sections,)),
-            dma((sections,)),
-            dma((ys,)),
-            dma((ys,)),
-            dma((sections * xs,)),
-            dma((sections * xs,)),
-            dma((xs,)),
-            dma((xs,)),
-            dma((ys,)),
-            dma((ys,)),
-            dma((zs,)),
-            dma((zs,)),
-            dma((zs,)),
-            dma((zs,)),
-            dma((xs,)),
-            dma((xs,)),
-            dma((1,)),
-            dma((1,)),
-            dma((sections,)),
-        ],
+        ]
+        + [
+            dma((turns * count,))
+            for count in (sections, ys, sections * xs, xs, ys, zs, zs, xs, 1)
+            for _ in ("send", "receive")
+        ]
+        + [dma((turns,)), dma((turns,))],
         compiler_params=pltpu.CompilerParams(
-            collective_id=1, has_side_effects=True, vmem_limit_bytes=40 * 1024 * 1024
+            collective_id=1, has_side_effects=True, vmem_limit_bytes=24 * 1024 * 1024
         ),
         name="reduce",
     )(grads)

time: 166 us -> 137 us (0.83)
  Pallas kernels: 153 us -> 125 us
    pallas_call x1, Pallas kernels: 49.4 us -> 31.4 us  [run_cells(): pl.pallas_call(cells_kernel, out_shape=jax.ShapeDtypeStruct((sections, CO...]
    pallas_call x1, Pallas kernels: 71.4 us -> 61.6 us  [reduce_grads(): pl.pallas_call(functools.partial(reduce_kernel, sections), out_shape=jax....]
where the time goes in v4:
time: 137 us
  Pallas kernels  125 us (91%)
  local copies, waits for them, and re-layouts  7.75 us (6%)
  other arithmetic  2.65 us (2%)
  between operations  1.44 us (1%)
    pallas_call x1, Pallas kernels, reduce_grads(): pl.pallas_call(functools.partial(reduce_kernel, sections), out_shape=jax....  61.6 us
    pallas_call x1, Pallas kernels, gather_weights(): pl.pallas_call(functools.partial(gather_kernel, sections), out_shape=(jax...  31.9 us
    pallas_call x1, Pallas kernels, run_cells(): pl.pallas_call(cells_kernel, out_shape=jax.ShapeDtypeStruct((sections, CO...  31.4 us
    unnamed x27, local copies, waits for them, and re-layouts  5.54 us

profile of v4, /device:TPU:1, one launch (start us, length us, event | category | flops | bytes accessed | tf_op | source)
XLA Modules:
  0.0 136.8 jit_solution(12793066357462982955)
XLA Ops:
  0.6 0.0 copy-start.10
  0.6 0.0 copy-start.11
  1.3 0.0 copy-start
  1.3 1.7 %copy-done = bf16[16,12,12,512]{3,0,2,1:T(8,128)(2,1)S(1)} copy-done((bf16[16,12,12,512]{3,0,2,1:T(8,128)(2,1)S(1)}, bf16[16,12,12,512]{3,0,2,1:T(8,128)(2,1)}, u32[]{:S(2)}) %copy-start) | copy-done | bytes 2359320
  3.0 0.0 copy-start.2
  3.0 1.4 %copy-done.2 = bf16[1,3,512,512]{3,2,1,0:T(8,128)(2,1)S(1)} copy-done((bf16[1,3,512,512]{3,2,1,0:T(8,128)(2,1)S(1)}, bf16[1,3,512,512]{3,2,1,0:T(8,128)(2,1)}, u32[]{:S(2)}) %copy-start.2) | copy-done | bytes 1572888
  4.4 0.0 copy-start.7
  4.4 0.8 copy-done.7
  5.2 0.0 copy-start.8
  5.2 0.8 copy-done.8
  6.0 0.0 copy-start.9
  6.0 0.7 copy-done.9
  6.7 0.0 copy-start.1
  6.7 0.0 copy-start.3
  6.7 0.0 copy-start.4
  6.7 0.0 copy-start.5
  6.7 0.0 copy-start.6
  6.7 31.9 %gather.1 = (bf16[4,2,832,512]{3,2,1,0:T(8,128)(2,1)S(1)}, bf16[576,512]{1,0:T(8,128)(2,1)S(1)}) custom-call(bf16[3,2,256,512]{3,2,1,0:T(8,128)(2,1)S(1)} %bitcast.29, bf16[3,3,512]{2,1,0:T(4,128)(2,1)S(1)} %bitcast.32, bf16[5,5,512]{2,1,0:T(8,128)(2,1)S(1)} %bitcast.31, bf16[7,7,512]{2,1,0:T(8,128)(2,1)S(1)} %bitcast.30, bf16[2304,512]{1,0:T(8,128)(2,1)S(1)} %bitcast.27), custom_call_target="tpu_custom_call" | custom-call | tf_op jit(solution)/shard_map/gather/pallas_call | solution.py:511
  38.6 0.0 copy-done.10
  38.7 0.0 copy-done.11
  38.7 0.0 copy-done.1
  38.7 0.0 copy-done.3
  38.7 0.0 copy-done.4
  38.7 0.0 copy-done.5
  38.7 0.0 copy-done.6
  38.7 31.4 %cells.1 = bf16[4,2,896,512]{3,2,1,0:T(8,128)(2,1)S(1)} custom-call(s32[4]{0:T(128)S(1)} %copy-done.10, s32[16]{0:T(128)S(1)} %copy-done.11, s32[1]{0:T(128)S(6)} %copy.26.live_count_ref, bf16[576,512]{1,0:T(8,128)(2,1)S(1)} %get-tuple-element.7.features_ref, bf16[4,2,832,512]{3,2,1,0:T(8,128)(2,1)S(1)} %get-tuple-element.8.weight_ref, ...), custom_call_target="tpu_custom_call" | custom-call | tf_op jit(solution)/shard_map/cells/pallas_call | solution.py:322
  70.2 61.6 %reduce.2 = bf16[2,8,112,512]{3,2,1,0:T(8,128)(2,1)S(1)} custom-call(bf16[4,2,8,112,512]{4,3,2,1,0:T(8,128)(2,1)S(1)} %bitcast.21), custom_call_target="tpu_custom_call" | custom-call | tf_op jit(solution)/shard_map/reduce/pallas_call | solution.py:791
  131.8 0.6 convert_reduce_fusion
  132.4 0.6 convert.7
  133.1 0.7 convert.8
  133.8 0.1 slice.21
  133.9 0.1 copy.25
  134.0 0.7 convert.9
  134.7 2.1 %copy.19 = f32[2,3,256,512]{3,2,0,1:T(8,128)} copy(bf16[2,3,256,512]{3,2,1,0:T(8,128)(2,1)S(1)} %bitcast.33) | data formatting | bytes 4718592 | tf_op jit(solution)/shard_map/reshape | solution.py:858
  (5 shorter events, 0.1 us)
Async XLA Ops:
  0.6 38.0 %copy-start.10 = (s32[4]{0:T(128)S(1)}, s32[4]{0:T(128)}, u32[]{:S(2)}) copy-start(s32[4]{0:T(128)} %cells_ref.1) | copy-start | bytes 52
  0.6 38.0 %copy-start.11 = (s32[16]{0:T(128)S(1)}, s32[16]{0:T(128)}, u32[]{:S(2)}) copy-start(s32[16]{0:T(128)} %labels_ref.1) | copy-start | bytes 196
  1.3 1.7 %copy-start = (bf16[16,12,12,512]{3,0,2,1:T(8,128)(2,1)S(1)}, bf16[16,12,12,512]{3,0,2,1:T(8,128)(2,1)}, u32[]{:S(2)}) copy-start(bf16[16,12,12,512]{3,0,2,1:T(8,128)(2,1)} %param.13) | copy-start | bytes 7077892
  3.0 1.4 %copy-start.2 = (bf16[1,3,512,512]{3,2,1,0:T(8,128)(2,1)S(1)}, bf16[1,3,512,512]{3,2,1,0:T(8,128)(2,1)}, u32[]{:S(2)}) copy-start(bf16[1,3,512,512]{3,2,1,0:T(8,128)(2,1)} %param.17) | copy-start | bytes 4718596
  4.4 0.8 copy-start.7
  5.2 0.8 copy-start.8
  6.0 0.7 copy-start.9
  6.7 32.0 %copy-start.1 = (f32[512,1000]{0,1:T(8,128)S(1)}, f32[512,1000]{0,1:T(8,128)}, u32[]{:S(2)}) copy-start(f32[512,1000]{0,1:T(8,128)} %param.21) | copy-start | bytes 6144004
  6.7 32.0 %copy-start.3 = (bf16[2,3,240,64]{3,2,1,0:T(8,128)(2,1)S(1)}, bf16[2,3,240,64]{3,2,1,0:T(8,128)(2,1)}, u32[]{:S(2)}) copy-start(bf16[2,3,240,64]{3,2,1,0:T(8,128)(2,1)} %constant.12.clone.tap_into_ref) | copy-start | bytes 552964
  6.7 32.0 %copy-start.4 = (bf16[2,3,64,240]{3,2,1,0:T(8,128)(2,1)S(1)}, bf16[2,3,64,240]{3,2,1,0:T(8,128)(2,1)}, u32[]{:S(2)}) copy-start(bf16[2,3,64,240]{3,2,1,0:T(8,128)(2,1)} %constant.13.clone.tap_back_ref) | copy-start | bytes 552964
  6.7 32.0 %copy-start.5 = (bf16[240,144]{1,0:T(8,128)(2,1)S(1)}, bf16[240,144]{1,0:T(8,128)(2,1)}, u32[]{:S(2)}) copy-start(bf16[240,144]{1,0:T(8,128)(2,1)} %constant.10.clone.into_ref) | copy-start | bytes 207364
  6.7 32.0 %copy-start.6 = (bf16[144,240]{1,0:T(8,128)(2,1)S(1)}, bf16[144,240]{1,0:T(8,128)(2,1)}, u32[]{:S(2)}) copy-start(bf16[144,240]{1,0:T(8,128)(2,1)} %constant.11.clone.back_ref) | copy-start | bytes 207364

commit v5 on v4

--- a/solution.py
+++ b/solution.py
@@ -30,9 +30,10 @@
 TAP_SPANS = (16, 32, 64)
 CHUNK = 112
 STREAMS = ((0, 32), (32, 32), (64, 32), (96, 16))
-TURNS = (0, 1, 2, 3, 0, 1, 0, 2, 1, 0, 0, 3, 2, 1, 0, 1, 3, 2, 1, 2, 0, 3, 2, 3, 1, 3, 2, 3)
+X_FIRST = (2,)
 FIRST_Z = 4
 LAST_Z = CHIPS_Z - FIRST_Z
+VIA_Z = 2
 HALF_ROWS = CHIPS_Z * CHUNK
 LOSS_ROWS = 16
 WEIGHT_A = 320
@@ -93,6 +94,17 @@
     return high, low
 
 
+def three_part(left, right_high, right_low, dim):
+    rows = left.shape[0]
+    dims = (((1,), (dim,)), ((), ()))
+    high, low = halves(left)
+    both = lax.dot_general(
+        jnp.concatenate([high, low], axis=0), right_high, dims, preferred_element_type=jnp.float32
+    )
+    rest = lax.dot_general(high, right_low, dims, preferred_element_type=jnp.float32)
+    return both[:rows] + (both[rows:] + rest)
+
+
 def cells_kernel(
     cells_ref,
     labels_ref,
@@ -190,13 +202,8 @@
     spare = jnp.zeros((8 - IMAGES, channels), jnp.float32)
     pooled = jnp.concatenate(means + [spare], axis=0) / AREA
     head = head_ref[...]
-    scores = lax.dot_general(
-        pooled,
-        head,
-        (((1,), (1,)), ((), ())),
-        precision=lax.Precision.HIGHEST,
-        preferred_element_type=jnp.float32,
-    )
+    head_high, head_low = halves(head)
+    scores = three_part(pooled, head_high, head_low, 1)
     capped = jnp.tanh(scores / LOGIT_CAP)
     logits = LOGIT_CAP * capped
     exponent = jnp.exp(logits)
@@ -213,9 +220,7 @@
     onehot = (classes == targets).astype(jnp.float32)
     row_loss = (jnp.log(total) - jnp.sum(logits * onehot, axis=1, keepdims=True)) * live
     score_cot = (exponent / total - onehot) * live * (1.0 - capped * capped)
-    pooled_cot = jnp.dot(
-        score_cot, head, precision=lax.Precision.HIGHEST, preferred_element_type=jnp.float32
-    )
+    pooled_cot = three_part(score_cot, head_high, head_low, 0)
     spread = pooled_cot / AREA
     for image in range(IMAGES):
         cot_ref[rows_of(image)] = jnp.broadcast_to(
@@ -541,6 +546,8 @@
     out_ref,
     pair_ref,
     part_ref,
+    via_a_ref,
+    via_b_ref,
     in_a1_ref,
     in_b1_ref,
     mid_a_ref,
@@ -553,6 +560,10 @@
     plane_ref,
     pair_send,
     pair_recv,
+    via_a_send,
+    via_a_recv,
+    via_b_send,
+    via_b_recv,
     a1_send,
     a1_recv,
     b1_send,
@@ -592,6 +603,8 @@
     first_z = pl.ds(0, FIRST_Z)
     last_z = pl.ds(FIRST_Z, LAST_Z)
     last_all = pl.ds(0, LAST_Z)
+    via_all = pl.ds(0, VIA_Z)
+    sides = (1, 3)
 
     def lanes(x):
         return pl.ds(pl.multiple_of(x * LANES, LANES), LANES)
@@ -601,7 +614,7 @@
 
     def stream(turn, start, size):
         rows = pl.ds(start, size)
-        paired, a1, b1, a2, b2 = {}, {}, {}, {}, {}
+        paired, via_a, via_b, a1, b1, a2, b2 = {}, {}, {}, {}, {}, {}, {}
         for k, d in enumerate(order):
             section = section_at(d)
             paired[d] = start_remote(
@@ -624,34 +637,81 @@
                 return 0
 
             lax.fori_loop(0, CHIPS_Z, add_pair, 0)
-            if d:
-                a1[d] = start_remote(
-                    part_ref.at[section, first_z, rows],
-                    in_a1_ref.at[d - 1, first_z, rows],
-                    a1_send,
-                    a1_recv,
-                    turn * len(others_y) + d - 1,
-                    at.device(pipe=d),
+            for n, side in enumerate(sides):
+                if d == 2:
+                    via_a[side] = start_remote(
+                        part_ref.at[section, pl.ds(n * VIA_Z, VIA_Z), rows],
+                        via_a_ref.at[n, via_all, rows],
+                        via_a_send,
+                        via_a_recv,
+                        turn * len(sides) + n,
+                        at.device(pipe=side),
+                    )
+                via_b[d, side] = start_remote(
+                    part_ref.at[
+                        section,
+                        pl.ds(FIRST_Z + n * VIA_Z, VIA_Z),
+                        rows,
+                        lanes(lax.rem(at.x + 2, CHIPS_X)),
+                    ],
+                    via_b_ref.at[n, section, via_all, rows],
+                    via_b_send,
+                    via_b_recv,
+                    (turn * sections + d) * len(sides) + n,
+                    at.device(x=side),
                 )
-            for e in others_x:
-                b1[d, e] = start_remote(
-                    part_ref.at[section, last_z, rows, lanes(lax.rem(at.x + e, CHIPS_X))],
-                    in_b1_ref.at[e - 1, section, last_all, rows],
+        yield
+        for n, side in enumerate(sides):
+            section = section_at(side)
+            via_a[side].wait_recv()
+
+            def add_via_a(z, _, section=section, n=n):
+                total = part_ref[section, n * VIA_Z + z, rows].astype(f32)
+                total = total + via_a_ref[n, z, rows].astype(f32)
+                part_ref[section, n * VIA_Z + z, rows] = total.astype(bf16)
+                return 0
+
+            lax.fori_loop(0, VIA_Z, add_via_a, 0)
+            a1[side] = start_remote(
+                part_ref.at[section, first_z, rows],
+                in_a1_ref.at[n, first_z, rows],
+                a1_send,
+                a1_recv,
+                turn * len(sides) + n,
+                at.device(pipe=side),
+            )
+        for d in order:
+            section = section_at(d)
+            for n, side in enumerate(sides):
+                via_b[d, side].wait_recv()
+                place = lanes(lax.rem(at.x + side, CHIPS_X))
+
+                def add_via_b(z, _, section=section, n=n, place=place):
+                    row = FIRST_Z + n * VIA_Z + z
+                    total = part_ref[section, row, rows, place].astype(f32)
+                    total = total + via_b_ref[n, section, z, rows].astype(f32)
+                    part_ref[section, row, rows, place] = total.astype(bf16)
+                    return 0
+
+                lax.fori_loop(0, VIA_Z, add_via_b, 0)
+                b1[d, side] = start_remote(
+                    part_ref.at[section, last_z, rows, place],
+                    in_b1_ref.at[n, section, last_all, rows],
                     b1_send,
                     b1_recv,
-                    (turn * sections + d) * len(others_x) + e - 1,
-                    at.device(x=e),
+                    (turn * sections + d) * len(sides) + n,
+                    at.device(x=side),
                 )
         yield
         for d in order:
             section = section_at(d)
-            for e in others_x:
-                b1[d, e].wait_recv()
+            for side in sides:
+                b1[d, side].wait_recv()
 
             def add_b1(z, _, section=section):
                 total = part_ref[section, FIRST_Z + z, rows, lanes(at.x)].astype(f32)
-                for e in others_x:
-                    total = total + in_b1_ref[e - 1, section, z, rows].astype(f32)
+                for n in range(len(sides)):
+                    total = total + in_b1_ref[n, section, z, rows].astype(f32)
                 mid_b_ref[section, z, rows] = total.astype(bf16)
                 return 0
 
@@ -665,13 +725,13 @@
                     turn * len(others_y) + d - 1,
                     at.device(pipe=d),
                 )
-        for d in others_y:
-            a1[d].wait_recv()
+        for side in sides:
+            a1[side].wait_recv()
 
         def add_a1(z, _):
             total = part_ref[at.pipe, z, rows].astype(f32)
-            for d in others_y:
-                total = total + in_a1_ref[d - 1, z, rows].astype(f32)
+            for n in range(len(sides)):
+                total = total + in_a1_ref[n, z, rows].astype(f32)
             mid_a_ref[z, rows] = total.astype(bf16)
             return 0
 
@@ -724,8 +784,27 @@
         total = small_ref[at.z, rows].astype(f32)
         for d in others_z:
             total = total + in_z_ref[d - 1, rows].astype(f32)
-        line_ref[at.z, rows] = total.astype(bf16)
-        piece = line_ref.at[at.z, rows]
+        if turn in X_FIRST:
+            plane_ref[at.z, rows, lanes(at.x)] = total.astype(bf16)
+            piece = plane_ref.at[at.z, rows, lanes(at.x)]
+            plane = [
+                start_remote(
+                    piece,
+                    piece,
+                    plane_send,
+                    plane_recv,
+                    turn * len(others_x) + e - 1,
+                    at.device(x=e),
+                )
+                for e in others_x
+            ]
+            yield
+            for copy in plane:
+                copy.wait_recv()
+            piece = plane_ref.at[at.z, rows]
+        else:
+            line_ref[at.z, rows] = total.astype(bf16)
+            piece = line_ref.at[at.z, rows]
         line = [
             start_remote(
                 piece,
@@ -740,23 +819,24 @@
         yield
         for copy in line:
             copy.wait_recv()
-        column = plane_ref.at[all_z, rows, lanes(at.x)]
-        plane = [
-            start_remote(
-                line_ref.at[all_z, rows],
-                column,
-                plane_send,
-                plane_recv,
-                turn * len(others_x) + e - 1,
-                at.device(x=e),
-            )
-            for e in others_x
-        ]
-        own_column = start_local(line_ref.at[all_z, rows], column, column_sem, turn)
-        yield
-        own_column.wait()
-        for copy in plane:
-            copy.wait_recv()
+        if turn not in X_FIRST:
+            column = plane_ref.at[all_z, rows, lanes(at.x)]
+            plane = [
+                start_remote(
+                    line_ref.at[all_z, rows],
+                    column,
+                    plane_send,
+                    plane_recv,
+                    turn * len(others_x) + e - 1,
+                    at.device(x=e),
+                )
+                for e in others_x
+            ]
+            own_column = start_local(line_ref.at[all_z, rows], column, column_sem, turn)
+            yield
+            own_column.wait()
+            for copy in plane:
+                copy.wait_recv()
         half = out_ref.at[at.core, all_z, rows]
         last = start_remote(
             plane_ref.at[all_z, rows], half, core_send, core_recv, turn, partner
@@ -765,18 +845,15 @@
         yield
         own_half.wait()
         last.wait()
-        for copies in (paired, a1, b1, a2, b2):
+        for copies in (paired, via_a, via_b, a1, b1, a2, b2):
             for copy in copies.values():
                 copy.wait_send()
         for copy in to_z + line + plane:
             copy.wait_send()
 
     running = [stream(turn, *span) for turn, span in enumerate(STREAMS)]
-    for turn in TURNS:
-        next(running[turn])
-    for one in running:
-        for _ in one:
-            pass
+    while running:
+        running = [one for one in running if next(one, running) is None]
 
 
 def reduce_grads(grads, sections):
@@ -796,8 +873,10 @@
         scratch_shapes=[
             vmem(sections, CHIPS_Z, CHUNK, channels),
             vmem(sections, CHIPS_Z, CHUNK, channels),
-            vmem(ys, FIRST_Z, CHUNK, channels),
-            vmem(xs, sections, LAST_Z, CHUNK, LANES),
+            vmem(2, VIA_Z, CHUNK, channels),
+            vmem(2, sections, VIA_Z, CHUNK, LANES),
+            vmem(2, FIRST_Z, CHUNK, channels),
+            vmem(2, sections, LAST_Z, CHUNK, LANES),
             vmem(FIRST_Z, CHUNK, channels),
             vmem(sections, LAST_Z, CHUNK, LANES),
             vmem(xs, FIRST_Z, CHUNK, LANES),
@@ -809,7 +888,7 @@
         ]
         + [
             dma((turns * count,))
-            for count in (sections, ys, sections * xs, xs, ys, zs, zs, xs, 1)
+            for count in (sections, 2, 2 * sections, 2, 2 * sections, xs, ys, zs, zs, xs, 1)
             for _ in ("send", "receive")
         ]
         + [dma((turns,)), dma((turns,))],

time: 137 us -> 133 us (0.971)
  Pallas kernels: 125 us -> 121 us
    pallas_call x1, Pallas kernels: 61.6 us -> 52.5 us  [reduce_grads(): pl.pallas_call(functools.partial(reduce_kernel, sections), out_shape=jax....]
    pallas_call x1, Pallas kernels: 31.4 us -> 36.6 us  [run_cells(): pl.pallas_call(cells_kernel, out_shape=jax.ShapeDtypeStruct((sections, CO...]
where the time goes in v5:
time: 133 us
  Pallas kernels  121 us (91%)
  local copies, waits for them, and re-layouts  7.75 us (6%)
  other arithmetic  2.65 us (2%)
  between operations  1.44 us (1%)
    pallas_call x1, Pallas kernels, reduce_grads(): pl.pallas_call(functools.partial(reduce_kernel, sections), out_shape=jax....  52.5 us
    pallas_call x1, Pallas kernels, run_cells(): pl.pallas_call(cells_kernel, out_shape=jax.ShapeDtypeStruct((sections, CO...  36.6 us
    pallas_call x1, Pallas kernels, gather_weights(): pl.pallas_call(functools.partial(gather_kernel, sections), out_shape=(jax...  31.9 us
    unnamed x27, local copies, waits for them, and re-layouts  5.54 us

profile of v5, /device:TPU:1, one launch (start us, length us, event | category | flops | bytes accessed | tf_op | source)
XLA Modules:
  0.0 132.9 jit_solution(5478925383158819805)
XLA Ops:
  0.6 0.0 copy-start.10
  0.6 0.0 copy-start.11
  1.3 0.0 copy-start
  1.3 1.7 %copy-done = bf16[16,12,12,512]{3,0,2,1:T(8,128)(2,1)S(1)} copy-done((bf16[16,12,12,512]{3,0,2,1:T(8,128)(2,1)S(1)}, bf16[16,12,12,512]{3,0,2,1:T(8,128)(2,1)}, u32[]{:S(2)}) %copy-start) | copy-done | bytes 2359320
  3.0 0.0 copy-start.2
  3.0 1.4 %copy-done.2 = bf16[1,3,512,512]{3,2,1,0:T(8,128)(2,1)S(1)} copy-done((bf16[1,3,512,512]{3,2,1,0:T(8,128)(2,1)S(1)}, bf16[1,3,512,512]{3,2,1,0:T(8,128)(2,1)}, u32[]{:S(2)}) %copy-start.2) | copy-done | bytes 1572888
  4.4 0.0 copy-start.7
  4.4 0.8 copy-done.7
  5.2 0.0 copy-start.8
  5.2 0.8 copy-done.8
  6.0 0.0 copy-start.9
  6.0 0.7 copy-done.9
  6.7 0.0 copy-start.1
  6.7 0.0 copy-start.3
  6.7 0.0 copy-start.4
  6.7 0.0 copy-start.5
  6.7 0.0 copy-start.6
  6.7 31.9 %gather.1 = (bf16[4,2,832,512]{3,2,1,0:T(8,128)(2,1)S(1)}, bf16[576,512]{1,0:T(8,128)(2,1)S(1)}) custom-call(bf16[3,2,256,512]{3,2,1,0:T(8,128)(2,1)S(1)} %bitcast.29, bf16[3,3,512]{2,1,0:T(4,128)(2,1)S(1)} %bitcast.32, bf16[5,5,512]{2,1,0:T(8,128)(2,1)S(1)} %bitcast.31, bf16[7,7,512]{2,1,0:T(8,128)(2,1)S(1)} %bitcast.30, bf16[2304,512]{1,0:T(8,128)(2,1)S(1)} %bitcast.27), custom_call_target="tpu_custom_call" | custom-call | tf_op jit(solution)/shard_map/gather/pallas_call | solution.py:516
  38.6 0.0 copy-done.10
  38.7 0.0 copy-done.11
  38.7 0.0 copy-done.1
  38.7 0.0 copy-done.3
  38.7 0.0 copy-done.4
  38.7 0.0 copy-done.5
  38.7 0.0 copy-done.6
  38.7 36.6 %cells.1 = bf16[4,2,896,512]{3,2,1,0:T(8,128)(2,1)S(1)} custom-call(s32[4]{0:T(128)S(1)} %copy-done.10, s32[16]{0:T(128)S(1)} %copy-done.11, s32[1]{0:T(128)S(6)} %copy.26.live_count_ref, bf16[576,512]{1,0:T(8,128)(2,1)S(1)} %get-tuple-element.7.features_ref, bf16[4,2,832,512]{3,2,1,0:T(8,128)(2,1)S(1)} %get-tuple-element.8.weight_ref, ...), custom_call_target="tpu_custom_call" | custom-call | tf_op jit(solution)/shard_map/cells/pallas_call | solution.py:327
  75.3 52.5 %reduce.2 = bf16[2,8,112,512]{3,2,1,0:T(8,128)(2,1)S(1)} custom-call(bf16[4,2,8,112,512]{4,3,2,1,0:T(8,128)(2,1)S(1)} %bitcast.21), custom_call_target="tpu_custom_call" | custom-call | tf_op jit(solution)/shard_map/reduce/pallas_call | solution.py:868
  127.9 0.6 convert_reduce_fusion
  128.5 0.6 convert.7
  129.2 0.7 convert.8
  129.9 0.1 slice.21
  130.0 0.1 copy.25
  130.1 0.7 convert.9
  130.8 2.1 %copy.19 = f32[2,3,256,512]{3,2,0,1:T(8,128)} copy(bf16[2,3,256,512]{3,2,1,0:T(8,128)(2,1)S(1)} %bitcast.33) | data formatting | bytes 4718592 | tf_op jit(solution)/shard_map/reshape | solution.py:937
  (5 shorter events, 0.1 us)
Async XLA Ops:
  0.6 38.0 %copy-start.10 = (s32[4]{0:T(128)S(1)}, s32[4]{0:T(128)}, u32[]{:S(2)}) copy-start(s32[4]{0:T(128)} %cells_ref.1) | copy-start | bytes 52
  0.6 38.0 %copy-start.11 = (s32[16]{0:T(128)S(1)}, s32[16]{0:T(128)}, u32[]{:S(2)}) copy-start(s32[16]{0:T(128)} %labels_ref.1) | copy-start | bytes 196
  1.3 1.7 %copy-start = (bf16[16,12,12,512]{3,0,2,1:T(8,128)(2,1)S(1)}, bf16[16,12,12,512]{3,0,2,1:T(8,128)(2,1)}, u32[]{:S(2)}) copy-start(bf16[16,12,12,512]{3,0,2,1:T(8,128)(2,1)} %param.13) | copy-start | bytes 7077892
  3.0 1.4 %copy-start.2 = (bf16[1,3,512,512]{3,2,1,0:T(8,128)(2,1)S(1)}, bf16[1,3,512,512]{3,2,1,0:T(8,128)(2,1)}, u32[]{:S(2)}) copy-start(bf16[1,3,512,512]{3,2,1,0:T(8,128)(2,1)} %param.17) | copy-start | bytes 4718596
  4.4 0.8 copy-start.7
  5.2 0.8 copy-start.8
  6.0 0.7 copy-start.9
  6.7 32.0 %copy-start.1 = (f32[512,1000]{0,1:T(8,128)S(1)}, f32[512,1000]{0,1:T(8,128)}, u32[]{:S(2)}) copy-start(f32[512,1000]{0,1:T(8,128)} %param.21) | copy-start | bytes 6144004
  6.7 32.0 %copy-start.3 = (bf16[2,3,240,64]{3,2,1,0:T(8,128)(2,1)S(1)}, bf16[2,3,240,64]{3,2,1,0:T(8,128)(2,1)}, u32[]{:S(2)}) copy-start(bf16[2,3,240,64]{3,2,1,0:T(8,128)(2,1)} %constant.12.clone.tap_into_ref) | copy-start | bytes 552964
  6.7 32.0 %copy-start.4 = (bf16[2,3,64,240]{3,2,1,0:T(8,128)(2,1)S(1)}, bf16[2,3,64,240]{3,2,1,0:T(8,128)(2,1)}, u32[]{:S(2)}) copy-start(bf16[2,3,64,240]{3,2,1,0:T(8,128)(2,1)} %constant.13.clone.tap_back_ref) | copy-start | bytes 552964
  6.7 32.0 %copy-start.5 = (bf16[240,144]{1,0:T(8,128)(2,1)S(1)}, bf16[240,144]{1,0:T(8,128)(2,1)}, u32[]{:S(2)}) copy-start(bf16[240,144]{1,0:T(8,128)(2,1)} %constant.10.clone.into_ref) | copy-start | bytes 207364
  6.7 32.0 %copy-start.6 = (bf16[144,240]{1,0:T(8,128)(2,1)S(1)}, bf16[144,240]{1,0:T(8,128)(2,1)}, u32[]{:S(2)}) copy-start(bf16[144,240]{1,0:T(8,128)(2,1)} %constant.11.clone.back_ref) | copy-start | bytes 207364

commit v6 on v5

--- a/solution.py
+++ b/solution.py
@@ -454,10 +454,14 @@
         split.append(
             start_remote(piece, piece, split_send, split_recv, d - 1, at.device(pipe=d))
         )
-    for d in others_y:
+    sides = (1, 3)
+    near_halves = [pl.ds(n * WEIGHT_A // 2, WEIGHT_A // 2) for n in range(2)]
+    far_rows = point_rows + TAP_ROWS - WEIGHT_A
+    far_halves = [pl.ds(WEIGHT_A + n * far_rows // 2, far_rows // 2) for n in range(2)]
+    for n, side in enumerate(sides):
         piece = weights_ref.at[at.pipe, core, near]
         direct.append(
-            start_remote(piece, piece, direct_send, direct_recv, d - 1, at.device(pipe=d))
+            start_remote(piece, piece, direct_send, direct_recv, n, at.device(pipe=side))
         )
     per_replica = features_ref.shape[0] // AREA
     group = (GROUP * IMAGES, GROUP * per_replica)
@@ -483,25 +487,43 @@
     for d in others_y:
         split[d - 1].wait_recv()
         piece = weights_ref.at[source(d), core, far, lanes(at.x)]
-        for e in others_x:
-            k = (d - 1) * (CHIPS_X - 1) + e - 1
+        for n, side in enumerate(sides):
+            k = (d - 1) * len(sides) + n
             spread.append(
-                start_remote(piece, piece, spread_send, spread_recv, k, at.device(x=e))
+                start_remote(piece, piece, spread_send, spread_recv, k, at.device(x=side))
             )
         share(piece)
+    near_relays, far_relays = [], []
+    for n, side in enumerate(sides):
+        direct[n].wait_recv()
+        piece = weights_ref.at[source(side), core, near_halves[n]]
+        near_relays.append(
+            start_remote(piece, piece, direct_send, direct_recv, 2 + n, at.device(pipe=side))
+        )
+        share(weights_ref.at[source(side), core, near])
     for d in others_y:
-        direct[d - 1].wait_recv()
-        share(weights_ref.at[source(d), core, near])
+        for n, side in enumerate(sides):
+            spread[(d - 1) * len(sides) + n].wait_recv()
+            x = lanes(lax.rem(at.x + CHIPS_X - side, CHIPS_X))
+            piece = weights_ref.at[source(d), core, far_halves[n], x]
+            k = (len(others_y) + d - 1) * len(sides) + n
+            far_relays.append(
+                start_remote(piece, piece, spread_send, spread_recv, k, at.device(x=side))
+            )
+            share(weights_ref.at[source(d), core, far, x])
+    for copy in near_relays:
+        copy.wait_recv()
+    share(weights_ref.at[source(2), core, near])
+    opposite = lanes(lax.rem(at.x + 2, CHIPS_X))
     for d in others_y:
-        for e in others_x:
-            spread[(d - 1) * (CHIPS_X - 1) + e - 1].wait_recv()
-            x = lax.rem(at.x + CHIPS_X - e, CHIPS_X)
-            share(weights_ref.at[source(d), core, far, lanes(x)])
+        for n in range(len(sides)):
+            far_relays[(d - 1) * len(sides) + n].wait_recv()
+        share(weights_ref.at[source(d), core, far, opposite])
     for copy in loads[CELLS_MAX:]:
         copy.wait()
     for copy in shared:
         copy.wait_recv()
-    for copy in shared + split + direct + spread:
+    for copy in shared + split + direct + near_relays + spread + far_relays:
         copy.wait_send()
 
 
@@ -523,12 +545,12 @@
         out_specs=(vmem, vmem),
         scratch_shapes=[
             pltpu.VMEM((CORES, TAP_ROWS, channels), jnp.float32),
+            dma((4,)),
+            dma((4,)),
             dma((ys,)),
             dma((ys,)),
-            dma((ys,)),
-            dma((ys,)),
-            dma((ys * xs,)),
-            dma((ys * xs,)),
+            dma((ys * 4,)),
+            dma((ys * 4,)),
             dma((2 * ys + ys * xs,)),
             dma((2 * ys + ys * xs,)),
             dma((CORES * cells,)),

time: 133 us -> 124 us (0.932)
  Pallas kernels: 121 us -> 112 us
    pallas_call x1, Pallas kernels: 36.6 us -> 29.7 us  [run_cells(): pl.pallas_call(cells_kernel, out_shape=jax.ShapeDtypeStruct((sections, CO...]
    pallas_call x1, Pallas kernels: 31.9 us -> 27.7 us  [gather_weights(): pl.pallas_call(functools.partial(gather_kernel, sections), out_shape=(jax...]
    pallas_call x1, Pallas kernels: 52.5 us -> 54.6 us  [reduce_grads(): pl.pallas_call(functools.partial(reduce_kernel, sections), out_shape=jax....]
where the time goes in v6:
time: 124 us
  Pallas kernels  112 us (90%)
  local copies, waits for them, and re-layouts  7.75 us (6%)
  other arithmetic  2.65 us (2%)
  between operations  1.44 us (1%)
    pallas_call x1, Pallas kernels, reduce_grads(): pl.pallas_call(functools.partial(reduce_kernel, sections), out_shape=jax....  54.6 us
    pallas_call x1, Pallas kernels, run_cells(): pl.pallas_call(cells_kernel, out_shape=jax.ShapeDtypeStruct((sections, CO...  29.7 us
    pallas_call x1, Pallas kernels, gather_weights(): pl.pallas_call(functools.partial(gather_kernel, sections), out_shape=(jax...  27.7 us
    unnamed x27, local copies, waits for them, and re-layouts  5.54 us

profile of v6, /device:TPU:1, one launch (start us, length us, event | category | flops | bytes accessed | tf_op | source)
XLA Modules:
  0.0 123.9 jit_solution(5678768070076548783)
XLA Ops:
  0.6 0.0 copy-start.10
  0.6 0.0 copy-start.11
  1.3 0.0 copy-start
  1.3 1.7 %copy-done = bf16[16,12,12,512]{3,0,2,1:T(8,128)(2,1)S(1)} copy-done((bf16[16,12,12,512]{3,0,2,1:T(8,128)(2,1)S(1)}, bf16[16,12,12,512]{3,0,2,1:T(8,128)(2,1)}, u32[]{:S(2)}) %copy-start) | copy-done | bytes 2359320
  3.0 0.0 copy-start.2
  3.0 1.4 %copy-done.2 = bf16[1,3,512,512]{3,2,1,0:T(8,128)(2,1)S(1)} copy-done((bf16[1,3,512,512]{3,2,1,0:T(8,128)(2,1)S(1)}, bf16[1,3,512,512]{3,2,1,0:T(8,128)(2,1)}, u32[]{:S(2)}) %copy-start.2) | copy-done | bytes 1572888
  4.4 0.0 copy-start.7
  4.4 0.8 copy-done.7
  5.2 0.0 copy-start.8
  5.2 0.8 copy-done.8
  6.0 0.0 copy-start.9
  6.0 0.7 copy-done.9
  6.7 0.0 copy-start.1
  6.7 0.0 copy-start.3
  6.7 0.0 copy-start.4
  6.7 0.0 copy-start.5
  6.7 0.0 copy-start.6
  6.7 27.7 %gather.1 = (bf16[4,2,832,512]{3,2,1,0:T(8,128)(2,1)S(1)}, bf16[576,512]{1,0:T(8,128)(2,1)S(1)}) custom-call(bf16[3,2,256,512]{3,2,1,0:T(8,128)(2,1)S(1)} %bitcast.29, bf16[3,3,512]{2,1,0:T(4,128)(2,1)S(1)} %bitcast.32, bf16[5,5,512]{2,1,0:T(8,128)(2,1)S(1)} %bitcast.31, bf16[7,7,512]{2,1,0:T(8,128)(2,1)S(1)} %bitcast.30, bf16[2304,512]{1,0:T(8,128)(2,1)S(1)} %bitcast.27), custom_call_target="tpu_custom_call" | custom-call | tf_op jit(solution)/shard_map/gather/pallas_call | solution.py:538
  34.4 0.0 copy-done.10
  34.4 0.0 copy-done.11
  34.5 0.0 copy-done.1
  34.5 0.0 copy-done.3
  34.5 0.0 copy-done.4
  34.5 0.0 copy-done.5
  34.5 0.0 copy-done.6
  34.5 29.7 %cells.1 = bf16[4,2,896,512]{3,2,1,0:T(8,128)(2,1)S(1)} custom-call(s32[4]{0:T(128)S(1)} %copy-done.10, s32[16]{0:T(128)S(1)} %copy-done.11, s32[1]{0:T(128)S(6)} %copy.26.live_count_ref, bf16[576,512]{1,0:T(8,128)(2,1)S(1)} %get-tuple-element.7.features_ref, bf16[4,2,832,512]{3,2,1,0:T(8,128)(2,1)S(1)} %get-tuple-element.8.weight_ref, ...), custom_call_target="tpu_custom_call" | custom-call | tf_op jit(solution)/shard_map/cells/pallas_call | solution.py:327
  64.3 54.6 %reduce.2 = bf16[2,8,112,512]{3,2,1,0:T(8,128)(2,1)S(1)} custom-call(bf16[4,2,8,112,512]{4,3,2,1,0:T(8,128)(2,1)S(1)} %bitcast.21), custom_call_target="tpu_custom_call" | custom-call | tf_op jit(solution)/shard_map/reduce/pallas_call | solution.py:890
  118.9 0.6 convert_reduce_fusion
  119.5 0.6 convert.7
  120.2 0.7 convert.8
  120.9 0.1 slice.21
  121.0 0.1 copy.25
  121.1 0.7 convert.9
  121.8 2.1 %copy.19 = f32[2,3,256,512]{3,2,0,1:T(8,128)} copy(bf16[2,3,256,512]{3,2,1,0:T(8,128)(2,1)S(1)} %bitcast.33) | data formatting | bytes 4718592 | tf_op jit(solution)/shard_map/reshape | solution.py:959
  (5 shorter events, 0.1 us)
Async XLA Ops:
  0.6 33.8 %copy-start.10 = (s32[4]{0:T(128)S(1)}, s32[4]{0:T(128)}, u32[]{:S(2)}) copy-start(s32[4]{0:T(128)} %cells_ref.1) | copy-start | bytes 52
  0.6 33.8 %copy-start.11 = (s32[16]{0:T(128)S(1)}, s32[16]{0:T(128)}, u32[]{:S(2)}) copy-start(s32[16]{0:T(128)} %labels_ref.1) | copy-start | bytes 196
  1.3 1.7 %copy-start = (bf16[16,12,12,512]{3,0,2,1:T(8,128)(2,1)S(1)}, bf16[16,12,12,512]{3,0,2,1:T(8,128)(2,1)}, u32[]{:S(2)}) copy-start(bf16[16,12,12,512]{3,0,2,1:T(8,128)(2,1)} %param.13) | copy-start | bytes 7077892
  3.0 1.4 %copy-start.2 = (bf16[1,3,512,512]{3,2,1,0:T(8,128)(2,1)S(1)}, bf16[1,3,512,512]{3,2,1,0:T(8,128)(2,1)}, u32[]{:S(2)}) copy-start(bf16[1,3,512,512]{3,2,1,0:T(8,128)(2,1)} %param.17) | copy-start | bytes 4718596
  4.4 0.8 copy-start.7
  5.2 0.8 copy-start.8
  6.0 0.7 copy-start.9
  6.7 27.8 %copy-start.1 = (f32[512,1000]{0,1:T(8,128)S(1)}, f32[512,1000]{0,1:T(8,128)}, u32[]{:S(2)}) copy-start(f32[512,1000]{0,1:T(8,128)} %param.21) | copy-start | bytes 6144004
  6.7 27.8 %copy-start.3 = (bf16[2,3,240,64]{3,2,1,0:T(8,128)(2,1)S(1)}, bf16[2,3,240,64]{3,2,1,0:T(8,128)(2,1)}, u32[]{:S(2)}) copy-start(bf16[2,3,240,64]{3,2,1,0:T(8,128)(2,1)} %constant.12.clone.tap_into_ref) | copy-start | bytes 552964
  6.7 27.8 %copy-start.4 = (bf16[2,3,64,240]{3,2,1,0:T(8,128)(2,1)S(1)}, bf16[2,3,64,240]{3,2,1,0:T(8,128)(2,1)}, u32[]{:S(2)}) copy-start(bf16[2,3,64,240]{3,2,1,0:T(8,128)(2,1)} %constant.13.clone.tap_back_ref) | copy-start | bytes 552964
  6.7 27.8 %copy-start.5 = (bf16[240,144]{1,0:T(8,128)(2,1)S(1)}, bf16[240,144]{1,0:T(8,128)(2,1)}, u32[]{:S(2)}) copy-start(bf16[240,144]{1,0:T(8,128)(2,1)} %constant.10.clone.into_ref) | copy-start | bytes 207364
  6.7 27.8 %copy-start.6 = (bf16[144,240]{1,0:T(8,128)(2,1)S(1)}, bf16[144,240]{1,0:T(8,128)(2,1)}, u32[]{:S(2)}) copy-start(bf16[144,240]{1,0:T(8,128)(2,1)} %constant.11.clone.back_ref) | copy-start | bytes 207364
